TPU v7x, 32 devices: a whole 2x2x4 slice. The times are simulated.
32 devices in a mesh: tm: 8 (over z, x), freq: 4 (over y, core).
Axes of the slice: x: 2, y: 2, z: 4, core: 2. Of those that a mesh axis runs over, the one named last changes fastest.
Arguments:
- visibilities: bfloat16 [2, 32, 2048, 4096], P(None, 'freq', 'tm'), may hold values from -6 to 6
- feed_gains: float32 [2, 32, 1024], P(None, 'freq'), may hold values from -4 to 4
- feed_pairs: int32 [4096, 2], replicated, may hold values from 0 to 1023
- m_order: int32 [8], replicated, may hold values from 0 to 7, each once
- beam_rows: bfloat16 [2, 8, 32, 64, 4096], P(None, 'tm', 'freq'), may hold values from -0.0625 to 0.0625
- kl_basis: bfloat16 [8, 32, 64, 512], P('tm', 'freq'), may hold values from -0.125 to 0.125
Outputs:
- kl_modes: float32 [2, 8, 512], P(None, 'tm', 'freq')
Inputs may be any that keep to these rules, and one draw needn't show every extreme that they name: `m_order`: each value appears once.
All inputs are finite; a program needn't handle non-finite values.
Results may differ from a plain program's by a relative error of at most 0.0057.
Values may be sent and summed in bfloat16 or wider, within the bound.
No kernel may reach another device: no remote copies, remote signals or barrier semaphores. Data moves between devices by JAX's collectives and lax.ppermute only.
A program may use at most 192 MiB of HBM per device.

v0:
```python
import jax
import jax.numpy as jnp
from jax import lax
from jax.sharding import PartitionSpec as P


def twiddle_table(m_order, length):
    slots = m_order.shape[0]
    shifted = m_order - slots // 2
    times = jnp.arange(length, dtype=jnp.int32)
    phase = shifted[:, None] * times[None, :] % length
    angle = 2.0 * jnp.pi / length * phase.astype(jnp.float32)
    norm = 1.0 / jnp.sqrt(jnp.float32(length))
    cosine = jnp.cos(angle) * norm
    sine = jnp.sin(angle) * norm
    table = jnp.stack([jnp.stack([cosine, sine]), jnp.stack([-sine, cosine])])
    return table.astype(jnp.bfloat16)


def pick_gains(feed_gains, column):
    feeds = jnp.arange(feed_gains.shape[2], dtype=jnp.int32)
    picker = (column[None, :] == feeds[:, None]).astype(jnp.float32)
    return jnp.einsum("cfn,nb->cfb", feed_gains, picker, precision=lax.Precision.HIGHEST)


def on_device(visibilities, feed_gains, feed_pairs, m_order, beam_rows, kl_basis):
    groups = lax.axis_size("tm")
    gain_i = pick_gains(feed_gains, feed_pairs[:, 0])
    gain_j = pick_gains(feed_gains, feed_pairs[:, 1])
    prod_re = (gain_i[0] * gain_j[0] + gain_i[1] * gain_j[1])[:, None, :]
    prod_im = (gain_i[1] * gain_j[0] - gain_i[0] * gain_j[1])[:, None, :]
    raw_re = visibilities[0].astype(jnp.float32)
    raw_im = visibilities[1].astype(jnp.float32)
    joined = jnp.stack([raw_re * prod_re - raw_im * prod_im, raw_re * prod_im + raw_im * prod_re])
    chans = joined.shape[1]
    local_times = joined.shape[2]
    block_width = joined.shape[3] // groups
    calibrated = jnp.transpose(
        joined.reshape(2, chans, local_times, groups, block_width), (3, 0, 1, 2, 4)
    ).astype(jnp.bfloat16)
    length = local_times * groups
    slots_here = m_order.shape[0] // groups
    table = twiddle_table(m_order, length).reshape(2, 2, groups, slots_here, groups, local_times)
    by_baseline = lax.all_to_all(calibrated, "tm", split_axis=0, concat_axis=0, tiled=True)
    spectrum = lax.all_to_all(
        jnp.einsum(
            "oidqsu,sifub->doqfb", table, by_baseline, preferred_element_type=jnp.float32
        ).astype(jnp.bfloat16),
        "tm",
        split_axis=0,
        concat_axis=0,
        tiled=True,
    )
    shape = beam_rows.shape
    beams = beam_rows.reshape(2, shape[1], shape[2], shape[3], groups, block_width)
    beam_re = beams[0]
    beam_im = beams[1]
    spec_re = spectrum[:, 0]
    spec_im = spectrum[:, 1]

    def project(beam, spec):
        return jnp.einsum("mfknb,nmfb->mfk", beam, spec, preferred_element_type=jnp.float32)

    tel_re = project(beam_re, spec_re) - project(beam_im, spec_im)
    tel_im = project(beam_re, spec_im) + project(beam_im, spec_re)
    telescope = jnp.stack([tel_re, tel_im]).astype(jnp.bfloat16)
    partial_modes = jnp.einsum(
        "cmfk,mfke->cme", telescope, kl_basis, preferred_element_type=jnp.float32
    )
    return lax.psum_scatter(partial_modes, "freq", scatter_dimension=2, tiled=True)


def solution(mesh):
    placed = (
        P(None, "freq", "tm", None),
        P(None, "freq", None),
        P(),
        P(),
        P(None, "tm", "freq", None, None),
        P("tm", "freq", None, None),
    )
    return jax.shard_map(
        on_device, mesh=mesh, in_specs=placed, out_specs=P(None, "tm", "freq"), check_vma=False
    )
```

profile of v0, /device:TPU:0, one launch (start us, length us, event | category | flops | bytes accessed | tf_op | source)
XLA Modules:
  0.0 984.8 jit_solution(7615485347170653181)
XLA Ops:
  6.5 0.9 fusion.54
  7.4 6.1 fusion.14
  13.5 6.1 fusion.17
  19.6 23.4 %fusion.51 = (bf16[1,8,256,4096]{3,2,1,0:T(8,128)(2,1)}, bf16[1,8,256,4096]{3,2,1,0:T(8,128)(2,1)}) fusion(bf16[2,8,256,4096]{3,2,1,0:T(8,128)(2,1)} %param.6), kind=kLoop, calls=%fused_computation.71 | loop fusion | bytes 67108864 | tf_op jit(solution)/shard_map/slice | solution.py:33
  42.9 21.2 %copy.45 = bf16[1,8,256,4096]{2,3,1,0:T(8,128)(2,1)} copy(bf16[1,8,256,4096]{3,2,1,0:T(8,128)(2,1)} %get-tuple-element.8) | data formatting | bytes 33554432
  64.1 21.2 %copy.46 = bf16[1,8,256,4096]{2,3,1,0:T(8,128)(2,1)} copy(bf16[1,8,256,4096]{3,2,1,0:T(8,128)(2,1)} %get-tuple-element.7) | data formatting | bytes 33554432
  85.3 23.0 %fusion.1 = (bf16[1,8,256,4096]{2,3,1,0:T(8,128)(2,1)}, bf16[1,8,256,4096]{2,3,1,0:T(8,128)(2,1)}) fusion(bf16[1,8,256,4096]{2,3,1,0:T(8,128)(2,1)} %copy.45, bf16[1,8,256,4096]{2,3,1,0:T(8,128)(2,1)} %copy.46, f32[8,4096]{1,0:T(8,128)S(1)} %get-tuple-element.12, f32[8,4096]{1,0:T(8,128)S(1)} %get-tuple-element.11), kind=kLoop, calls=%fused_computation.5 | loop fusion | flops 83886080 | bytes 67371008 | tf_op jit(solution)/shard_map/convert.13
  108.3 22.9 %maximum_bitcast_fusion = bf16[8,2,8,256,512]{3,4,0,2,1:T(8,128)(2,1)} fusion(bf16[1,8,256,8,512]{2,4,3,1,0:T(8,128)(2,1)} %bitcast.102, bf16[1,8,256,8,512]{2,4,3,1,0:T(8,128)(2,1)} %bitcast.101), kind=kLoop, calls=%fused_computation.8 | loop fusion | flops 16777216 | bytes 67108864 | tf_op jit(solution)/shard_map/convert_element_type | solution.py:40
  131.2 42.4 %copy.25 = bf16[8,2,8,256,512]{4,3,1,2,0:T(8,128)(2,1)} copy(bf16[8,2,8,256,512]{3,4,0,2,1:T(8,128)(2,1)} %maximum_bitcast_fusion) | data formatting | bytes 67108864 | tf_op jit(solution)/shard_map/convert_element_type | solution.py:40
  173.6 7.4 all-to-all-start
  181.4 723.7 %all-to-all-done = bf16[8,2,8,256,512]{4,3,1,2,0:T(8,128)(2,1)} async-done(((bf16[8,2,8,256,512]{4,3,1,2,0:T(8,128)(2,1)}), bf16[8,2,8,256,512]{4,3,1,2,0:T(8,128)(2,1)}, u32[]{:S(2)}, u32[]{:S(2)}) %all-to-all-start) | async-done | bytes 33554464 | tf_op jit(solution)/shard_map/all_to_all | solution.py:44
  905.1 12.8 %fusion.4 = bf16[8,512,2,8,1,1]{1,3,4,2,0,5:T(8,128)(2,1)S(1)} fusion(bf16[8,2,8,256,512]{4,3,1,2,0:T(8,128)(2,1)} %all-to-all-done, bf16[1,1,8,8,256]{4,2,1,0,3:T(8,128)(2,1)S(1)} %get-tuple-element.19, bf16[1,1,8,8,256]{4,2,1,0,3:T(8,128)(2,1)S(1)} %get-tuple-element.18, bf16[1,1,8,8,256]{4,2,1,0,3:T(8,128)(2,1)S(1)} %get-tuple-element.17), kind=kOutput, calls=%fused_computation.9 | convolution fusion | flops 537395200 | bytes 33783808 | tf_op jit(solution)/shard_map/oidqsu,sifub->doqfb/dot_general | solution.py:46
  918.0 0.8 copy.26
  918.8 3.4 all-to-all-start.1
  922.2 3.8 fusion.52
  926.0 4.2 copy.50
  930.2 4.2 copy.49
  934.7 4.7 fusion.22
  939.3 4.7 fusion.20
  944.0 4.9 fusion.26
  948.9 4.7 fusion.24
  953.6 1.2 convolution_bitcast_fusion
  954.9 21.6 %reduce-scatter.4.cloned.1.call-done = f32[128,2]{1,0:T(8,128)} async-done(((f32[512,2]{1,0:T(8,128)}), f32[128,2]{1,0:T(8,128)}) %reduce-scatter.4.cloned.1.call-update) | async-done | bytes 1040
  976.5 1.5 copy.44
  (18 shorter events, 0.7 us)
Async XLA Ops:
  6.5 947.1 %copy-start = (bf16[1,8,64,512]{3,2,1,0:T(8,128)(2,1)S(1)}, bf16[1,8,64,512]{3,2,1,0:T(8,128)(2,1)}, u32[]{:S(2)}) copy-start(bf16[1,8,64,512]{3,2,1,0:T(8,128)(2,1)} %param.11) | copy-start | bytes 1572868
  173.6 7.4 copy-start.1
  173.6 731.5 %all-to-all-start = ((bf16[8,2,8,256,512]{4,3,1,2,0:T(8,128)(2,1)}), bf16[8,2,8,256,512]{4,3,1,2,0:T(8,128)(2,1)}, u32[]{:S(2)}, u32[]{:S(2)}) async-start(bf16[8,2,8,256,512]{4,3,1,2,0:T(8,128)(2,1)} %copy.25), calls=%async_computation | async-start | bytes 67108864 | tf_op jit(solution)/shard_map/all_to_all | solution.py:44
  918.8 15.6 %all-to-all-start.1 = ((bf16[8,2,1,8,512]{4,1,3,2,0:T(2,128)(2,1)}), bf16[8,2,1,8,512]{4,1,3,2,0:T(2,128)(2,1)S(1)}, u32[]{:S(2)}, u32[]{:S(2)}) async-start(bf16[8,2,1,8,512]{4,1,3,2,0:T(2,128)(2,1)} %copy.26), calls=%async_computation.1 | async-start | bytes 262144 | tf_op jit(solution)/shard_map/all_to_all | solution.py:45
  922.2 54.3 %reduce-scatter.4.cloned.1.call-start = ((), (), s32[]{:S(2)}) async-start(), calls=%async_computation.3 | async-start | bytes 327680
Sparse Core Ops, SparseCore 0:
  955.0 21.4 reduce-scatter.3
where the time goes:
time: 987 us; the launch traced here: 985 us
  waiting for transfers between devices  745 us (75%)
  local copies, waits for them, and re-layouts  124 us (13%)
  other arithmetic  46.3 us (5%)
  matrix products  45.1 us (5%)
  between operations  13.5 us (1%)
  starting transfers between devices  10.8 us (1%)
    all_to_all x1, waiting for transfers between devices, on_device(): lax.all_to_all(calibrated, 'tm', split_axis=0, concat_axis=0, tiled=True)  724 us
    unnamed x9, local copies, waits for them, and re-layouts  52.2 us
    convert_element_type x1, local copies, waits for them, and re-layouts, on_device(): calibrated = jnp.transpose(joined.reshape(2, chans, local_times, groups,...  42.4 us
    slice x1, local copies, waits for them, and re-layouts, on_device(): raw_im = visibilities[1].astype(jnp.float32)  23.4 us
    another operation x2, other arithmetic  23.3 us
    convert_element_type x1, other arithmetic, on_device(): calibrated = jnp.transpose(joined.reshape(2, chans, local_times, groups,...  22.9 us
    unnamed x2, waiting for transfers between devices  21.6 us
  transfers between devices with their start and end apart: 3, of which 2 were waited for; matrix products, arithmetic and copies ran while one was open for 1% of the time, Pallas kernels for 0%

commit v1 on v0

v1 whole, which is shorter than its diff:
```python
import functools

import jax
import jax.numpy as jnp
from jax import lax
from jax.experimental import pallas as pl
from jax.experimental.pallas import tpu as pltpu
from jax.sharding import PartitionSpec as P

LANES = 128
TILE = 512
PARTS = (5, 3)
MIB = 1 << 20
F32 = jnp.float32
BF16 = jnp.bfloat16


def relative_table(m_order, groups, local_times):
    me = lax.axis_index("tm")
    slots = m_order.shape[0]
    here = slots // groups
    high = groups // 4
    owners = jnp.arange(groups, dtype=jnp.int32)
    relative = (owners % high) * 4 + owners // high
    wanted = jnp.bitwise_xor(relative, me)[:, None] * here + jnp.arange(here, dtype=jnp.int32)[None, :]
    wanted = wanted.reshape(-1)
    held = jnp.sum(
        jnp.where(wanted[:, None] == jnp.arange(slots, dtype=jnp.int32)[None, :], m_order[None, :], 0), axis=1
    )
    length = local_times * groups
    times = me * local_times + jnp.arange(local_times, dtype=jnp.int32)
    phase = (held - slots // 2)[:, None] * times[None, :] % length
    angle = 2.0 * jnp.pi / length * phase.astype(F32)
    norm = 1.0 / jnp.sqrt(F32(length))
    cosine = jnp.cos(angle) * norm
    sine = jnp.sin(angle) * norm
    table = jnp.stack([jnp.stack([cosine, -sine], 1), jnp.stack([sine, cosine], 1)])
    return table.reshape(2, 2 * slots, local_times).astype(BF16)


def transform_kernel(first, rows, table_ref, vis_ref, *refs):
    outs, (held, sums, sems) = refs[:-3], refs[-3:]
    chans = held.shape[1]
    tiles = held.shape[3] // TILE

    def copy(tile, f):
        return pltpu.make_async_copy(
            vis_ref.at[:, f, :, pl.ds(first + tile * TILE, TILE)],
            held.at[:, f, :, pl.ds(tile * TILE, TILE)],
            sems.at[tile, f],
        )

    for tile in range(tiles):
        for f in range(chans):
            copy(tile, f).start()
    table_re = table_ref[0]
    table_im = table_ref[1]
    each = rows * chans // len(outs)
    for tile in range(tiles):
        cols = pl.ds(tile * TILE, TILE)
        for f in range(chans):
            copy(tile, f).wait()
            both = jnp.dot(table_re, held[0, f, :, cols], preferred_element_type=F32) + jnp.dot(
                table_im, held[1, f, :, cols], preferred_element_type=F32
            )
            for lane in range(0, TILE, LANES):
                sums[lane // LANES, pl.ds(f, rows, stride=chans), :] = both[:, lane : lane + LANES]
        for d, out in enumerate(outs):
            for lane in range(0, TILE, LANES):
                part = sums[lane // LANES, pl.ds(d * each, each), :]
                out[:, :, pl.ds(tile * TILE + lane, LANES)] = part.reshape(*out.shape[:2], LANES).astype(out.dtype)


def transform(table, visibilities, first, width):
    _, chans, times, _ = visibilities.shape
    rows = table.shape[1]
    shape = (rows // 8, 2 * chans, width)
    return pl.pallas_call(
        functools.partial(transform_kernel, first, rows),
        out_shape=[jax.ShapeDtypeStruct(shape, F32 if d == 0 else BF16) for d in range(4)],
        in_specs=[pl.BlockSpec(memory_space=pltpu.VMEM), pl.BlockSpec(memory_space=pl.ANY)],
        out_specs=[pl.BlockSpec(memory_space=pltpu.VMEM)] * 4,
        scratch_shapes=[
            pltpu.VMEM((2, chans, times, width), BF16),
            pltpu.VMEM((TILE // LANES, rows * chans, LANES), F32),
            pltpu.SemaphoreType.DMA((width // TILE, chans)),
        ],
        compiler_params=pltpu.CompilerParams(vmem_limit_bytes=36 * MIB),
        cost_estimate=pl.CostEstimate(
            flops=64 * rows * 2 * chans * times * width,
            bytes_accessed=4 * chans * times * width,
            transcendentals=0,
        ),
        name="transform",
    )(table, visibilities)


def gains_kernel(gains_ref, pairs_ref, out_ref):
    chans = gains_ref.shape[1]
    groups = gains_ref.shape[2] // LANES

    def step(tile, _):
        cols = pl.ds(pl.multiple_of(tile * LANES, LANES), LANES)
        picked = []
        for side in range(2):
            index = jnp.broadcast_to(pairs_ref[side : side + 1, cols], (chans, LANES))
            low = jnp.bitwise_and(index, LANES - 1)
            high = jnp.right_shift(index, 7)
            for c in range(2):
                value = jnp.zeros((chans, LANES), F32)
                for group in range(groups):
                    table = gains_ref[c, :, group * LANES : (group + 1) * LANES]
                    value = jnp.where(high == group, jnp.take_along_axis(table, low, axis=1), value)
                picked.append(value)
        i_re, i_im, j_re, j_im = picked
        out_ref[0:chans, cols] = i_re * j_re + i_im * j_im
        out_ref[chans : 2 * chans, cols] = i_im * j_re - i_re * j_im
        return 0

    lax.fori_loop(0, pairs_ref.shape[1] // LANES, step, 0)


def pair_gains(feed_gains, feed_pairs):
    chans = feed_gains.shape[1]
    count = feed_pairs.shape[0]
    return pl.pallas_call(
        gains_kernel,
        out_shape=jax.ShapeDtypeStruct((2 * chans, count), F32),
        in_specs=[pl.BlockSpec(memory_space=pltpu.VMEM)] * 2,
        out_specs=pl.BlockSpec(memory_space=pltpu.VMEM),
        cost_estimate=pl.CostEstimate(flops=4 << 20, bytes_accessed=4 << 20, transcendentals=0),
        name="pair_gains",
    )(feed_gains, feed_pairs.T)


def project_kernel(first, n_recv, *refs):
    keep, recvs = refs[0], refs[1 : 1 + n_recv]
    gains, beams, out = refs[1 + n_recv : 4 + n_recv]
    chans = beams.shape[1]
    modes = beams.shape[2]
    width = keep.shape[1]
    total = keep[...]
    for recv in recvs:
        total = total + recv[...].astype(F32)
    cols = pl.ds(first, width)
    p_re, p_im = gains[0:chans, cols], gains[chans : 2 * chans, cols]
    re, im = total[:chans], total[chans:]
    spec = jnp.concatenate([re * p_re - im * p_im, re * p_im + im * p_re]).astype(BF16)
    for f in range(chans):
        beam = jnp.concatenate([beams[0, f, :, cols], beams[1, f, :, cols]])
        both = lax.dot_general(spec, beam, (((1,), (1,)), ((), ())), preferred_element_type=F32)
        straight, crossed = both[:, :modes], both[:, modes:]
        out[f] = jnp.concatenate(
            [straight[:chans] - crossed[chans:], straight[chans:] + crossed[:chans]]
        )


def project(keep, recvs, gains, beams, first):
    _, chans, modes, _ = beams.shape
    width = keep.shape[1]
    return pl.pallas_call(
        functools.partial(project_kernel, first, len(recvs)),
        out_shape=jax.ShapeDtypeStruct((chans, 2 * chans, modes), F32),
        in_specs=[pl.BlockSpec(memory_space=pltpu.VMEM)] * (3 + len(recvs)),
        out_specs=pl.BlockSpec(memory_space=pltpu.VMEM),
        compiler_params=pltpu.CompilerParams(vmem_limit_bytes=24 * MIB),
        cost_estimate=pl.CostEstimate(
            flops=16 * 4 * chans * modes * width * chans, bytes_accessed=4 * chans * modes * width, transcendentals=0
        ),
        name="project",
    )(keep, *recvs, gains, beams)


def modes_kernel(n_tel, *refs):
    tels, (where_ref, basis, out) = refs[:n_tel], refs[n_tel:]
    chans = basis.shape[0]
    me = where_ref[0]
    row = lax.broadcasted_iota(jnp.int32, tels[0].shape[1:], 0)
    total = jnp.zeros((2 * chans, basis.shape[2]), F32)
    for f in range(chans):
        tel = functools.reduce(lambda a, b: a + b, [t[f] for t in tels])
        tel = jnp.where(jnp.bitwise_and(row, chans - 1) == f, tel, 0.0).astype(BF16)
        total = total + jnp.dot(tel, basis[f], preferred_element_type=F32)
    both = jnp.concatenate(
        [jnp.sum(total[:chans], axis=0, keepdims=True), jnp.sum(total[chans:], axis=0, keepdims=True)]
    )
    width = out.shape[2]
    for block in range(out.shape[0]):
        out[jnp.bitwise_xor(block, me)] = both[:, block * width : (block + 1) * width]


def partial_modes(tels, basis, blocks):
    where = lax.axis_index("freq").astype(jnp.int32).reshape(1)
    return pl.pallas_call(
        functools.partial(modes_kernel, len(tels)),
        out_shape=jax.ShapeDtypeStruct((blocks, 2, basis.shape[2] // blocks), F32),
        in_specs=[pl.BlockSpec(memory_space=pltpu.VMEM)] * len(tels)
        + [pl.BlockSpec(memory_space=pltpu.SMEM), pl.BlockSpec(memory_space=pltpu.VMEM)],
        out_specs=pl.BlockSpec(memory_space=pltpu.VMEM),
        name="partial_modes",
    )(*tels, where, basis)


def swap(x, axis, mask):
    return lax.ppermute(x, axis, [(i, i ^ mask) for i in range(lax.axis_size(axis))])


def reduce_slots(parts, groups):
    shift = 0
    while True:
        received = [swap(part, "tm", d << shift) for d, part in enumerate(parts) if d]
        left = groups >> (shift + (len(parts) - 1).bit_length())
        if left == 1:
            return parts[0][0], [r[0] for r in received]
        total = parts[0] + functools.reduce(lambda a, b: a + b, [r.astype(F32) for r in received])
        shift += (len(parts) - 1).bit_length()
        ways = min(4, left)
        total = total.reshape(left // ways, ways, *total.shape[1:])
        parts = [total[:, d] if d == 0 else total[:, d].astype(BF16) for d in range(ways)]


def on_device(visibilities, feed_gains, feed_pairs, m_order, beam_rows, kl_basis):
    groups = lax.axis_size("tm")
    count = visibilities.shape[3]
    table = relative_table(m_order, groups, visibilities.shape[2])
    first = 0
    spectra = []
    for share in PARTS:
        width = count // sum(PARTS) * share
        parts = transform(table, visibilities, first, width)
        spectra.append((first, reduce_slots(parts, groups)))
        first += width
    gains = pair_gains(feed_gains, feed_pairs)
    tels = [project(keep, recvs, gains, beam_rows[:, 0], start) for start, (keep, recvs) in spectra]
    held = partial_modes(tels, kl_basis[0], lax.axis_size("freq"))
    held = held.reshape(held.shape[0] // 2, 2, *held.shape[1:])
    held = held[:, 0] + swap(held[:, 1], "freq", 1)
    held = held[0] + swap(held[1], "freq", 2)
    return held[:, None, :]


def solution(mesh):
    placed = (
        P(None, "freq", "tm", None),
        P(None, "freq", None),
        P(),
        P(),
        P(None, "tm", "freq", None, None),
        P("tm", "freq", None, None),
    )
    return jax.shard_map(
        on_device, mesh=mesh, in_specs=placed, out_specs=P(None, "tm", "freq"), check_vma=False
    )
```

time: 987 us -> 59.9 us (0.06)
  waiting for transfers between devices: 745 us -> 7.41 us
  local copies, waits for them, and re-layouts: 124 us -> 9.12 us
  matrix products: 45.1 us -> 0 us
  other arithmetic: 46.3 us -> 2.32 us
  Pallas kernels: 0 us -> 24.5 us
  between operations: 13.5 us -> 0.14 us
    all_to_all x2 -> x0, waiting for transfers between devices: 724 us -> none  [the longest x1 724 us: on_device(): lax.all_to_all(calibrated, 'tm', split_axis=0, concat_axis=0, tiled=True)]
    dot_general x8 -> x0, matrix products: 45.1 us -> none  [the longest x4 18.8 us: project(): jnp.einsum('mfknb,nmfb->mfk', beam, spec, preferred_element_type=jnp.floa...]
    unnamed x9 -> x11, local copies, waits for them, and re-layouts: 52.2 us -> 8.36 us
    convert_element_type x2, local copies, waits for them, and re-layouts: 43.2 us -> 0.02 us  [reduce_slots(): total[:, d].astype(BF16)]
    slice x4 -> x0, local copies, waits for them, and re-layouts: 28.2 us -> none  [the longest x1 23.4 us: on_device(): raw_im = visibilities[1].astype(jnp.float32)]
    pallas_call x0 -> x6, Pallas kernels: none -> 24.5 us  [the longest x2 14.8 us: transform(): pl.pallas_call(functools.partial(transform_kernel, first, rows), out_shap...]
    another operation x4 -> x2, other arithmetic: 23.3 us -> 0.14 us
    convert_element_type x1 -> x0, other arithmetic: 22.9 us -> none  [on_device(): calibrated = jnp.transpose(joined.reshape(2, chans, local_times, groups,...]
  transfers between devices with their start and end apart: 3 -> 10, of which waited for: 2 -> 4; matrix products, arithmetic and copies ran while one was open for 1% -> 0% of each run, Pallas kernels for 0% -> 26%
where the time goes in v1:
time: 59.9 us; the launch traced here: 59.6 us
  Pallas kernels  24.5 us (41%)
  starting transfers between devices  16 us (27%)
  local copies, waits for them, and re-layouts  9.12 us (15%)
  waiting for transfers between devices  7.41 us (12%)
  other arithmetic  2.32 us (4%)
    ppermute x10, starting transfers between devices, swap(): lax.ppermute(x, axis, [(i, i ^ mask) for i in range(lax.axis_size(axis))])  16 us
    pallas_call x2, Pallas kernels, transform(): pl.pallas_call(functools.partial(transform_kernel, first, rows), out_shap...  14.8 us
    unnamed x11, local copies, waits for them, and re-layouts  8.36 us
    ppermute x10, waiting for transfers between devices, swap(): lax.ppermute(x, axis, [(i, i ^ mask) for i in range(lax.axis_size(axis))])  7.41 us
    pallas_call x1, Pallas kernels, pair_gains(): pl.pallas_call(gains_kernel, out_shape=jax.ShapeDtypeStruct((2 * chans, c...  5.31 us
    pallas_call x2, Pallas kernels, project(): pl.pallas_call(functools.partial(project_kernel, first, len(recvs)), out_...  2.51 us
    pallas_call x1, Pallas kernels, partial_modes(): pl.pallas_call(functools.partial(modes_kernel, len(tels)), out_shape=jax....  1.9 us
  transfers between devices with their start and end apart: 10, of which 4 were waited for; matrix products, arithmetic and copies ran while one was open for 0% of the time, Pallas kernels for 26%

profile of v1, /device:TPU:0, one launch (start us, length us, event | category | flops | bytes accessed | tf_op | source)
XLA Modules:
  0.0 59.6 jit_solution(12236501506063462239)
XLA Ops:
  0.0 0.8 %select_reduce_fusion = s32[8]{0:T(128)S(1)} fusion(s32[8]{0:T(128)} %param.9, s32[8]{0:T(128)S(1)} %fusion.10), kind=kLoop, calls=%fused_computation.24 | loop fusion | flops 184 | bytes 96 | tf_op jit(solution)/shard_map/reduce_sum | solution.py:27
  1.1 5.8 %transform.3 = (f32[2,16,1536]{2,1,0:T(8,128)S(1)}, bf16[2,16,1536]{2,1,0:T(8,128)(2,1)S(1)}, bf16[2,16,1536]{2,1,0:T(8,128)(2,1)S(1)}, bf16[2,16,1536]{2,1,0:T(8,128)(2,1)S(1)}) custom-call(bf16[2,16,256]{2,1,0:T(8,128)(2,1)S(1)} %constant_dynamic-update-slice_fusion.table_ref, bf16[2,8,256,4096]{3,2,1,0:T(8,128)(2,1)} %vis_ref.3), custom_call_target="tpu_custom_call" | custom-call | flops 6442450944 | bytes 12582912 | tf_op jit(solution)/shard_map/transform/pallas_call | solution.py:78
  6.9 4.0 %collective-permute-start.6 = (bf16[2,16,1536]{2,1,0:T(8,128)(2,1)S(1)}, bf16[2,16,1536]{2,1,0:T(8,128)(2,1)S(1)}, u32[]{:S(2)}, u32[]{:S(2)}) collective-permute-start(bf16[2,16,1536]{2,1,0:T(8,128)(2,1)S(1)} %get-tuple-element.20), channel_id=1, source_target_pairs={{0,12},{4,8},{8,4},{12,0},{16,28},{20,24},{24,20},{28,16},{1,13},{... | collective-permute-start | bytes 294920 | tf_op jit(solution)/shard_map/ppermute | solution.py:205
  10.9 0.4 collective-permute-start.5
  11.6 9.0 %transform.2 = (f32[2,16,2560]{2,1,0:T(8,128)S(1)}, bf16[2,16,2560]{2,1,0:T(8,128)(2,1)S(1)}, bf16[2,16,2560]{2,1,0:T(8,128)(2,1)S(1)}, bf16[2,16,2560]{2,1,0:T(8,128)(2,1)S(1)}) custom-call(bf16[2,16,256]{2,1,0:T(8,128)(2,1)S(1)} %constant_dynamic-update-slice_fusion.table_ref, bf16[2,8,256,4096]{3,2,1,0:T(8,128)(2,1)} %vis_ref.3), custom_call_target="tpu_custom_call" | custom-call | flops 10737418240 | bytes 20971520 | tf_op jit(solution)/shard_map/transform/pallas_call | solution.py:78
  20.6 2.9 %collective-permute-start.2 = (bf16[2,16,2560]{2,1,0:T(8,128)(2,1)S(1)}, bf16[2,16,2560]{2,1,0:T(8,128)(2,1)S(1)}, u32[]{:S(2)}, u32[]{:S(2)}) collective-permute-start(bf16[2,16,2560]{2,1,0:T(8,128)(2,1)S(1)} %get-tuple-element.16), channel_id=1, source_target_pairs={{0,12},{4,8},{8,4},{12,0},{16,28},{20,24},{24,20},{28,16},{1,13},{... | collective-permute-start | bytes 491528 | tf_op jit(solution)/shard_map/ppermute | solution.py:205
  24.0 5.3 %pair_gains.1.refs_2_ = f32[16,4096]{1,0:T(8,128)} custom-call(f32[2,8,1024]{2,1,0:T(8,128)} %gains_ref.1, s32[2,4096]{1,0:T(2,128)} %bitcast.41), custom_call_target="tpu_custom_call" | custom-call | flops 4194304 | bytes 4194304 | tf_op jit(solution)/shard_map/pair_gains/pallas_call | solution.py:126
  29.5 3.0 %collective-permute-start.7 = (bf16[1,16,1536]{2,1,0:T(8,128)(2,1)S(1)}, bf16[1,16,1536]{2,1,0:T(8,128)(2,1)S(1)}, u32[]{:S(2)}, u32[]{:S(2)}) collective-permute-start(bf16[1,16,1536]{2,1,0:T(8,128)(2,1)S(1)} %fusion.1), channel_id=1, source_target_pairs={{0,16},{4,20},{8,24},{12,28},{16,0},{20,4},{24,8},{28,12},{1,17},{... | collective-permute-start | bytes 147464 | tf_op jit(solution)/shard_map/ppermute | solution.py:205
  32.5 2.1 %collective-permute-done.7 = bf16[1,16,1536]{2,1,0:T(8,128)(2,1)S(1)} collective-permute-done((bf16[1,16,1536]{2,1,0:T(8,128)(2,1)S(1)}, bf16[1,16,1536]{2,1,0:T(8,128)(2,1)S(1)}, u32[]{:S(2)}, u32[]{:S(2)}) %collective-permute-start.7) | collective-permute-done | bytes 49184 | tf_op jit(solution)/shard_map/ppermute | solution.py:205
  34.6 3.4 %copy-done = bf16[2,1,8,64,4096]{4,3,2,1,0:T(8,128)(2,1)S(1)} copy-done((bf16[2,1,8,64,4096]{4,3,2,1,0:T(8,128)(2,1)S(1)}, bf16[2,1,8,64,4096]{4,3,2,1,0:T(8,128)(2,1)}, u32[]{:S(2)}) %copy-start) | copy-done | bytes 8388632
  38.0 0.9 %copy-done.2 = f32[16,4096]{1,0:T(8,128)S(1)} copy-done((f32[16,4096]{1,0:T(8,128)S(1)}, f32[16,4096]{1,0:T(8,128)}, u32[]{:S(2)}) %copy-start.2) | copy-done | bytes 262168
  38.9 1.0 %project.3.refs_1_ = f32[8,16,64]{2,1,0:T(8,128)S(1)} custom-call(f32[16,1536]{1,0:T(8,128)S(1)} %slice_bitcast_fusion.1.refs_0_, bf16[16,1536]{1,0:T(8,128)(2,1)S(1)} %bitcast.39, f32[16,4096]{1,0:T(8,128)S(1)} %copy-done.2, bf16[2,8,64,4096]{3,2,1,0:T(8,128)(2,1)S(1)} %bitcast.36), custom_call_target="tpu_custom_call" | custom-call | flops 402653184 | bytes 3145728 | tf_op jit(solution)/shard_map/project/pallas_call | solution.py:161
  40.1 3.0 %collective-permute-start.3 = (bf16[1,16,2560]{2,1,0:T(8,128)(2,1)S(1)}, bf16[1,16,2560]{2,1,0:T(8,128)(2,1)S(1)}, u32[]{:S(2)}, u32[]{:S(2)}) collective-permute-start(bf16[1,16,2560]{2,1,0:T(8,128)(2,1)S(1)} %fusion), channel_id=1, source_target_pairs={{0,16},{4,20},{8,24},{12,28},{16,0},{20,4},{24,8},{28,12},{1,17},{... | collective-permute-start | bytes 245768 | tf_op jit(solution)/shard_map/ppermute | solution.py:205
  43.1 2.4 %collective-permute-done.3 = bf16[1,16,2560]{2,1,0:T(8,128)(2,1)S(1)} collective-permute-done((bf16[1,16,2560]{2,1,0:T(8,128)(2,1)S(1)}, bf16[1,16,2560]{2,1,0:T(8,128)(2,1)S(1)}, u32[]{:S(2)}, u32[]{:S(2)}) %collective-permute-start.3) | collective-permute-done | bytes 81952 | tf_op jit(solution)/shard_map/ppermute | solution.py:205
  45.5 3.4 %copy-done.1 = bf16[2,1,8,64,4096]{4,3,2,1,0:T(8,128)(2,1)S(1)} copy-done((bf16[2,1,8,64,4096]{4,3,2,1,0:T(8,128)(2,1)S(1)}, bf16[2,1,8,64,4096]{4,3,2,1,0:T(8,128)(2,1)}, u32[]{:S(2)}) %copy-start.1) | copy-done | bytes 8388632
  48.9 1.5 %project.2.refs_0_ = f32[8,16,64]{2,1,0:T(8,128)S(1)} custom-call(f32[16,2560]{1,0:T(8,128)S(1)} %slice_bitcast_fusion.refs_0_, bf16[16,2560]{1,0:T(8,128)(2,1)S(1)} %bitcast.38, f32[16,4096]{1,0:T(8,128)S(1)} %copy-done.2, bf16[2,8,64,4096]{3,2,1,0:T(8,128)(2,1)S(1)} %bitcast.37), custom_call_target="tpu_custom_call" | custom-call | flops 671088640 | bytes 5242880 | tf_op jit(solution)/shard_map/project/pallas_call | solution.py:161
  50.4 0.6 %copy-done.4 = f32[8,16,64]{2,1,0:T(8,128)} copy-done((f32[8,16,64]{2,1,0:T(8,128)}, f32[8,16,64]{2,1,0:T(8,128)S(1)}, u32[]{:S(2)}) %copy-start.4) | copy-done | bytes 32792
  51.1 1.9 %partial_modes.1 = f32[4,2,128]{2,1,0:T(2,128)} custom-call(f32[8,16,64]{2,1,0:T(8,128)} %copy-done.4, f32[8,16,64]{2,1,0:T(8,128)} %copy-done.3, s32[1]{0:T(128)} %bitcast.10.refs_2_, bf16[8,64,512]{2,1,0:T(8,128)(2,1)} %bitcast.40), custom_call_target="tpu_custom_call" | custom-call | tf_op jit(solution)/shard_map/partial_modes/pallas_call | solution.py:194
  53.0 0.7 %slice_bitcast_fusion.2 = f32[2,2,128]{2,1,0:T(2,128)S(1)} fusion(f32[2,2,2,128]{3,2,1,0:T(2,128)} %bitcast.42), kind=kLoop, calls=%fused_computation.26 | loop fusion | bytes 4096 | tf_op jit(solution)/shard_map/squeeze | solution.py:237
  53.6 1.2 %collective-permute-done.8 = f32[2,2,128]{2,1,0:T(2,128)S(1)} collective-permute-done((f32[2,2,128]{2,1,0:T(2,128)S(1)}, f32[2,2,128]{2,1,0:T(2,128)S(1)}, u32[]{:S(2)}, u32[]{:S(2)}) %collective-permute-start.8) | collective-permute-done | bytes 2080 | tf_op jit(solution)/shard_map/ppermute | solution.py:205
  54.8 0.7 %fusion.6 = f32[2,2,128]{2,1,0:T(2,128)S(1)} fusion(f32[2,2,128]{2,1,0:T(2,128)S(1)} %collective-permute-done.8, f32[2,2,2,128]{3,2,1,0:T(2,128)} %bitcast.43), kind=kLoop, calls=%fused_computation.28 | loop fusion | flops 512 | bytes 6144 | tf_op jit(solution)/shard_map/add | solution.py:237
  55.5 1.8 %collective-permute-start.9 = (f32[2,128]{1,0:T(2,128)S(1)}, f32[2,128]{1,0:T(2,128)S(1)}, u32[]{:S(2)}, u32[]{:S(2)}) collective-permute-start(f32[2,128]{1,0:T(2,128)S(1)} %slice_bitcast_fusion.4), channel_id=1, source_target_pairs={{0,2},{1,3},{2,0},{3,1},{4,6},{5,7},{6,4},{7,5},{8,10},{9,11},{10,... | collective-permute-start | bytes 3080 | tf_op jit(solution)/shard_map/ppermute | solution.py:205
  57.3 1.8 %collective-permute-done.9 = f32[2,128]{1,0:T(2,128)S(1)} collective-permute-done((f32[2,128]{1,0:T(2,128)S(1)}, f32[2,128]{1,0:T(2,128)S(1)}, u32[]{:S(2)}, u32[]{:S(2)}) %collective-permute-start.9) | collective-permute-done | bytes 1056 | tf_op jit(solution)/shard_map/ppermute | solution.py:205
  59.0 0.6 fusion.7
  (34 shorter events, 1.2 us)
Async XLA Ops:
  6.9 22.3 %collective-permute-start.6 = (bf16[2,16,1536]{2,1,0:T(8,128)(2,1)S(1)}, bf16[2,16,1536]{2,1,0:T(8,128)(2,1)S(1)}, u32[]{:S(2)}, u32[]{:S(2)}) collective-permute-start(bf16[2,16,1536]{2,1,0:T(8,128)(2,1)S(1)} %get-tuple-element.20), channel_id=1, source_target_pairs={{0,12},{4,8},{8,4},{12,0},{16,28},{20,24},{24,20},{28,16},{1,13},{... | collective-permute-start | bytes 294920 | tf_op jit(solution)/shard_map/ppermute | solution.py:205
  10.9 18.5 %collective-permute-start.5 = (bf16[2,16,1536]{2,1,0:T(8,128)(2,1)S(1)}, bf16[2,16,1536]{2,1,0:T(8,128)(2,1)S(1)}, u32[]{:S(2)}, u32[]{:S(2)}) collective-permute-start(bf16[2,16,1536]{2,1,0:T(8,128)(2,1)S(1)} %get-tuple-element.19), channel_id=1, source_target_pairs={{0,8},{4,12},{8,0},{12,4},{16,24},{20,28},{24,16},{28,20},{1,9},{5... | collective-permute-start | bytes 294920 | tf_op jit(solution)/shard_map/ppermute | solution.py:205
  11.4 18.1 %collective-permute-start.4 = (bf16[2,16,1536]{2,1,0:T(8,128)(2,1)S(1)}, bf16[2,16,1536]{2,1,0:T(8,128)(2,1)S(1)}, u32[]{:S(2)}, u32[]{:S(2)}) collective-permute-start(bf16[2,16,1536]{2,1,0:T(8,128)(2,1)S(1)} %get-tuple-element.18), channel_id=1, source_target_pairs={{0,4},{4,0},{8,12},{12,8},{16,20},{20,16},{24,28},{28,24},{1,5},{5... | collective-permute-start | bytes 294920 | tf_op jit(solution)/shard_map/ppermute | solution.py:205
  20.6 19.3 %collective-permute-start.2 = (bf16[2,16,2560]{2,1,0:T(8,128)(2,1)S(1)}, bf16[2,16,2560]{2,1,0:T(8,128)(2,1)S(1)}, u32[]{:S(2)}, u32[]{:S(2)}) collective-permute-start(bf16[2,16,2560]{2,1,0:T(8,128)(2,1)S(1)} %get-tuple-element.16), channel_id=1, source_target_pairs={{0,12},{4,8},{8,4},{12,0},{16,28},{20,24},{24,20},{28,16},{1,13},{... | collective-permute-start | bytes 491528 | tf_op jit(solution)/shard_map/ppermute | solution.py:205
  23.5 16.4 %collective-permute-start.1 = (bf16[2,16,2560]{2,1,0:T(8,128)(2,1)S(1)}, bf16[2,16,2560]{2,1,0:T(8,128)(2,1)S(1)}, u32[]{:S(2)}, u32[]{:S(2)}) collective-permute-start(bf16[2,16,2560]{2,1,0:T(8,128)(2,1)S(1)} %get-tuple-element.15), channel_id=1, source_target_pairs={{0,8},{4,12},{8,0},{12,4},{16,24},{20,28},{24,16},{28,20},{1,9},{5... | collective-permute-start | bytes 491528 | tf_op jit(solution)/shard_map/ppermute | solution.py:205
  29.3 10.7 %collective-permute-start = (bf16[2,16,2560]{2,1,0:T(8,128)(2,1)S(1)}, bf16[2,16,2560]{2,1,0:T(8,128)(2,1)S(1)}, u32[]{:S(2)}, u32[]{:S(2)}) collective-permute-start(bf16[2,16,2560]{2,1,0:T(8,128)(2,1)S(1)} %get-tuple-element.14), channel_id=1, source_target_pairs={{0,4},{4,0},{8,12},{12,8},{16,20},{20,16},{24,28},{28,24},{1,5},{5... | collective-permute-start | bytes 491528 | tf_op jit(solution)/shard_map/ppermute | solution.py:205
  29.5 5.1 %collective-permute-start.7 = (bf16[1,16,1536]{2,1,0:T(8,128)(2,1)S(1)}, bf16[1,16,1536]{2,1,0:T(8,128)(2,1)S(1)}, u32[]{:S(2)}, u32[]{:S(2)}) collective-permute-start(bf16[1,16,1536]{2,1,0:T(8,128)(2,1)S(1)} %fusion.1), channel_id=1, source_target_pairs={{0,16},{4,20},{8,24},{12,28},{16,0},{20,4},{24,8},{28,12},{1,17},{... | collective-permute-start | bytes 147464 | tf_op jit(solution)/shard_map/ppermute | solution.py:205
  34.6 3.4 %copy-start = (bf16[2,1,8,64,4096]{4,3,2,1,0:T(8,128)(2,1)S(1)}, bf16[2,1,8,64,4096]{4,3,2,1,0:T(8,128)(2,1)}, u32[]{:S(2)}) copy-start(bf16[2,1,8,64,4096]{4,3,2,1,0:T(8,128)(2,1)} %param.10) | copy-start | bytes 25165828
  38.0 0.9 %copy-start.2 = (f32[16,4096]{1,0:T(8,128)S(1)}, f32[16,4096]{1,0:T(8,128)}, u32[]{:S(2)}) copy-start(f32[16,4096]{1,0:T(8,128)} %pair_gains.1.refs_2_) | copy-start | bytes 786436
  39.9 5.6 %copy-start.3 = (f32[8,16,64]{2,1,0:T(8,128)}, f32[8,16,64]{2,1,0:T(8,128)S(1)}, u32[]{:S(2)}) copy-start(f32[8,16,64]{2,1,0:T(8,128)S(1)} %project.3.refs_1_) | copy-start | bytes 98308
  40.1 5.4 %collective-permute-start.3 = (bf16[1,16,2560]{2,1,0:T(8,128)(2,1)S(1)}, bf16[1,16,2560]{2,1,0:T(8,128)(2,1)S(1)}, u32[]{:S(2)}, u32[]{:S(2)}) collective-permute-start(bf16[1,16,2560]{2,1,0:T(8,128)(2,1)S(1)} %fusion), channel_id=1, source_target_pairs={{0,16},{4,20},{8,24},{12,28},{16,0},{20,4},{24,8},{28,12},{1,17},{... | collective-permute-start | bytes 245768 | tf_op jit(solution)/shard_map/ppermute | solution.py:205
  45.5 3.4 %copy-start.1 = (bf16[2,1,8,64,4096]{4,3,2,1,0:T(8,128)(2,1)S(1)}, bf16[2,1,8,64,4096]{4,3,2,1,0:T(8,128)(2,1)}, u32[]{:S(2)}) copy-start(bf16[2,1,8,64,4096]{4,3,2,1,0:T(8,128)(2,1)} %param.10) | copy-start | bytes 25165828
  50.4 0.6 %copy-start.4 = (f32[8,16,64]{2,1,0:T(8,128)}, f32[8,16,64]{2,1,0:T(8,128)S(1)}, u32[]{:S(2)}) copy-start(f32[8,16,64]{2,1,0:T(8,128)S(1)} %project.2.refs_0_) | copy-start | bytes 98308
  53.6 1.2 %collective-permute-start.8 = (f32[2,2,128]{2,1,0:T(2,128)S(1)}, f32[2,2,128]{2,1,0:T(2,128)S(1)}, u32[]{:S(2)}, u32[]{:S(2)}) collective-permute-start(f32[2,2,128]{2,1,0:T(2,128)S(1)} %slice_bitcast_fusion.2), channel_id=1, source_target_pairs={{0,1},{1,0},{2,3},{3,2},{4,5},{5,4},{6,7},{7,6},{8,9},{9,8},{10,11... | collective-permute-start | bytes 6152 | tf_op jit(solution)/shard_map/ppermute | solution.py:205
  55.5 3.6 %collective-permute-start.9 = (f32[2,128]{1,0:T(2,128)S(1)}, f32[2,128]{1,0:T(2,128)S(1)}, u32[]{:S(2)}, u32[]{:S(2)}) collective-permute-start(f32[2,128]{1,0:T(2,128)S(1)} %slice_bitcast_fusion.4), channel_id=1, source_target_pairs={{0,2},{1,3},{2,0},{3,1},{4,6},{5,7},{6,4},{7,5},{8,10},{9,11},{10,... | collective-permute-start | bytes 3080 | tf_op jit(solution)/shard_map/ppermute | solution.py:205

commit v2 on v1

v2 whole, which is shorter than its diff:
```python
import functools

import jax
import jax.numpy as jnp
from jax import lax
from jax.experimental import pallas as pl
from jax.experimental.pallas import tpu as pltpu
from jax.sharding import PartitionSpec as P

LANES = 128
PARTS = ((5, 2), (3, 1))
MIB = 1 << 20
F32 = jnp.float32
BF16 = jnp.bfloat16
VMEM = pl.BlockSpec(memory_space=pltpu.VMEM)
SMEM = pl.BlockSpec(memory_space=pltpu.SMEM)
HBM = pl.BlockSpec(memory_space=pltpu.HBM)


def twiddles(place, order, groups, here, local_times):
    slots = groups * here
    high = groups // 4
    me = place[0]
    length = local_times * groups
    shape = (2 * slots, local_times)
    row = lax.broadcasted_iota(jnp.int32, shape, 0)
    wanted = jnp.right_shift(row, 1)
    held = jnp.zeros(shape, jnp.int32)
    for index in range(slots):
        relative, slot = divmod(index, here)
        owner = jnp.bitwise_xor(relative % high * 4 + relative // high, me)
        held = jnp.where(wanted == index, order[owner * here + slot], held)
    times = me * local_times + lax.broadcasted_iota(jnp.int32, shape, 1)
    phase = (held - slots // 2) * times
    phase = jnp.bitwise_and(phase, length - 1) if length & (length - 1) == 0 else phase % length
    angle = 2.0 * jnp.pi / length * phase.astype(F32)
    norm = 1.0 / jnp.sqrt(F32(length))
    cosine = jnp.cos(angle) * norm
    sine = jnp.sin(angle) * norm
    real = jnp.bitwise_and(row, 1) == 0
    return jnp.where(real, cosine, -sine).astype(BF16), jnp.where(real, sine, cosine).astype(BF16)


def transform_kernel(first, tiles, groups, place, order, vis_ref, *refs):
    outs, (held, sums, order_held, order_sem, sems) = refs[:-5], refs[-5:]
    _, chans, local_times, width = held.shape
    here = order.shape[0] // groups
    rows = 2 * order.shape[0]
    tile = width // tiles

    def copy(t, f):
        return pltpu.make_async_copy(
            vis_ref.at[:, f, :, pl.ds(first + t * tile, tile)],
            held.at[:, f, :, pl.ds(t * tile, tile)],
            sems.at[t, f],
        )

    for t in range(tiles):
        for f in range(chans):
            copy(t, f).start()
    order_copy = pltpu.make_async_copy(order, order_held, order_sem)
    order_copy.start()
    order_copy.wait()
    table_re, table_im = twiddles(place, order_held, groups, here, local_times)
    each = rows * chans // len(outs)
    for t in range(tiles):
        cols = pl.ds(t * tile, tile)
        for f in range(chans):
            copy(t, f).wait()
            both = jnp.dot(table_re, held[0, f, :, cols], preferred_element_type=F32) + jnp.dot(
                table_im, held[1, f, :, cols], preferred_element_type=F32
            )
            for lane in range(0, tile, LANES):
                sums[lane // LANES, pl.ds(f, rows, stride=chans), :] = both[:, lane : lane + LANES]
        for d, out in enumerate(outs):
            for lane in range(0, tile, LANES):
                part = sums[lane // LANES, pl.ds(d * each, each), :]
                out[:, :, pl.ds(t * tile + lane, LANES)] = part.reshape(*out.shape[:2], LANES).astype(out.dtype)


def transform(place, order, visibilities, first, width, tiles, groups):
    _, chans, times, _ = visibilities.shape
    rows = 2 * order.shape[0]
    shape = (rows // 8, 2 * chans, width)
    return pl.pallas_call(
        functools.partial(transform_kernel, first, tiles, groups),
        out_shape=[jax.ShapeDtypeStruct(shape, F32 if d == 0 else BF16) for d in range(4)],
        in_specs=[SMEM, HBM, HBM],
        out_specs=[VMEM] * 4,
        scratch_shapes=[
            pltpu.VMEM((2, chans, times, width), BF16),
            pltpu.VMEM((width // tiles // LANES, rows * chans, LANES), F32),
            pltpu.SMEM(order.shape, jnp.int32),
            pltpu.SemaphoreType.DMA,
            pltpu.SemaphoreType.DMA((tiles, chans)),
        ],
        compiler_params=pltpu.CompilerParams(vmem_limit_bytes=30 * MIB),
        cost_estimate=pl.CostEstimate(
            flops=64 * rows * 2 * chans * times * width,
            bytes_accessed=4 * chans * times * width,
            transcendentals=0,
        ),
        name="transform",
    )(place, order, visibilities)


def prepare_kernel(gains_ref, pairs_ref, beams_ref, out_ref, beams_out, sem):
    copy = pltpu.make_async_copy(beams_ref.at[:, 0], beams_out, sem)
    copy.start()
    chans = gains_ref.shape[1]
    groups = gains_ref.shape[2] // LANES

    def step(tile, _):
        cols = pl.ds(pl.multiple_of(tile * LANES, LANES), LANES)
        picked = []
        for side in range(2):
            index = jnp.broadcast_to(pairs_ref[side : side + 1, cols], (chans, LANES))
            low = jnp.bitwise_and(index, LANES - 1)
            high = jnp.right_shift(index, 7)
            for c in range(2):
                value = jnp.zeros((chans, LANES), F32)
                for group in range(groups):
                    table = gains_ref[c, :, group * LANES : (group + 1) * LANES]
                    value = jnp.where(high == group, jnp.take_along_axis(table, low, axis=1), value)
                picked.append(value)
        i_re, i_im, j_re, j_im = picked
        out_ref[0:chans, cols] = i_re * j_re + i_im * j_im
        out_ref[chans : 2 * chans, cols] = i_im * j_re - i_re * j_im
        return 0

    lax.fori_loop(0, pairs_ref.shape[1] // LANES, step, 0, unroll=8)
    copy.wait()


def prepare(feed_gains, feed_pairs, beam_rows):
    chans = feed_gains.shape[1]
    count = feed_pairs.shape[0]
    beams = (beam_rows.shape[0], *beam_rows.shape[2:])
    return pl.pallas_call(
        prepare_kernel,
        out_shape=[jax.ShapeDtypeStruct((2 * chans, count), F32), jax.ShapeDtypeStruct(beams, BF16)],
        in_specs=[VMEM, VMEM, HBM],
        out_specs=[VMEM, VMEM],
        scratch_shapes=[pltpu.SemaphoreType.DMA],
        compiler_params=pltpu.CompilerParams(vmem_limit_bytes=12 * MIB),
        cost_estimate=pl.CostEstimate(flops=4 << 20, bytes_accessed=9 << 20, transcendentals=0),
        name="prepare",
    )(feed_gains, feed_pairs.T, beam_rows)


def project_kernel(first, n_recv, *refs):
    keep, recvs = refs[0], refs[1 : 1 + n_recv]
    gains, beams, out = refs[1 + n_recv : 4 + n_recv]
    for f, value in enumerate(telescope(first, keep, recvs, gains, beams)):
        out[f] = value


def telescope(first, keep, recvs, gains, beams):
    _, chans, modes, _ = beams.shape
    width = keep.shape[1]
    total = keep[...]
    for recv in recvs:
        total = total + recv[...].astype(F32)
    cols = pl.ds(first, width)
    p_re, p_im = gains[0:chans, cols], gains[chans : 2 * chans, cols]
    re, im = total[:chans], total[chans:]
    spec = jnp.concatenate([re * p_re - im * p_im, re * p_im + im * p_re]).astype(BF16)
    found = []
    for f in range(chans):
        beam = jnp.concatenate([beams[0, f, :, cols], beams[1, f, :, cols]])
        both = lax.dot_general(spec, beam, (((1,), (1,)), ((), ())), preferred_element_type=F32)
        straight, crossed = both[:, :modes], both[:, modes:]
        found.append(
            jnp.concatenate([straight[:chans] - crossed[chans:], straight[chans:] + crossed[:chans]])
        )
    return found


def project(keep, recvs, gains, beams, first):
    _, chans, modes, _ = beams.shape
    width = keep.shape[1]
    return pl.pallas_call(
        functools.partial(project_kernel, first, len(recvs)),
        out_shape=jax.ShapeDtypeStruct((chans, 2 * chans, modes), F32),
        in_specs=[VMEM] * (3 + len(recvs)),
        out_specs=VMEM,
        compiler_params=pltpu.CompilerParams(vmem_limit_bytes=8 * MIB),
        cost_estimate=pl.CostEstimate(
            flops=16 * 4 * chans * modes * width * chans, bytes_accessed=4 * chans * modes * width, transcendentals=0
        ),
        name="project",
    )(keep, *recvs, gains, beams)


def finish_kernel(first, n_recv, n_tel, place, *refs):
    keep, recvs = refs[0], refs[1 : 1 + n_recv]
    gains, beams, basis = refs[1 + n_recv : 4 + n_recv]
    tels, outs = refs[4 + n_recv : 4 + n_recv + n_tel], refs[4 + n_recv + n_tel :]
    chans = basis.shape[0]
    last = telescope(first, keep, recvs, gains, beams)
    row = lax.broadcasted_iota(jnp.int32, last[0].shape, 0)
    total = jnp.zeros((2 * chans, basis.shape[2]), F32)
    for f in range(chans):
        tel = functools.reduce(lambda a, b: a + b, [t[f] for t in tels], last[f])
        tel = jnp.where(jnp.bitwise_and(row, chans - 1) == f, tel, 0.0).astype(BF16)
        total = total + jnp.dot(tel, basis[f], preferred_element_type=F32)
    both = jnp.concatenate(
        [jnp.sum(total[:chans], axis=0, keepdims=True), jnp.sum(total[chans:], axis=0, keepdims=True)]
    )
    me = place[1]
    width = outs[0].shape[2]
    for half, out in enumerate(outs):
        for high in range(out.shape[0]):
            value = jnp.zeros((2, width), F32)
            for block in range(2 * out.shape[0]):
                part = both[:, block * width : (block + 1) * width]
                value = jnp.where(jnp.bitwise_xor(block, me) == 2 * high + half, part, value)
            out[high] = value


def finish(place, keep, recvs, gains, beams, first, tels, basis, blocks):
    shape = jax.ShapeDtypeStruct((blocks // 2, 2, basis.shape[2] // blocks), F32)
    return pl.pallas_call(
        functools.partial(finish_kernel, first, len(recvs), len(tels)),
        out_shape=[shape, shape],
        in_specs=[SMEM] + [VMEM] * (4 + len(recvs) + len(tels)),
        out_specs=[VMEM, VMEM],
        compiler_params=pltpu.CompilerParams(vmem_limit_bytes=8 * MIB),
        name="finish",
    )(place, keep, *recvs, gains, beams, basis, *tels)


def swap(x, axis, mask):
    return lax.ppermute(x, axis, [(i, i ^ mask) for i in range(lax.axis_size(axis))])


def exchange(parts, shift):
    return [swap(part, "tm", d << shift) for d, part in enumerate(parts) if d]


def combine(parts, received, left):
    total = parts[0] + functools.reduce(lambda a, b: a + b, [r.astype(F32) for r in received])
    ways = min(4, left)
    total = total.reshape(left // ways, ways, *total.shape[1:])
    return [total[:, d] if d == 0 else total[:, d].astype(BF16) for d in range(ways)]


def on_device(visibilities, feed_gains, feed_pairs, m_order, beam_rows, kl_basis):
    groups = lax.axis_size("tm")
    count = visibilities.shape[3]
    place = jnp.stack([lax.axis_index("tm"), lax.axis_index("freq")]).astype(jnp.int32)
    shares = sum(share for share, _ in PARTS)
    firsts, sent, arrived = [0], [], []
    for share, tiles in PARTS:
        width = count // shares * share
        parts = transform(place, m_order, visibilities, firsts[-1], width, tiles, groups)
        if arrived:
            parts, arrived[-1][:1] = lax.optimization_barrier((parts, arrived[-1][:1]))
        sent.append(parts)
        arrived.append(exchange(parts, 0))
        firsts.append(firsts[-1] + width)
    spectra = []
    for index, (parts, received) in enumerate(zip(sent, arrived)):
        left, shift = groups // 4, 2
        if index == len(PARTS) - 1:
            received, gains = lax.optimization_barrier((received, gains))
        while left > 1:
            parts = combine(parts, received, left)
            received = exchange(parts, shift)
            left, shift = left // len(parts), shift + (len(parts) - 1).bit_length()
        if index == 0:
            feed_gains, parts = lax.optimization_barrier((feed_gains, parts))
            gains, beams = prepare(feed_gains, feed_pairs, beam_rows)
        spectra.append((parts[0][0], [r[0] for r in received]))
    tels = [project(keep, recvs, gains, beams, first) for first, (keep, recvs) in zip(firsts, spectra[:-1])]
    keep, recvs = spectra[-1]
    held, sent = finish(place, keep, recvs, gains, beams, firsts[-2], tels, kl_basis[0], lax.axis_size("freq"))
    held = held + swap(sent, "freq", 1)
    held = held[0] + swap(held[1], "freq", 2)
    return held[:, None, :]


def solution(mesh):
    placed = (
        P(None, "freq", "tm", None),
        P(None, "freq", None),
        P(),
        P(),
        P(None, "tm", "freq", None, None),
        P("tm", "freq", None, None),
    )
    return jax.shard_map(
        on_device, mesh=mesh, in_specs=placed, out_specs=P(None, "tm", "freq"), check_vma=False
    )
```

time: 59.9 us -> 41 us (0.68)
  local copies, waits for them, and re-layouts: 9.12 us -> 0.73 us
  Pallas kernels: 24.5 us -> 19.4 us
  waiting for transfers between devices: 7.41 us -> 4.14 us
  other arithmetic: 2.32 us -> 0.77 us
    unnamed x11 -> x14, local copies, waits for them, and re-layouts: 8.36 us -> 0.68 us
    pallas_call x4, Pallas kernels: 22 us -> 17.9 us  [the longest x2 14 us: transform(): pl.pallas_call(functools.partial(transform_kernel, first, tiles, groups),...]
    ppermute x10, waiting for transfers between devices: 7.41 us -> 4.14 us  [swap(): lax.ppermute(x, axis, [(i, i ^ mask) for i in range(lax.axis_size(axis))])]
    pallas_call x2 -> x1, Pallas kernels: 2.51 us -> 1.52 us  [project(): pl.pallas_call(functools.partial(project_kernel, first, len(recvs)), out_...]
    reduce_sum x1 -> x0, other arithmetic: 0.84 us -> none  [relative_table(): jnp.sum(jnp.where(wanted[:, None] == jnp.arange(slots, dtype=jnp.int32)[N...]
    squeeze x1, local copies, waits for them, and re-layouts: 0.67 us -> 0.01 us  [combine(): total[:, d]]
    add x2 -> x1, other arithmetic: 0.66 us -> 0.01 us  [on_device(): held = held + swap(sent, 'freq', 1)]
  transfers between devices with their start and end apart: 10 -> 10, of which waited for: 4 -> 4; matrix products, arithmetic and copies ran while one was open for 0% -> 0% of each run, Pallas kernels for 26% -> 24%
where the time goes in v2:
time: 41 us; the launch traced here: 40.9 us
  Pallas kernels  19.4 us (47%)
  starting transfers between devices  15.7 us (38%)
  waiting for transfers between devices  4.14 us (10%)
  other arithmetic  0.77 us (2%)
  local copies, waits for them, and re-layouts  0.73 us (2%)
    ppermute x10, starting transfers between devices, swap(): lax.ppermute(x, axis, [(i, i ^ mask) for i in range(lax.axis_size(axis))])  15.7 us
    pallas_call x2, Pallas kernels, transform(): pl.pallas_call(functools.partial(transform_kernel, first, tiles, groups),...  14 us
    ppermute x10, waiting for transfers between devices, swap(): lax.ppermute(x, axis, [(i, i ^ mask) for i in range(lax.axis_size(axis))])  4.14 us
    pallas_call x1, Pallas kernels, prepare(): pl.pallas_call(prepare_kernel, out_shape=[jax.ShapeDtypeStruct((2 * chans...  2.16 us
    pallas_call x1, Pallas kernels, finish(): pl.pallas_call(functools.partial(finish_kernel, first, len(recvs), len(te...  1.67 us
    pallas_call x1, Pallas kernels, project(): pl.pallas_call(functools.partial(project_kernel, first, len(recvs)), out_...  1.52 us
  transfers between devices with their start and end apart: 10, of which 4 were waited for; matrix products, arithmetic and copies ran while one was open for 0% of the time, Pallas kernels for 24%

profile of v2, /device:TPU:0, one launch (start us, length us, event | category | flops | bytes accessed | tf_op | source)
XLA Modules:
  0.0 40.9 jit_solution(708633908660927652)
XLA Ops:
  0.0 0.1 pad_add_fusion.place
  0.1 0.7 %copy-done.3 = s32[8]{0:T(128)S(1)} copy-done((s32[8]{0:T(128)S(1)}, s32[8]{0:T(128)}, u32[]{:S(2)}) %copy-start.3) | copy-done | bytes 56
  0.7 8.1 %transform.3 = (f32[2,16,2560]{2,1,0:T(8,128)S(1)}, bf16[2,16,2560]{2,1,0:T(8,128)(2,1)S(1)}, bf16[2,16,2560]{2,1,0:T(8,128)(2,1)S(1)}, bf16[2,16,2560]{2,1,0:T(8,128)(2,1)S(1)}) custom-call(s32[2]{0:T(128)S(1)} %pad_add_fusion.place, s32[8]{0:T(128)S(1)} %copy-done.3, bf16[2,8,256,4096]{3,2,1,0:T(8,128)(2,1)} %vis_ref.3), custom_call_target="tpu_custom_call" | custom-call | flops 10737418240 | bytes 20971520 | tf_op jit(solution)/shard_map/transform/pallas_call | solution.py:85
  8.8 3.0 %collective-permute-start = (bf16[2,16,2560]{2,1,0:T(8,128)(2,1)S(1)}, bf16[2,16,2560]{2,1,0:T(8,128)(2,1)S(1)}, u32[]{:S(2)}, u32[]{:S(2)}) collective-permute-start(bf16[2,16,2560]{2,1,0:T(8,128)(2,1)S(1)} %get-tuple-element.32), channel_id=1, source_target_pairs={{0,4},{4,0},{8,12},{12,8},{16,20},{20,16},{24,28},{28,24},{1,5},{5... | collective-permute-start | bytes 491528 | tf_op jit(solution)/shard_map/ppermute | solution.py:234
  11.8 1.6 %collective-permute-start.4 = (bf16[2,16,2560]{2,1,0:T(8,128)(2,1)S(1)}, bf16[2,16,2560]{2,1,0:T(8,128)(2,1)S(1)}, u32[]{:S(2)}, u32[]{:S(2)}) collective-permute-start(bf16[2,16,2560]{2,1,0:T(8,128)(2,1)S(1)} %get-tuple-element.39), channel_id=1, source_target_pairs={{0,8},{4,12},{8,0},{12,4},{16,24},{20,28},{24,16},{28,20},{1,9},{5... | collective-permute-start | bytes 491528 | tf_op jit(solution)/shard_map/ppermute | solution.py:234
  13.4 0.1 collective-permute-start.5
  13.5 5.9 %transform.2 = (f32[2,16,1536]{2,1,0:T(8,128)S(1)}, bf16[2,16,1536]{2,1,0:T(8,128)(2,1)S(1)}, bf16[2,16,1536]{2,1,0:T(8,128)(2,1)S(1)}, bf16[2,16,1536]{2,1,0:T(8,128)(2,1)S(1)}) custom-call(s32[2]{0:T(128)S(1)} %pad_add_fusion.place, s32[8]{0:T(128)S(1)} %copy-done.4, bf16[2,8,256,4096]{3,2,1,0:T(8,128)(2,1)} %vis_ref.3), custom_call_target="tpu_custom_call" | custom-call | flops 6442450944 | bytes 12582912 | tf_op jit(solution)/shard_map/transform/pallas_call | solution.py:85
  19.5 2.1 %collective-permute-start.1 = (bf16[2,16,1536]{2,1,0:T(8,128)(2,1)S(1)}, bf16[2,16,1536]{2,1,0:T(8,128)(2,1)S(1)}, u32[]{:S(2)}, u32[]{:S(2)}) collective-permute-start(bf16[2,16,1536]{2,1,0:T(8,128)(2,1)S(1)} %get-tuple-element.34), channel_id=1, source_target_pairs={{0,4},{4,0},{8,12},{12,8},{16,20},{20,16},{24,28},{28,24},{1,5},{5... | collective-permute-start | bytes 294920 | tf_op jit(solution)/shard_map/ppermute | solution.py:234
  21.6 1.1 %collective-permute-start.2 = (bf16[2,16,1536]{2,1,0:T(8,128)(2,1)S(1)}, bf16[2,16,1536]{2,1,0:T(8,128)(2,1)S(1)}, u32[]{:S(2)}, u32[]{:S(2)}) collective-permute-start(bf16[2,16,1536]{2,1,0:T(8,128)(2,1)S(1)} %get-tuple-element.35), channel_id=1, source_target_pairs={{0,8},{4,12},{8,0},{12,4},{16,24},{20,28},{24,16},{28,20},{1,9},{5... | collective-permute-start | bytes 294920 | tf_op jit(solution)/shard_map/ppermute | solution.py:234
  22.7 0.4 %collective-permute-start.3 = (bf16[2,16,1536]{2,1,0:T(8,128)(2,1)S(1)}, bf16[2,16,1536]{2,1,0:T(8,128)(2,1)S(1)}, u32[]{:S(2)}, u32[]{:S(2)}) collective-permute-start(bf16[2,16,1536]{2,1,0:T(8,128)(2,1)S(1)} %get-tuple-element.36), channel_id=1, source_target_pairs={{0,12},{4,8},{8,4},{12,0},{16,28},{20,24},{24,20},{28,16},{1,13},{... | collective-permute-start | bytes 294920 | tf_op jit(solution)/shard_map/ppermute | solution.py:234
  23.2 0.1 add_bitcast_fusion
  23.3 3.1 %collective-permute-start.7 = (bf16[1,16,2560]{2,1,0:T(8,128)(2,1)S(1)}, bf16[1,16,2560]{2,1,0:T(8,128)(2,1)S(1)}, u32[]{:S(2)}, u32[]{:S(2)}) collective-permute-start(bf16[1,16,2560]{2,1,0:T(8,128)(2,1)S(1)} %fusion), channel_id=1, source_target_pairs={{0,16},{4,20},{8,24},{12,28},{16,0},{20,4},{24,8},{28,12},{1,17},{... | collective-permute-start | bytes 245768 | tf_op jit(solution)/shard_map/ppermute | solution.py:234
  26.4 0.0 copy-start
  26.4 2.2 %prepare.1 = (f32[16,4096]{1,0:T(8,128)S(1)}, bf16[2,8,64,4096]{3,2,1,0:T(8,128)(2,1)S(1)}) custom-call(f32[2,8,1024]{2,1,0:T(8,128)S(1)} %copy-done.1, s32[2,4096]{1,0:T(2,128)S(1)} %bitcast.34, bf16[2,1,8,64,4096]{4,3,2,1,0:T(8,128)(2,1)S(1)} %bitcast.29), custom_call_target="tpu_custom_call" | custom-call | flops 4194304 | bytes 9437184 | tf_op jit(solution)/shard_map/prepare/pallas_call | solution.py:139
  28.6 0.1 collective-permute-done.3
  28.8 2.7 %collective-permute-start.6 = (bf16[1,16,1536]{2,1,0:T(8,128)(2,1)S(1)}, bf16[1,16,1536]{2,1,0:T(8,128)(2,1)S(1)}, u32[]{:S(2)}, u32[]{:S(2)}) collective-permute-start(bf16[1,16,1536]{2,1,0:T(8,128)(2,1)S(1)} %fusion.1), channel_id=1, source_target_pairs={{0,16},{4,20},{8,24},{12,28},{16,0},{20,4},{24,8},{28,12},{1,17},{... | collective-permute-start | bytes 147464 | tf_op jit(solution)/shard_map/ppermute | solution.py:234
  31.4 1.5 %project.1.refs_5_ = f32[8,16,64]{2,1,0:T(8,128)S(1)} custom-call(f32[16,2560]{1,0:T(8,128)S(1)} %bitcast.30, bf16[16,2560]{1,0:T(8,128)(2,1)S(1)} %bitcast.32, f32[16,4096]{1,0:T(8,128)S(1)} %get-tuple-element.46.refs_2_, bf16[2,8,64,4096]{3,2,1,0:T(8,128)(2,1)S(1)} %get-tuple-element.47.refs_3_), custom_call_target="tpu_custom_call" | custom-call | flops 671088640 | bytes 5242880 | tf_op jit(solution)/shard_map/project/pallas_call | solution.py:182
  32.9 0.9 %collective-permute-done.6 = bf16[1,16,1536]{2,1,0:T(8,128)(2,1)S(1)} collective-permute-done((bf16[1,16,1536]{2,1,0:T(8,128)(2,1)S(1)}, bf16[1,16,1536]{2,1,0:T(8,128)(2,1)S(1)}, u32[]{:S(2)}, u32[]{:S(2)}) %collective-permute-start.6) | collective-permute-done | bytes 49184 | tf_op jit(solution)/shard_map/ppermute | solution.py:234
  33.8 1.7 %finish.1 = (f32[2,2,128]{2,1,0:T(2,128)S(1)}, f32[2,2,128]{2,1,0:T(2,128)S(1)}) custom-call(s32[2]{0:T(128)S(1)} %pad_add_fusion.place, f32[16,1536]{1,0:T(8,128)S(1)} %slice_bitcast_fusion.1.refs_0_, bf16[16,1536]{1,0:T(8,128)(2,1)S(1)} %bitcast.33, f32[16,4096]{1,0:T(8,128)S(1)} %get-tuple-element.46.refs_2_, ...), custom_call_target="tpu_custom_call" | custom-call | tf_op jit(solution)/shard_map/finish/pallas_call | solution.py:223
  35.5 0.1 collective-permute-start.8
  35.6 1.1 %collective-permute-done.8 = f32[2,2,128]{2,1,0:T(2,128)S(1)} collective-permute-done((f32[2,2,128]{2,1,0:T(2,128)S(1)}, f32[2,2,128]{2,1,0:T(2,128)S(1)}, u32[]{:S(2)}, u32[]{:S(2)}) %collective-permute-start.8) | collective-permute-done | bytes 2080 | tf_op jit(solution)/shard_map/ppermute | solution.py:234
  36.7 1.5 %collective-permute-start.9 = (f32[2,128]{1,0:T(2,128)S(1)}, f32[2,128]{1,0:T(2,128)S(1)}, u32[]{:S(2)}, u32[]{:S(2)}) collective-permute-start(f32[2,128]{1,0:T(2,128)S(1)} %slice_bitcast_fusion.2), channel_id=1, source_target_pairs={{0,2},{1,3},{2,0},{3,1},{4,6},{5,7},{6,4},{7,5},{8,10},{9,11},{10,... | collective-permute-start | bytes 3080 | tf_op jit(solution)/shard_map/ppermute | solution.py:234
  38.3 2.0 %collective-permute-done.9 = f32[2,128]{1,0:T(2,128)S(1)} collective-permute-done((f32[2,128]{1,0:T(2,128)S(1)}, f32[2,128]{1,0:T(2,128)S(1)}, u32[]{:S(2)}, u32[]{:S(2)}) %collective-permute-start.9) | collective-permute-done | bytes 1056 | tf_op jit(solution)/shard_map/ppermute | solution.py:234
  40.3 0.6 %fusion.2 = f32[2,128]{1,0:T(2,128)} fusion(f32[2,128]{1,0:T(2,128)S(1)} %collective-permute-done.9, f32[2,2,128]{2,1,0:T(2,128)S(1)} %add.30), kind=kLoop, calls=%fused_computation.10 | loop fusion | flops 256 | bytes 3072 | tf_op jit(solution)/shard_map/add | solution.py:279
  (26 shorter events, 0.1 us)
Async XLA Ops:
  0.1 0.7 %copy-start.3 = (s32[8]{0:T(128)S(1)}, s32[8]{0:T(128)}, u32[]{:S(2)}) copy-start(s32[8]{0:T(128)} %order.3) | copy-start | bytes 100
  0.7 12.8 %copy-start.4 = (s32[8]{0:T(128)S(1)}, s32[8]{0:T(128)}, u32[]{:S(2)}) copy-start(s32[8]{0:T(128)} %order.3) | copy-start | bytes 100
  8.8 10.6 %collective-permute-start = (bf16[2,16,2560]{2,1,0:T(8,128)(2,1)S(1)}, bf16[2,16,2560]{2,1,0:T(8,128)(2,1)S(1)}, u32[]{:S(2)}, u32[]{:S(2)}) collective-permute-start(bf16[2,16,2560]{2,1,0:T(8,128)(2,1)S(1)} %get-tuple-element.32), channel_id=1, source_target_pairs={{0,4},{4,0},{8,12},{12,8},{16,20},{20,16},{24,28},{28,24},{1,5},{5... | collective-permute-start | bytes 491528 | tf_op jit(solution)/shard_map/ppermute | solution.py:234
  11.8 11.3 %collective-permute-start.4 = (bf16[2,16,2560]{2,1,0:T(8,128)(2,1)S(1)}, bf16[2,16,2560]{2,1,0:T(8,128)(2,1)S(1)}, u32[]{:S(2)}, u32[]{:S(2)}) collective-permute-start(bf16[2,16,2560]{2,1,0:T(8,128)(2,1)S(1)} %get-tuple-element.39), channel_id=1, source_target_pairs={{0,8},{4,12},{8,0},{12,4},{16,24},{20,28},{24,16},{28,20},{1,9},{5... | collective-permute-start | bytes 491528 | tf_op jit(solution)/shard_map/ppermute | solution.py:234
  13.4 13.0 %slice-start = ((s8[8388608]{0:T(1024)(128)(4,1)}), s8[4194304]{0:T(1024)(128)(4,1)S(1)}, s32[]{:S(2)}) async-start(s8[8388608]{0:T(1024)(128)(4,1)} %bitcast.28), calls=%async_computation | async-start | bytes 8388608
  13.4 13.0 %slice-start.1 = ((s8[8388608]{0:T(1024)(128)(4,1)}), s8[4194304]{0:T(1024)(128)(4,1)S(1)}, s32[]{:S(2)}) async-start(s8[8388608]{0:T(1024)(128)(4,1)} %bitcast.28), calls=%async_computation.1 | async-start | bytes 8388608
  13.4 13.0 %copy-start.1 = (f32[2,8,1024]{2,1,0:T(8,128)S(1)}, f32[2,8,1024]{2,1,0:T(8,128)}, u32[]{:S(2)}) copy-start(f32[2,8,1024]{2,1,0:T(8,128)} %gains_ref) | copy-start | bytes 196612
  13.4 13.0 %copy-start.2 = (s32[4096,2]{0,1:T(2,128)S(1)}, s32[4096,2]{0,1:T(2,128)}, u32[]{:S(2)}) copy-start(s32[4096,2]{0,1:T(2,128)} %param.8) | copy-start | bytes 98308
  13.4 9.7 %collective-permute-start.5 = (bf16[2,16,2560]{2,1,0:T(8,128)(2,1)S(1)}, bf16[2,16,2560]{2,1,0:T(8,128)(2,1)S(1)}, u32[]{:S(2)}, u32[]{:S(2)}) collective-permute-start(bf16[2,16,2560]{2,1,0:T(8,128)(2,1)S(1)} %get-tuple-element.40), channel_id=1, source_target_pairs={{0,12},{4,8},{8,4},{12,0},{16,28},{20,24},{24,20},{28,16},{1,13},{... | collective-permute-start | bytes 491528 | tf_op jit(solution)/shard_map/ppermute | solution.py:234
  19.5 9.1 %collective-permute-start.1 = (bf16[2,16,1536]{2,1,0:T(8,128)(2,1)S(1)}, bf16[2,16,1536]{2,1,0:T(8,128)(2,1)S(1)}, u32[]{:S(2)}, u32[]{:S(2)}) collective-permute-start(bf16[2,16,1536]{2,1,0:T(8,128)(2,1)S(1)} %get-tuple-element.34), channel_id=1, source_target_pairs={{0,4},{4,0},{8,12},{12,8},{16,20},{20,16},{24,28},{28,24},{1,5},{5... | collective-permute-start | bytes 294920 | tf_op jit(solution)/shard_map/ppermute | solution.py:234
  21.6 7.0 %collective-permute-start.2 = (bf16[2,16,1536]{2,1,0:T(8,128)(2,1)S(1)}, bf16[2,16,1536]{2,1,0:T(8,128)(2,1)S(1)}, u32[]{:S(2)}, u32[]{:S(2)}) collective-permute-start(bf16[2,16,1536]{2,1,0:T(8,128)(2,1)S(1)} %get-tuple-element.35), channel_id=1, source_target_pairs={{0,8},{4,12},{8,0},{12,4},{16,24},{20,28},{24,16},{28,20},{1,9},{5... | collective-permute-start | bytes 294920 | tf_op jit(solution)/shard_map/ppermute | solution.py:234
  22.7 6.0 %collective-permute-start.3 = (bf16[2,16,1536]{2,1,0:T(8,128)(2,1)S(1)}, bf16[2,16,1536]{2,1,0:T(8,128)(2,1)S(1)}, u32[]{:S(2)}, u32[]{:S(2)}) collective-permute-start(bf16[2,16,1536]{2,1,0:T(8,128)(2,1)S(1)} %get-tuple-element.36), channel_id=1, source_target_pairs={{0,12},{4,8},{8,4},{12,0},{16,28},{20,24},{24,20},{28,16},{1,13},{... | collective-permute-start | bytes 294920 | tf_op jit(solution)/shard_map/ppermute | solution.py:234
  23.3 8.1 %collective-permute-start.7 = (bf16[1,16,2560]{2,1,0:T(8,128)(2,1)S(1)}, bf16[1,16,2560]{2,1,0:T(8,128)(2,1)S(1)}, u32[]{:S(2)}, u32[]{:S(2)}) collective-permute-start(bf16[1,16,2560]{2,1,0:T(8,128)(2,1)S(1)} %fusion), channel_id=1, source_target_pairs={{0,16},{4,20},{8,24},{12,28},{16,0},{20,4},{24,8},{28,12},{1,17},{... | collective-permute-start | bytes 245768 | tf_op jit(solution)/shard_map/ppermute | solution.py:234
  26.4 7.4 %copy-start = (bf16[1,8,64,512]{3,2,1,0:T(8,128)(2,1)S(1)}, bf16[1,8,64,512]{3,2,1,0:T(8,128)(2,1)}, u32[]{:S(2)}) copy-start(bf16[1,8,64,512]{3,2,1,0:T(8,128)(2,1)} %param.11) | copy-start | bytes 1572868
  28.8 5.1 %collective-permute-start.6 = (bf16[1,16,1536]{2,1,0:T(8,128)(2,1)S(1)}, bf16[1,16,1536]{2,1,0:T(8,128)(2,1)S(1)}, u32[]{:S(2)}, u32[]{:S(2)}) collective-permute-start(bf16[1,16,1536]{2,1,0:T(8,128)(2,1)S(1)} %fusion.1), channel_id=1, source_target_pairs={{0,16},{4,20},{8,24},{12,28},{16,0},{20,4},{24,8},{28,12},{1,17},{... | collective-permute-start | bytes 147464 | tf_op jit(solution)/shard_map/ppermute | solution.py:234
  35.5 1.2 %collective-permute-start.8 = (f32[2,2,128]{2,1,0:T(2,128)S(1)}, f32[2,2,128]{2,1,0:T(2,128)S(1)}, u32[]{:S(2)}, u32[]{:S(2)}) collective-permute-start(f32[2,2,128]{2,1,0:T(2,128)S(1)} %get-tuple-element.50), channel_id=1, source_target_pairs={{0,1},{1,0},{2,3},{3,2},{4,5},{5,4},{6,7},{7,6},{8,9},{9,8},{10,11... | collective-permute-start | bytes 6152 | tf_op jit(solution)/shard_map/ppermute | solution.py:234
  36.7 3.6 %collective-permute-start.9 = (f32[2,128]{1,0:T(2,128)S(1)}, f32[2,128]{1,0:T(2,128)S(1)}, u32[]{:S(2)}, u32[]{:S(2)}) collective-permute-start(f32[2,128]{1,0:T(2,128)S(1)} %slice_bitcast_fusion.2), channel_id=1, source_target_pairs={{0,2},{1,3},{2,0},{3,1},{4,6},{5,7},{6,4},{7,5},{8,10},{9,11},{10,... | collective-permute-start | bytes 3080 | tf_op jit(solution)/shard_map/ppermute | solution.py:234

commit v3 on v2

--- a/solution.py
+++ b/solution.py
@@ -8,7 +8,8 @@
 from jax.sharding import PartitionSpec as P
 
 LANES = 128
-PARTS = ((5, 2), (3, 1))
+PARTS = ((11,11), (10,))
+SHARES = 32
 MIB = 1 << 20
 F32 = jnp.float32
 BF16 = jnp.bfloat16
@@ -41,21 +42,22 @@
     return jnp.where(real, cosine, -sine).astype(BF16), jnp.where(real, sine, cosine).astype(BF16)
 
 
-def transform_kernel(first, tiles, groups, place, order, vis_ref, *refs):
+def transform_kernel(first, ends, groups, place, order, vis_ref, *refs):
     outs, (held, sums, order_held, order_sem, sems) = refs[:-5], refs[-5:]
-    _, chans, local_times, width = held.shape
+    _, chans, local_times, _ = held.shape
     here = order.shape[0] // groups
     rows = 2 * order.shape[0]
-    tile = width // tiles
+    tiles = list(zip((0, *ends), ends))
 
     def copy(t, f):
+        begin, end = tiles[t]
         return pltpu.make_async_copy(
-            vis_ref.at[:, f, :, pl.ds(first + t * tile, tile)],
-            held.at[:, f, :, pl.ds(t * tile, tile)],
+            vis_ref.at[:, f, :, pl.ds(first + begin, end - begin)],
+            held.at[:, f, :, pl.ds(begin, end - begin)],
             sems.at[t, f],
         )
 
-    for t in range(tiles):
+    for t in range(len(tiles)):
         for f in range(chans):
             copy(t, f).start()
     order_copy = pltpu.make_async_copy(order, order_held, order_sem)
@@ -63,36 +65,38 @@
     order_copy.wait()
     table_re, table_im = twiddles(place, order_held, groups, here, local_times)
     each = rows * chans // len(outs)
-    for t in range(tiles):
-        cols = pl.ds(t * tile, tile)
+    for t, (begin, end) in enumerate(tiles):
+        cols = pl.ds(begin, end - begin)
         for f in range(chans):
             copy(t, f).wait()
             both = jnp.dot(table_re, held[0, f, :, cols], preferred_element_type=F32) + jnp.dot(
                 table_im, held[1, f, :, cols], preferred_element_type=F32
             )
-            for lane in range(0, tile, LANES):
+            for lane in range(0, end - begin, LANES):
                 sums[lane // LANES, pl.ds(f, rows, stride=chans), :] = both[:, lane : lane + LANES]
         for d, out in enumerate(outs):
-            for lane in range(0, tile, LANES):
+            for lane in range(0, end - begin, LANES):
                 part = sums[lane // LANES, pl.ds(d * each, each), :]
-                out[:, :, pl.ds(t * tile + lane, LANES)] = part.reshape(*out.shape[:2], LANES).astype(out.dtype)
-
-
-def transform(place, order, visibilities, first, width, tiles, groups):
+                out[:, :, pl.ds(begin + lane, LANES)] = part.reshape(*out.shape[:2], LANES).astype(out.dtype)
+
+
+def transform(place, order, visibilities, first, ends, groups):
     _, chans, times, _ = visibilities.shape
     rows = 2 * order.shape[0]
+    width = ends[-1]
+    widest = max(end - begin for begin, end in zip((0, *ends), ends))
     shape = (rows // 8, 2 * chans, width)
     return pl.pallas_call(
-        functools.partial(transform_kernel, first, tiles, groups),
+        functools.partial(transform_kernel, first, ends, groups),
         out_shape=[jax.ShapeDtypeStruct(shape, F32 if d == 0 else BF16) for d in range(4)],
         in_specs=[SMEM, HBM, HBM],
         out_specs=[VMEM] * 4,
         scratch_shapes=[
             pltpu.VMEM((2, chans, times, width), BF16),
-            pltpu.VMEM((width // tiles // LANES, rows * chans, LANES), F32),
+            pltpu.VMEM((widest // LANES, rows * chans, LANES), F32),
             pltpu.SMEM(order.shape, jnp.int32),
             pltpu.SemaphoreType.DMA,
-            pltpu.SemaphoreType.DMA((tiles, chans)),
+            pltpu.SemaphoreType.DMA((len(ends), chans)),
         ],
         compiler_params=pltpu.CompilerParams(vmem_limit_bytes=30 * MIB),
         cost_estimate=pl.CostEstimate(
@@ -104,9 +108,7 @@
     )(place, order, visibilities)
 
 
-def prepare_kernel(gains_ref, pairs_ref, beams_ref, out_ref, beams_out, sem):
-    copy = pltpu.make_async_copy(beams_ref.at[:, 0], beams_out, sem)
-    copy.start()
+def pair_gains_kernel(gains_ref, pairs_ref, out_ref):
     chans = gains_ref.shape[1]
     groups = gains_ref.shape[2] // LANES
 
@@ -129,23 +131,20 @@
         return 0
 
     lax.fori_loop(0, pairs_ref.shape[1] // LANES, step, 0, unroll=8)
-    copy.wait()
-
-
-def prepare(feed_gains, feed_pairs, beam_rows):
+
+
+def pair_gains(feed_gains, feed_pairs):
     chans = feed_gains.shape[1]
     count = feed_pairs.shape[0]
-    beams = (beam_rows.shape[0], *beam_rows.shape[2:])
-    return pl.pallas_call(
-        prepare_kernel,
-        out_shape=[jax.ShapeDtypeStruct((2 * chans, count), F32), jax.ShapeDtypeStruct(beams, BF16)],
-        in_specs=[VMEM, VMEM, HBM],
-        out_specs=[VMEM, VMEM],
-        scratch_shapes=[pltpu.SemaphoreType.DMA],
-        compiler_params=pltpu.CompilerParams(vmem_limit_bytes=12 * MIB),
-        cost_estimate=pl.CostEstimate(flops=4 << 20, bytes_accessed=9 << 20, transcendentals=0),
-        name="prepare",
-    )(feed_gains, feed_pairs.T, beam_rows)
+    return pl.pallas_call(
+        pair_gains_kernel,
+        out_shape=jax.ShapeDtypeStruct((2 * chans, count), F32),
+        in_specs=[VMEM, VMEM],
+        out_specs=VMEM,
+        compiler_params=pltpu.CompilerParams(vmem_limit_bytes=4 * MIB),
+        cost_estimate=pl.CostEstimate(flops=4 << 20, bytes_accessed=4 << 20, transcendentals=0),
+        name="pair_gains",
+    )(feed_gains, feed_pairs.T)
 
 
 def project_kernel(first, n_recv, *refs):
@@ -166,10 +165,10 @@
     re, im = total[:chans], total[chans:]
     spec = jnp.concatenate([re * p_re - im * p_im, re * p_im + im * p_re]).astype(BF16)
     found = []
-    for f in range(chans):
-        beam = jnp.concatenate([beams[0, f, :, cols], beams[1, f, :, cols]])
+    for f in range(0, chans, 2):
+        beam = jnp.concatenate([beams[0, f, :, cols], beams[0, f + 1, :, cols], beams[1, f, :, cols], beams[1, f + 1, :, cols]])
         both = lax.dot_general(spec, beam, (((1,), (1,)), ((), ())), preferred_element_type=F32)
-        straight, crossed = both[:, :modes], both[:, modes:]
+        straight, crossed = both[:, : 2 * modes], both[:, 2 * modes :]
         found.append(
             jnp.concatenate([straight[:chans] - crossed[chans:], straight[chans:] + crossed[:chans]])
         )
@@ -181,7 +180,7 @@
     width = keep.shape[1]
     return pl.pallas_call(
         functools.partial(project_kernel, first, len(recvs)),
-        out_shape=jax.ShapeDtypeStruct((chans, 2 * chans, modes), F32),
+        out_shape=jax.ShapeDtypeStruct((chans // 2, 2 * chans, 2 * modes), F32),
         in_specs=[VMEM] * (3 + len(recvs)),
         out_specs=VMEM,
         compiler_params=pltpu.CompilerParams(vmem_limit_bytes=8 * MIB),
@@ -196,35 +195,36 @@
     keep, recvs = refs[0], refs[1 : 1 + n_recv]
     gains, beams, basis = refs[1 + n_recv : 4 + n_recv]
     tels, outs = refs[4 + n_recv : 4 + n_recv + n_tel], refs[4 + n_recv + n_tel :]
-    chans = basis.shape[0]
+    chans = 2 * basis.shape[0]
     last = telescope(first, keep, recvs, gains, beams)
-    row = lax.broadcasted_iota(jnp.int32, last[0].shape, 0)
+    shape = last[0].shape
+    channel = lax.broadcasted_iota(jnp.int32, shape, 0) % chans
+    second = (lax.broadcasted_iota(jnp.int32, shape, 1) >= shape[1] // 2).astype(jnp.int32)
     total = jnp.zeros((2 * chans, basis.shape[2]), F32)
-    for f in range(chans):
-        tel = functools.reduce(lambda a, b: a + b, [t[f] for t in tels], last[f])
-        tel = jnp.where(jnp.bitwise_and(row, chans - 1) == f, tel, 0.0).astype(BF16)
-        total = total + jnp.dot(tel, basis[f], preferred_element_type=F32)
+    for pair, tel in enumerate(last):
+        tel = functools.reduce(lambda a, b: a + b, [t[pair] for t in tels], tel)
+        tel = jnp.where(channel == 2 * pair + second, tel, 0.0).astype(BF16)
+        total = total + jnp.dot(tel, basis[pair], preferred_element_type=F32)
     both = jnp.concatenate(
         [jnp.sum(total[:chans], axis=0, keepdims=True), jnp.sum(total[chans:], axis=0, keepdims=True)]
     )
     me = place[1]
-    width = outs[0].shape[2]
-    for half, out in enumerate(outs):
-        for high in range(out.shape[0]):
-            value = jnp.zeros((2, width), F32)
-            for block in range(2 * out.shape[0]):
-                part = both[:, block * width : (block + 1) * width]
-                value = jnp.where(jnp.bitwise_xor(block, me) == 2 * high + half, part, value)
-            out[high] = value
+    width = outs[0].shape[1]
+    for apart, out in enumerate(outs):
+        value = jnp.zeros((2, width), F32)
+        for block in range(len(outs)):
+            part = both[:, block * width : (block + 1) * width]
+            value = jnp.where(jnp.bitwise_xor(block, me) == apart, part, value)
+        out[...] = value
 
 
 def finish(place, keep, recvs, gains, beams, first, tels, basis, blocks):
-    shape = jax.ShapeDtypeStruct((blocks // 2, 2, basis.shape[2] // blocks), F32)
+    shape = jax.ShapeDtypeStruct((2, basis.shape[2] // blocks), F32)
     return pl.pallas_call(
         functools.partial(finish_kernel, first, len(recvs), len(tels)),
-        out_shape=[shape, shape],
+        out_shape=[shape] * blocks,
         in_specs=[SMEM] + [VMEM] * (4 + len(recvs) + len(tels)),
-        out_specs=[VMEM, VMEM],
+        out_specs=[VMEM] * blocks,
         compiler_params=pltpu.CompilerParams(vmem_limit_bytes=8 * MIB),
         name="finish",
     )(place, keep, *recvs, gains, beams, basis, *tels)
@@ -249,17 +249,17 @@
     groups = lax.axis_size("tm")
     count = visibilities.shape[3]
     place = jnp.stack([lax.axis_index("tm"), lax.axis_index("freq")]).astype(jnp.int32)
-    shares = sum(share for share, _ in PARTS)
     firsts, sent, arrived = [0], [], []
-    for share, tiles in PARTS:
-        width = count // shares * share
-        parts = transform(place, m_order, visibilities, firsts[-1], width, tiles, groups)
+    for tiles in PARTS:
+        ends = tuple(count // SHARES * sum(tiles[: t + 1]) for t in range(len(tiles)))
+        parts = transform(place, m_order, visibilities, firsts[-1], ends, groups)
         if arrived:
             parts, arrived[-1][:1] = lax.optimization_barrier((parts, arrived[-1][:1]))
         sent.append(parts)
         arrived.append(exchange(parts, 0))
-        firsts.append(firsts[-1] + width)
+        firsts.append(firsts[-1] + ends[-1])
     spectra = []
+    beams = beam_rows[:, 0]
     for index, (parts, received) in enumerate(zip(sent, arrived)):
         left, shift = groups // 4, 2
         if index == len(PARTS) - 1:
@@ -270,13 +270,13 @@
             left, shift = left // len(parts), shift + (len(parts) - 1).bit_length()
         if index == 0:
             feed_gains, parts = lax.optimization_barrier((feed_gains, parts))
-            gains, beams = prepare(feed_gains, feed_pairs, beam_rows)
+            gains = pair_gains(feed_gains, feed_pairs)
         spectra.append((parts[0][0], [r[0] for r in received]))
     tels = [project(keep, recvs, gains, beams, first) for first, (keep, recvs) in zip(firsts, spectra[:-1])]
     keep, recvs = spectra[-1]
-    held, sent = finish(place, keep, recvs, gains, beams, firsts[-2], tels, kl_basis[0], lax.axis_size("freq"))
-    held = held + swap(sent, "freq", 1)
-    held = held[0] + swap(held[1], "freq", 2)
+    basis = kl_basis.reshape(kl_basis.shape[1] // 2, 2 * kl_basis.shape[2], kl_basis.shape[3])
+    held, *sent = finish(place, keep, recvs, gains, beams, firsts[-2], tels, basis, lax.axis_size("freq"))
+    held = functools.reduce(lambda a, b: a + b, [swap(part, "freq", d + 1) for d, part in enumerate(sent)], held)
     return held[:, None, :]
 
 

time: 41 us -> 40.1 us (0.978)
  Pallas kernels: 19.4 us -> 18.6 us
    pallas_call x3, Pallas kernels: 16.2 us -> 15.6 us  [the longest x2 14 us: transform(): pl.pallas_call(functools.partial(transform_kernel, first, ends, groups),...]
    ppermute x10 -> x11, waiting for transfers between devices: 4.14 us -> 3.73 us  [swap(): lax.ppermute(x, axis, [(i, i ^ mask) for i in range(lax.axis_size(axis))])]
    ppermute x10 -> x11, starting transfers between devices: 15.7 us -> 15.9 us  [swap(): lax.ppermute(x, axis, [(i, i ^ mask) for i in range(lax.axis_size(axis))])]
  transfers between devices with their start and end apart: 10 -> 11, of which waited for: 4 -> 4; matrix products, arithmetic and copies ran while one was open for 0% -> 0% of each run, Pallas kernels for 24% -> 21%
where the time goes in v3:
time: 40.1 us; the launch traced here: 39.9 us
  Pallas kernels  18.6 us (46%)
  starting transfers between devices  15.9 us (40%)
  waiting for transfers between devices  3.73 us (9%)
  other arithmetic  0.76 us (2%)
  local copies, waits for them, and re-layouts  0.72 us (2%)
    ppermute x11, starting transfers between devices, swap(): lax.ppermute(x, axis, [(i, i ^ mask) for i in range(lax.axis_size(axis))])  15.9 us
    pallas_call x2, Pallas kernels, transform(): pl.pallas_call(functools.partial(transform_kernel, first, ends, groups),...  14 us
    ppermute x11, waiting for transfers between devices, swap(): lax.ppermute(x, axis, [(i, i ^ mask) for i in range(lax.axis_size(axis))])  3.73 us
    pallas_call x1, Pallas kernels, project(): pl.pallas_call(functools.partial(project_kernel, first, len(recvs)), out_...  1.59 us
    pallas_call x1, Pallas kernels, pair_gains(): pl.pallas_call(pair_gains_kernel, out_shape=jax.ShapeDtypeStruct((2 * cha...  1.59 us
    pallas_call x1, Pallas kernels, finish(): pl.pallas_call(functools.partial(finish_kernel, first, len(recvs), len(te...  1.48 us
  transfers between devices with their start and end apart: 11, of which 4 were waited for; matrix products, arithmetic and copies ran while one was open for 0% of the time, Pallas kernels for 21%

profile of v3, /device:TPU:0, one launch (start us, length us, event | category | flops | bytes accessed | tf_op | source)
XLA Modules:
  0.0 39.9 jit_solution(16662504249240173740)
XLA Ops:
  0.0 0.1 pad_add_fusion.place
  0.1 0.7 %copy-done.3 = s32[8]{0:T(128)S(1)} copy-done((s32[8]{0:T(128)S(1)}, s32[8]{0:T(128)}, u32[]{:S(2)}) %copy-start.3) | copy-done | bytes 56
  0.7 8.7 %transform.3 = (f32[2,16,2816]{2,1,0:T(8,128)S(1)}, bf16[2,16,2816]{2,1,0:T(8,128)(2,1)S(1)}, bf16[2,16,2816]{2,1,0:T(8,128)(2,1)S(1)}, bf16[2,16,2816]{2,1,0:T(8,128)(2,1)S(1)}) custom-call(s32[2]{0:T(128)S(1)} %pad_add_fusion.place, s32[8]{0:T(128)S(1)} %copy-done.3, bf16[2,8,256,4096]{3,2,1,0:T(8,128)(2,1)} %vis_ref.3), custom_call_target="tpu_custom_call" | custom-call | flops 11811160064 | bytes 23068672 | tf_op jit(solution)/shard_map/transform/pallas_call | solution.py:89
  9.5 0.0 slice-start
  9.5 3.0 %collective-permute-start = (bf16[2,16,2816]{2,1,0:T(8,128)(2,1)S(1)}, bf16[2,16,2816]{2,1,0:T(8,128)(2,1)S(1)}, u32[]{:S(2)}, u32[]{:S(2)}) collective-permute-start(bf16[2,16,2816]{2,1,0:T(8,128)(2,1)S(1)} %get-tuple-element.32), channel_id=1, source_target_pairs={{0,4},{4,0},{8,12},{12,8},{16,20},{20,16},{24,28},{28,24},{1,5},{5... | collective-permute-start | bytes 540680 | tf_op jit(solution)/shard_map/ppermute | solution.py:234
  12.5 1.6 %collective-permute-start.4 = (bf16[2,16,2816]{2,1,0:T(8,128)(2,1)S(1)}, bf16[2,16,2816]{2,1,0:T(8,128)(2,1)S(1)}, u32[]{:S(2)}, u32[]{:S(2)}) collective-permute-start(bf16[2,16,2816]{2,1,0:T(8,128)(2,1)S(1)} %get-tuple-element.39), channel_id=1, source_target_pairs={{0,8},{4,12},{8,0},{12,4},{16,24},{20,28},{24,16},{28,20},{1,9},{5... | collective-permute-start | bytes 540680 | tf_op jit(solution)/shard_map/ppermute | solution.py:234
  14.1 5.3 %transform.2 = (f32[2,16,1280]{2,1,0:T(8,128)S(1)}, bf16[2,16,1280]{2,1,0:T(8,128)(2,1)S(1)}, bf16[2,16,1280]{2,1,0:T(8,128)(2,1)S(1)}, bf16[2,16,1280]{2,1,0:T(8,128)(2,1)S(1)}) custom-call(s32[2]{0:T(128)S(1)} %pad_add_fusion.place, s32[8]{0:T(128)S(1)} %copy-done.3, bf16[2,8,256,4096]{3,2,1,0:T(8,128)(2,1)} %vis_ref.3), custom_call_target="tpu_custom_call" | custom-call | flops 5368709120 | bytes 10485760 | tf_op jit(solution)/shard_map/transform/pallas_call | solution.py:89
  19.4 1.7 %collective-permute-start.1 = (bf16[2,16,1280]{2,1,0:T(8,128)(2,1)S(1)}, bf16[2,16,1280]{2,1,0:T(8,128)(2,1)S(1)}, u32[]{:S(2)}, u32[]{:S(2)}) collective-permute-start(bf16[2,16,1280]{2,1,0:T(8,128)(2,1)S(1)} %get-tuple-element.34), channel_id=1, source_target_pairs={{0,4},{4,0},{8,12},{12,8},{16,20},{20,16},{24,28},{28,24},{1,5},{5... | collective-permute-start | bytes 245768 | tf_op jit(solution)/shard_map/ppermute | solution.py:234
  21.1 1.6 %collective-permute-start.2 = (bf16[2,16,1280]{2,1,0:T(8,128)(2,1)S(1)}, bf16[2,16,1280]{2,1,0:T(8,128)(2,1)S(1)}, u32[]{:S(2)}, u32[]{:S(2)}) collective-permute-start(bf16[2,16,1280]{2,1,0:T(8,128)(2,1)S(1)} %get-tuple-element.35), channel_id=1, source_target_pairs={{0,8},{4,12},{8,0},{12,4},{16,24},{20,28},{24,16},{28,20},{1,9},{5... | collective-permute-start | bytes 245768 | tf_op jit(solution)/shard_map/ppermute | solution.py:234
  22.6 0.3 collective-permute-start.3
  22.9 0.1 add_bitcast_fusion
  23.0 3.1 %collective-permute-start.7 = (bf16[1,16,2816]{2,1,0:T(8,128)(2,1)S(1)}, bf16[1,16,2816]{2,1,0:T(8,128)(2,1)S(1)}, u32[]{:S(2)}, u32[]{:S(2)}) collective-permute-start(bf16[1,16,2816]{2,1,0:T(8,128)(2,1)S(1)} %fusion), channel_id=1, source_target_pairs={{0,16},{4,20},{8,24},{12,28},{16,0},{20,4},{24,8},{28,12},{1,17},{... | collective-permute-start | bytes 270344 | tf_op jit(solution)/shard_map/ppermute | solution.py:234
  26.1 1.6 %pair_gains.1.refs_2_ = f32[16,4096]{1,0:T(8,128)S(1)} custom-call(f32[2,8,1024]{2,1,0:T(8,128)S(1)} %copy-done.1, s32[2,4096]{1,0:T(2,128)S(1)} %bitcast.31), custom_call_target="tpu_custom_call" | custom-call | flops 4194304 | bytes 4194304 | tf_op jit(solution)/shard_map/pair_gains/pallas_call | solution.py:139
  27.7 0.3 collective-permute-done.3
  28.1 2.8 %collective-permute-start.6 = (bf16[1,16,1280]{2,1,0:T(8,128)(2,1)S(1)}, bf16[1,16,1280]{2,1,0:T(8,128)(2,1)S(1)}, u32[]{:S(2)}, u32[]{:S(2)}) collective-permute-start(bf16[1,16,1280]{2,1,0:T(8,128)(2,1)S(1)} %fusion.1), channel_id=1, source_target_pairs={{0,16},{4,20},{8,24},{12,28},{16,0},{20,4},{24,8},{28,12},{1,17},{... | collective-permute-start | bytes 122888 | tf_op jit(solution)/shard_map/ppermute | solution.py:234
  30.9 1.6 %project.1.refs_5_ = f32[4,16,128]{2,1,0:T(8,128)S(1)} custom-call(f32[16,2816]{1,0:T(8,128)S(1)} %bitcast.27, bf16[16,2816]{1,0:T(8,128)(2,1)S(1)} %bitcast.29, f32[16,4096]{1,0:T(8,128)S(1)} %pair_gains.1.refs_2_, bf16[2,8,64,4096]{3,2,1,0:T(8,128)(2,1)S(1)} %bitcast.25), custom_call_target="tpu_custom_call" | custom-call | flops 738197504 | bytes 5767168 | tf_op jit(solution)/shard_map/project/pallas_call | solution.py:181
  32.5 0.6 %collective-permute-done.6 = bf16[1,16,1280]{2,1,0:T(8,128)(2,1)S(1)} collective-permute-done((bf16[1,16,1280]{2,1,0:T(8,128)(2,1)S(1)}, bf16[1,16,1280]{2,1,0:T(8,128)(2,1)S(1)}, u32[]{:S(2)}, u32[]{:S(2)}) %collective-permute-start.6) | collective-permute-done | bytes 40992 | tf_op jit(solution)/shard_map/ppermute | solution.py:234
  33.1 1.5 %finish.1 = (f32[2,128]{1,0:T(2,128)S(1)}, f32[2,128]{1,0:T(2,128)S(1)}, f32[2,128]{1,0:T(2,128)S(1)}, f32[2,128]{1,0:T(2,128)S(1)}) custom-call(s32[2]{0:T(128)S(1)} %pad_add_fusion.place, f32[16,1280]{1,0:T(8,128)S(1)} %slice_bitcast_fusion.1.refs_0_, bf16[16,1280]{1,0:T(8,128)(2,1)S(1)} %bitcast.30, f32[16,4096]{1,0:T(8,128)S(1)} %pair_gains.1.refs_2_, ...), custom_call_target="tpu_custom_call" | custom-call | tf_op jit(solution)/shard_map/finish/pallas_call | solution.py:223
  34.6 0.1 collective-permute-start.8
  34.7 1.7 %collective-permute-start.9 = (f32[2,128]{1,0:T(2,128)S(1)}, f32[2,128]{1,0:T(2,128)S(1)}, u32[]{:S(2)}, u32[]{:S(2)}) collective-permute-start(f32[2,128]{1,0:T(2,128)S(1)} %get-tuple-element.49), channel_id=1, source_target_pairs={{0,2},{1,3},{2,0},{3,1},{4,6},{5,7},{6,4},{7,5},{8,10},{9,11},{10,... | collective-permute-start | bytes 3080 | tf_op jit(solution)/shard_map/ppermute | solution.py:234
  36.4 0.2 collective-permute-start.10
  36.5 1.8 %collective-permute-done.9 = f32[2,128]{1,0:T(2,128)S(1)} collective-permute-done((f32[2,128]{1,0:T(2,128)S(1)}, f32[2,128]{1,0:T(2,128)S(1)}, u32[]{:S(2)}, u32[]{:S(2)}) %collective-permute-start.9) | collective-permute-done | bytes 1056 | tf_op jit(solution)/shard_map/ppermute | solution.py:234
  38.3 1.1 %collective-permute-done.10 = f32[2,128]{1,0:T(2,128)S(1)} collective-permute-done((f32[2,128]{1,0:T(2,128)S(1)}, f32[2,128]{1,0:T(2,128)S(1)}, u32[]{:S(2)}, u32[]{:S(2)}) %collective-permute-start.10) | collective-permute-done | bytes 1056 | tf_op jit(solution)/shard_map/ppermute | solution.py:234
  39.4 0.6 %add_add_fusion = f32[2,128]{1,0:T(2,128)} fusion(f32[2,128]{1,0:T(2,128)S(1)} %collective-permute-done.10, f32[2,128]{1,0:T(2,128)S(1)} %collective-permute-done.9, f32[2,128]{1,0:T(2,128)S(1)} %get-tuple-element.47, f32[2,128]{1,0:T(2,128)S(1)} %collective-permute-done.8), kind=kLoop, calls=%fused_computation.8 | loop fusion | flops 768 | bytes 5120 | tf_op jit(solution)/shard_map/add | solution.py:279
  (24 shorter events, 0.1 us)
Async XLA Ops:
  0.1 0.7 %copy-start.3 = (s32[8]{0:T(128)S(1)}, s32[8]{0:T(128)}, u32[]{:S(2)}) copy-start(s32[8]{0:T(128)} %order.3) | copy-start | bytes 100
  0.7 25.4 %copy-start.1 = (f32[2,8,1024]{2,1,0:T(8,128)S(1)}, f32[2,8,1024]{2,1,0:T(8,128)}, u32[]{:S(2)}) copy-start(f32[2,8,1024]{2,1,0:T(8,128)} %gains_ref) | copy-start | bytes 196612
  0.7 25.4 %copy-start.2 = (s32[4096,2]{0,1:T(2,128)S(1)}, s32[4096,2]{0,1:T(2,128)}, u32[]{:S(2)}) copy-start(s32[4096,2]{0,1:T(2,128)} %param.8) | copy-start | bytes 98308
  9.5 21.5 %slice-start = ((s8[8388608]{0:T(1024)(128)(4,1)}), s8[4194304]{0:T(1024)(128)(4,1)S(1)}, s32[]{:S(2)}) async-start(s8[8388608]{0:T(1024)(128)(4,1)} %bitcast.23), calls=%async_computation | async-start | bytes 8388608
  9.5 23.6 %copy-start = (bf16[1,8,64,512]{3,2,1,0:T(8,128)(2,1)S(1)}, bf16[1,8,64,512]{3,2,1,0:T(8,128)(2,1)}, u32[]{:S(2)}) copy-start(bf16[1,8,64,512]{3,2,1,0:T(8,128)(2,1)} %param.11) | copy-start | bytes 1572868
  9.5 9.9 %collective-permute-start = (bf16[2,16,2816]{2,1,0:T(8,128)(2,1)S(1)}, bf16[2,16,2816]{2,1,0:T(8,128)(2,1)S(1)}, u32[]{:S(2)}, u32[]{:S(2)}) collective-permute-start(bf16[2,16,2816]{2,1,0:T(8,128)(2,1)S(1)} %get-tuple-element.32), channel_id=1, source_target_pairs={{0,4},{4,0},{8,12},{12,8},{16,20},{20,16},{24,28},{28,24},{1,5},{5... | collective-permute-start | bytes 540680 | tf_op jit(solution)/shard_map/ppermute | solution.py:234
  12.5 10.4 %collective-permute-start.4 = (bf16[2,16,2816]{2,1,0:T(8,128)(2,1)S(1)}, bf16[2,16,2816]{2,1,0:T(8,128)(2,1)S(1)}, u32[]{:S(2)}, u32[]{:S(2)}) collective-permute-start(bf16[2,16,2816]{2,1,0:T(8,128)(2,1)S(1)} %get-tuple-element.39), channel_id=1, source_target_pairs={{0,8},{4,12},{8,0},{12,4},{16,24},{20,28},{24,16},{28,20},{1,9},{5... | collective-permute-start | bytes 540680 | tf_op jit(solution)/shard_map/ppermute | solution.py:234
  14.1 16.8 %slice-start.1 = ((s8[8388608]{0:T(1024)(128)(4,1)}), s8[4194304]{0:T(1024)(128)(4,1)S(1)}, s32[]{:S(2)}) async-start(s8[8388608]{0:T(1024)(128)(4,1)} %bitcast.23), calls=%async_computation.1 | async-start | bytes 8388608
  14.1 8.9 %collective-permute-start.5 = (bf16[2,16,2816]{2,1,0:T(8,128)(2,1)S(1)}, bf16[2,16,2816]{2,1,0:T(8,128)(2,1)S(1)}, u32[]{:S(2)}, u32[]{:S(2)}) collective-permute-start(bf16[2,16,2816]{2,1,0:T(8,128)(2,1)S(1)} %get-tuple-element.40), channel_id=1, source_target_pairs={{0,12},{4,8},{8,4},{12,0},{16,28},{20,24},{24,20},{28,16},{1,13},{... | collective-permute-start | bytes 540680 | tf_op jit(solution)/shard_map/ppermute | solution.py:234
  19.4 8.4 %collective-permute-start.1 = (bf16[2,16,1280]{2,1,0:T(8,128)(2,1)S(1)}, bf16[2,16,1280]{2,1,0:T(8,128)(2,1)S(1)}, u32[]{:S(2)}, u32[]{:S(2)}) collective-permute-start(bf16[2,16,1280]{2,1,0:T(8,128)(2,1)S(1)} %get-tuple-element.34), channel_id=1, source_target_pairs={{0,4},{4,0},{8,12},{12,8},{16,20},{20,16},{24,28},{28,24},{1,5},{5... | collective-permute-start | bytes 245768 | tf_op jit(solution)/shard_map/ppermute | solution.py:234
  21.1 6.7 %collective-permute-start.2 = (bf16[2,16,1280]{2,1,0:T(8,128)(2,1)S(1)}, bf16[2,16,1280]{2,1,0:T(8,128)(2,1)S(1)}, u32[]{:S(2)}, u32[]{:S(2)}) collective-permute-start(bf16[2,16,1280]{2,1,0:T(8,128)(2,1)S(1)} %get-tuple-element.35), channel_id=1, source_target_pairs={{0,8},{4,12},{8,0},{12,4},{16,24},{20,28},{24,16},{28,20},{1,9},{5... | collective-permute-start | bytes 245768 | tf_op jit(solution)/shard_map/ppermute | solution.py:234
  22.6 5.4 %collective-permute-start.3 = (bf16[2,16,1280]{2,1,0:T(8,128)(2,1)S(1)}, bf16[2,16,1280]{2,1,0:T(8,128)(2,1)S(1)}, u32[]{:S(2)}, u32[]{:S(2)}) collective-permute-start(bf16[2,16,1280]{2,1,0:T(8,128)(2,1)S(1)} %get-tuple-element.36), channel_id=1, source_target_pairs={{0,12},{4,8},{8,4},{12,0},{16,28},{20,24},{24,20},{28,16},{1,13},{... | collective-permute-start | bytes 245768 | tf_op jit(solution)/shard_map/ppermute | solution.py:234
  23.0 7.9 %collective-permute-start.7 = (bf16[1,16,2816]{2,1,0:T(8,128)(2,1)S(1)}, bf16[1,16,2816]{2,1,0:T(8,128)(2,1)S(1)}, u32[]{:S(2)}, u32[]{:S(2)}) collective-permute-start(bf16[1,16,2816]{2,1,0:T(8,128)(2,1)S(1)} %fusion), channel_id=1, source_target_pairs={{0,16},{4,20},{8,24},{12,28},{16,0},{20,4},{24,8},{28,12},{1,17},{... | collective-permute-start | bytes 270344 | tf_op jit(solution)/shard_map/ppermute | solution.py:234
  28.1 5.0 %collective-permute-start.6 = (bf16[1,16,1280]{2,1,0:T(8,128)(2,1)S(1)}, bf16[1,16,1280]{2,1,0:T(8,128)(2,1)S(1)}, u32[]{:S(2)}, u32[]{:S(2)}) collective-permute-start(bf16[1,16,1280]{2,1,0:T(8,128)(2,1)S(1)} %fusion.1), channel_id=1, source_target_pairs={{0,16},{4,20},{8,24},{12,28},{16,0},{20,4},{24,8},{28,12},{1,17},{... | collective-permute-start | bytes 122888 | tf_op jit(solution)/shard_map/ppermute | solution.py:234
  34.6 1.9 %collective-permute-start.8 = (f32[2,128]{1,0:T(2,128)S(1)}, f32[2,128]{1,0:T(2,128)S(1)}, u32[]{:S(2)}, u32[]{:S(2)}) collective-permute-start(f32[2,128]{1,0:T(2,128)S(1)} %get-tuple-element.48), channel_id=1, source_target_pairs={{0,1},{1,0},{2,3},{3,2},{4,5},{5,4},{6,7},{7,6},{8,9},{9,8},{10,11... | collective-permute-start | bytes 3080 | tf_op jit(solution)/shard_map/ppermute | solution.py:234
  34.7 3.6 %collective-permute-start.9 = (f32[2,128]{1,0:T(2,128)S(1)}, f32[2,128]{1,0:T(2,128)S(1)}, u32[]{:S(2)}, u32[]{:S(2)}) collective-permute-start(f32[2,128]{1,0:T(2,128)S(1)} %get-tuple-element.49), channel_id=1, source_target_pairs={{0,2},{1,3},{2,0},{3,1},{4,6},{5,7},{6,4},{7,5},{8,10},{9,11},{10,... | collective-permute-start | bytes 3080 | tf_op jit(solution)/shard_map/ppermute | solution.py:234
  36.4 3.0 %collective-permute-start.10 = (f32[2,128]{1,0:T(2,128)S(1)}, f32[2,128]{1,0:T(2,128)S(1)}, u32[]{:S(2)}, u32[]{:S(2)}) collective-permute-start(f32[2,128]{1,0:T(2,128)S(1)} %get-tuple-element.50), channel_id=1, source_target_pairs={{0,3},{1,2},{2,1},{3,0},{4,7},{5,6},{6,5},{7,4},{8,11},{9,10},{10,... | collective-permute-start | bytes 3080 | tf_op jit(solution)/shard_map/ppermute | solution.py:234

commit v4 on v3

--- a/solution.py
+++ b/solution.py
@@ -8,7 +8,7 @@
 from jax.sharding import PartitionSpec as P
 
 LANES = 128
-PARTS = ((11,11), (10,))
+PARTS = ((11, 11), (10,))
 SHARES = 32
 MIB = 1 << 20
 F32 = jnp.float32
@@ -18,7 +18,7 @@
 HBM = pl.BlockSpec(memory_space=pltpu.HBM)
 
 
-def twiddles(place, order, groups, here, local_times):
+def twiddles(place, groups, here, local_times):
     slots = groups * here
     high = groups // 4
     me = place[0]
@@ -30,7 +30,7 @@
     for index in range(slots):
         relative, slot = divmod(index, here)
         owner = jnp.bitwise_xor(relative % high * 4 + relative // high, me)
-        held = jnp.where(wanted == index, order[owner * here + slot], held)
+        held = jnp.where(wanted == index, place[2 + owner * here + slot], held)
     times = me * local_times + lax.broadcasted_iota(jnp.int32, shape, 1)
     phase = (held - slots // 2) * times
     phase = jnp.bitwise_and(phase, length - 1) if length & (length - 1) == 0 else phase % length
@@ -42,11 +42,11 @@
     return jnp.where(real, cosine, -sine).astype(BF16), jnp.where(real, sine, cosine).astype(BF16)
 
 
-def transform_kernel(first, ends, groups, place, order, vis_ref, *refs):
-    outs, (held, sums, order_held, order_sem, sems) = refs[:-5], refs[-5:]
+def transform_kernel(first, ends, groups, place, vis_ref, *refs):
+    outs, (held, sums, sems) = refs[:-3], refs[-3:]
     _, chans, local_times, _ = held.shape
-    here = order.shape[0] // groups
-    rows = 2 * order.shape[0]
+    here = (place.shape[0] - 2) // groups
+    rows = 2 * groups * here
     tiles = list(zip((0, *ends), ends))
 
     def copy(t, f):
@@ -60,10 +60,7 @@
     for t in range(len(tiles)):
         for f in range(chans):
             copy(t, f).start()
-    order_copy = pltpu.make_async_copy(order, order_held, order_sem)
-    order_copy.start()
-    order_copy.wait()
-    table_re, table_im = twiddles(place, order_held, groups, here, local_times)
+    table_re, table_im = twiddles(place, groups, here, local_times)
     each = rows * chans // len(outs)
     for t, (begin, end) in enumerate(tiles):
         cols = pl.ds(begin, end - begin)
@@ -80,22 +77,20 @@
                 out[:, :, pl.ds(begin + lane, LANES)] = part.reshape(*out.shape[:2], LANES).astype(out.dtype)
 
 
-def transform(place, order, visibilities, first, ends, groups):
+def transform(place, visibilities, first, ends, groups):
     _, chans, times, _ = visibilities.shape
-    rows = 2 * order.shape[0]
+    rows = 2 * (place.shape[0] - 2)
     width = ends[-1]
     widest = max(end - begin for begin, end in zip((0, *ends), ends))
     shape = (rows // 8, 2 * chans, width)
     return pl.pallas_call(
         functools.partial(transform_kernel, first, ends, groups),
         out_shape=[jax.ShapeDtypeStruct(shape, F32 if d == 0 else BF16) for d in range(4)],
-        in_specs=[SMEM, HBM, HBM],
+        in_specs=[SMEM, HBM],
         out_specs=[VMEM] * 4,
         scratch_shapes=[
             pltpu.VMEM((2, chans, times, width), BF16),
             pltpu.VMEM((widest // LANES, rows * chans, LANES), F32),
-            pltpu.SMEM(order.shape, jnp.int32),
-            pltpu.SemaphoreType.DMA,
             pltpu.SemaphoreType.DMA((len(ends), chans)),
         ],
         compiler_params=pltpu.CompilerParams(vmem_limit_bytes=30 * MIB),
@@ -105,7 +100,7 @@
             transcendentals=0,
         ),
         name="transform",
-    )(place, order, visibilities)
+    )(place, visibilities)
 
 
 def pair_gains_kernel(gains_ref, pairs_ref, out_ref):
@@ -235,7 +230,7 @@
 
 
 def exchange(parts, shift):
-    return [swap(part, "tm", d << shift) for d, part in enumerate(parts) if d]
+    return [swap(parts[d], "tm", d << shift) for d in range(len(parts) - 1, 0, -1)]
 
 
 def combine(parts, received, left):
@@ -249,10 +244,11 @@
     groups = lax.axis_size("tm")
     count = visibilities.shape[3]
     place = jnp.stack([lax.axis_index("tm"), lax.axis_index("freq")]).astype(jnp.int32)
+    place = jnp.concatenate([place, m_order])
     firsts, sent, arrived = [0], [], []
     for tiles in PARTS:
         ends = tuple(count // SHARES * sum(tiles[: t + 1]) for t in range(len(tiles)))
-        parts = transform(place, m_order, visibilities, firsts[-1], ends, groups)
+        parts = transform(place, visibilities, firsts[-1], ends, groups)
         if arrived:
             parts, arrived[-1][:1] = lax.optimization_barrier((parts, arrived[-1][:1]))
         sent.append(parts)

time: 40.1 us -> 39.5 us (0.985)
  starting transfers between devices: 15.9 us -> 15 us
  other arithmetic: 0.76 us -> 1.42 us
  local copies, waits for them, and re-layouts: 0.72 us -> 0.07 us
    ppermute x11, starting transfers between devices: 15.9 us -> 15 us  [swap(): lax.ppermute(x, axis, [(i, i ^ mask) for i in range(lax.axis_size(axis))])]
    concatenate x0 -> x1, other arithmetic: none -> 0.73 us  [on_device(): place = jnp.concatenate([place, m_order])]
    unnamed x12 -> x10, local copies, waits for them, and re-layouts: 0.68 us -> 0.02 us
  transfers between devices with their start and end apart: 11 -> 11, of which waited for: 4 -> 3; matrix products, arithmetic and copies ran while one was open for 0% -> 0% of each run, Pallas kernels for 21% -> 22%
where the time goes in v4:
time: 39.5 us; the launch traced here: 39.4 us
  Pallas kernels  18.7 us (47%)
  starting transfers between devices  15 us (38%)
  waiting for transfers between devices  4.1 us (10%)
  other arithmetic  1.42 us (4%)
    ppermute x11, starting transfers between devices, swap(): lax.ppermute(x, axis, [(i, i ^ mask) for i in range(lax.axis_size(axis))])  15 us
    pallas_call x2, Pallas kernels, transform(): pl.pallas_call(functools.partial(transform_kernel, first, ends, groups),...  14.1 us
    ppermute x11, waiting for transfers between devices, swap(): lax.ppermute(x, axis, [(i, i ^ mask) for i in range(lax.axis_size(axis))])  4.1 us
    pallas_call x1, Pallas kernels, pair_gains(): pl.pallas_call(pair_gains_kernel, out_shape=jax.ShapeDtypeStruct((2 * cha...  1.59 us
    pallas_call x1, Pallas kernels, project(): pl.pallas_call(functools.partial(project_kernel, first, len(recvs)), out_...  1.59 us
    pallas_call x1, Pallas kernels, finish(): pl.pallas_call(functools.partial(finish_kernel, first, len(recvs), len(te...  1.47 us
  transfers between devices with their start and end apart: 11, of which 3 were waited for; matrix products, arithmetic and copies ran while one was open for 0% of the time, Pallas kernels for 22%

profile of v4, /device:TPU:0, one launch (start us, length us, event | category | flops | bytes accessed | tf_op | source)
XLA Modules:
  0.0 39.4 jit_solution(2448464977124081350)
XLA Ops:
  0.0 0.7 %pad_add_fusion.place = s32[10]{0:T(128)S(1)} fusion(s32[8]{0:T(128)} %param.9, s32[1]{0:T(128)} %bitcast.1, s32[1]{0:T(128)} %bitcast), kind=kLoop, calls=%fused_computation.9 | loop fusion | flops 20 | bytes 80 | tf_op jit(solution)/shard_map/concatenate | solution.py:247
  0.7 8.7 %transform.3 = (f32[2,16,2816]{2,1,0:T(8,128)S(1)}, bf16[2,16,2816]{2,1,0:T(8,128)(2,1)S(1)}, bf16[2,16,2816]{2,1,0:T(8,128)(2,1)S(1)}, bf16[2,16,2816]{2,1,0:T(8,128)(2,1)S(1)}) custom-call(s32[10]{0:T(128)S(1)} %pad_add_fusion.place, bf16[2,8,256,4096]{3,2,1,0:T(8,128)(2,1)} %vis_ref.3), custom_call_target="tpu_custom_call" | custom-call | flops 11811160064 | bytes 23068672 | tf_op jit(solution)/shard_map/transform/pallas_call | solution.py:86
  9.4 0.0 slice-start
  9.5 0.0 copy-start
  9.5 4.0 %collective-permute-start = (bf16[2,16,2816]{2,1,0:T(8,128)(2,1)S(1)}, bf16[2,16,2816]{2,1,0:T(8,128)(2,1)S(1)}, u32[]{:S(2)}, u32[]{:S(2)}) collective-permute-start(bf16[2,16,2816]{2,1,0:T(8,128)(2,1)S(1)} %get-tuple-element.32), channel_id=1, source_target_pairs={{0,12},{4,8},{8,4},{12,0},{16,28},{20,24},{24,20},{28,16},{1,13},{... | collective-permute-start | bytes 540680 | tf_op jit(solution)/shard_map/ppermute | solution.py:229
  13.5 0.4 %collective-permute-start.4 = (bf16[2,16,2816]{2,1,0:T(8,128)(2,1)S(1)}, bf16[2,16,2816]{2,1,0:T(8,128)(2,1)S(1)}, u32[]{:S(2)}, u32[]{:S(2)}) collective-permute-start(bf16[2,16,2816]{2,1,0:T(8,128)(2,1)S(1)} %get-tuple-element.39), channel_id=1, source_target_pairs={{0,8},{4,12},{8,0},{12,4},{16,24},{20,28},{24,16},{28,20},{1,9},{5... | collective-permute-start | bytes 540680 | tf_op jit(solution)/shard_map/ppermute | solution.py:229
  13.9 0.2 collective-permute-start.5
  14.1 5.3 %transform.2 = (f32[2,16,1280]{2,1,0:T(8,128)S(1)}, bf16[2,16,1280]{2,1,0:T(8,128)(2,1)S(1)}, bf16[2,16,1280]{2,1,0:T(8,128)(2,1)S(1)}, bf16[2,16,1280]{2,1,0:T(8,128)(2,1)S(1)}) custom-call(s32[10]{0:T(128)S(1)} %pad_add_fusion.place, bf16[2,8,256,4096]{3,2,1,0:T(8,128)(2,1)} %vis_ref.3), custom_call_target="tpu_custom_call" | custom-call | flops 5368709120 | bytes 10485760 | tf_op jit(solution)/shard_map/transform/pallas_call | solution.py:86
  19.5 2.6 %collective-permute-start.1 = (bf16[2,16,1280]{2,1,0:T(8,128)(2,1)S(1)}, bf16[2,16,1280]{2,1,0:T(8,128)(2,1)S(1)}, u32[]{:S(2)}, u32[]{:S(2)}) collective-permute-start(bf16[2,16,1280]{2,1,0:T(8,128)(2,1)S(1)} %get-tuple-element.34), channel_id=1, source_target_pairs={{0,12},{4,8},{8,4},{12,0},{16,28},{20,24},{24,20},{28,16},{1,13},{... | collective-permute-start | bytes 245768 | tf_op jit(solution)/shard_map/ppermute | solution.py:229
  22.1 0.4 %collective-permute-start.2 = (bf16[2,16,1280]{2,1,0:T(8,128)(2,1)S(1)}, bf16[2,16,1280]{2,1,0:T(8,128)(2,1)S(1)}, u32[]{:S(2)}, u32[]{:S(2)}) collective-permute-start(bf16[2,16,1280]{2,1,0:T(8,128)(2,1)S(1)} %get-tuple-element.35), channel_id=1, source_target_pairs={{0,8},{4,12},{8,0},{12,4},{16,24},{20,28},{24,16},{28,20},{1,9},{5... | collective-permute-start | bytes 245768 | tf_op jit(solution)/shard_map/ppermute | solution.py:229
  22.5 0.5 %collective-permute-start.3 = (bf16[2,16,1280]{2,1,0:T(8,128)(2,1)S(1)}, bf16[2,16,1280]{2,1,0:T(8,128)(2,1)S(1)}, u32[]{:S(2)}, u32[]{:S(2)}) collective-permute-start(bf16[2,16,1280]{2,1,0:T(8,128)(2,1)S(1)} %get-tuple-element.36), channel_id=1, source_target_pairs={{0,4},{4,0},{8,12},{12,8},{16,20},{20,16},{24,28},{28,24},{1,5},{5... | collective-permute-start | bytes 245768 | tf_op jit(solution)/shard_map/ppermute | solution.py:229
  23.1 0.1 add_bitcast_fusion
  23.2 2.8 %collective-permute-start.7 = (bf16[1,16,2816]{2,1,0:T(8,128)(2,1)S(1)}, bf16[1,16,2816]{2,1,0:T(8,128)(2,1)S(1)}, u32[]{:S(2)}, u32[]{:S(2)}) collective-permute-start(bf16[1,16,2816]{2,1,0:T(8,128)(2,1)S(1)} %fusion), channel_id=1, source_target_pairs={{0,16},{4,20},{8,24},{12,28},{16,0},{20,4},{24,8},{28,12},{1,17},{... | collective-permute-start | bytes 270344 | tf_op jit(solution)/shard_map/ppermute | solution.py:229
  26.0 1.6 %pair_gains.1.refs_2_ = f32[16,4096]{1,0:T(8,128)S(1)} custom-call(f32[2,8,1024]{2,1,0:T(8,128)S(1)} %copy-done.1, s32[2,4096]{1,0:T(2,128)S(1)} %bitcast.31), custom_call_target="tpu_custom_call" | custom-call | flops 4194304 | bytes 4194304 | tf_op jit(solution)/shard_map/pair_gains/pallas_call | solution.py:134
  27.7 2.0 %collective-permute-start.6 = (bf16[1,16,1280]{2,1,0:T(8,128)(2,1)S(1)}, bf16[1,16,1280]{2,1,0:T(8,128)(2,1)S(1)}, u32[]{:S(2)}, u32[]{:S(2)}) collective-permute-start(bf16[1,16,1280]{2,1,0:T(8,128)(2,1)S(1)} %fusion.1), channel_id=1, source_target_pairs={{0,16},{4,20},{8,24},{12,28},{16,0},{20,4},{24,8},{28,12},{1,17},{... | collective-permute-start | bytes 122888 | tf_op jit(solution)/shard_map/ppermute | solution.py:229
  29.7 1.6 %project.1.refs_5_ = f32[4,16,128]{2,1,0:T(8,128)S(1)} custom-call(f32[16,2816]{1,0:T(8,128)S(1)} %bitcast.27, bf16[16,2816]{1,0:T(8,128)(2,1)S(1)} %bitcast.29, f32[16,4096]{1,0:T(8,128)S(1)} %pair_gains.1.refs_2_, bf16[2,8,64,4096]{3,2,1,0:T(8,128)(2,1)S(1)} %bitcast.25), custom_call_target="tpu_custom_call" | custom-call | flops 738197504 | bytes 5767168 | tf_op jit(solution)/shard_map/project/pallas_call | solution.py:176
  31.3 1.4 %collective-permute-done.6 = bf16[1,16,1280]{2,1,0:T(8,128)(2,1)S(1)} collective-permute-done((bf16[1,16,1280]{2,1,0:T(8,128)(2,1)S(1)}, bf16[1,16,1280]{2,1,0:T(8,128)(2,1)S(1)}, u32[]{:S(2)}, u32[]{:S(2)}) %collective-permute-start.6) | collective-permute-done | bytes 40992 | tf_op jit(solution)/shard_map/ppermute | solution.py:229
  32.7 1.5 %finish.1 = (f32[2,128]{1,0:T(2,128)S(1)}, f32[2,128]{1,0:T(2,128)S(1)}, f32[2,128]{1,0:T(2,128)S(1)}, f32[2,128]{1,0:T(2,128)S(1)}) custom-call(s32[10]{0:T(128)S(1)} %pad_add_fusion.place, f32[16,1280]{1,0:T(8,128)S(1)} %slice_bitcast_fusion.1.refs_0_, bf16[16,1280]{1,0:T(8,128)(2,1)S(1)} %bitcast.30, f32[16,4096]{1,0:T(8,128)S(1)} %pair_gains.1.refs_2_, ...), custom_call_target="tpu_custom_call" | custom-call | tf_op jit(solution)/shard_map/finish/pallas_call | solution.py:218
  34.2 0.1 collective-permute-start.8
  34.2 1.6 %collective-permute-start.9 = (f32[2,128]{1,0:T(2,128)S(1)}, f32[2,128]{1,0:T(2,128)S(1)}, u32[]{:S(2)}, u32[]{:S(2)}) collective-permute-start(f32[2,128]{1,0:T(2,128)S(1)} %get-tuple-element.49), channel_id=1, source_target_pairs={{0,2},{1,3},{2,0},{3,1},{4,6},{5,7},{6,4},{7,5},{8,10},{9,11},{10,... | collective-permute-start | bytes 3080 | tf_op jit(solution)/shard_map/ppermute | solution.py:229
  35.8 0.3 collective-permute-start.10
  36.1 1.8 %collective-permute-done.9 = f32[2,128]{1,0:T(2,128)S(1)} collective-permute-done((f32[2,128]{1,0:T(2,128)S(1)}, f32[2,128]{1,0:T(2,128)S(1)}, u32[]{:S(2)}, u32[]{:S(2)}) %collective-permute-start.9) | collective-permute-done | bytes 1056 | tf_op jit(solution)/shard_map/ppermute | solution.py:229
  37.9 0.9 %collective-permute-done.10 = f32[2,128]{1,0:T(2,128)S(1)} collective-permute-done((f32[2,128]{1,0:T(2,128)S(1)}, f32[2,128]{1,0:T(2,128)S(1)}, u32[]{:S(2)}, u32[]{:S(2)}) %collective-permute-start.10) | collective-permute-done | bytes 1056 | tf_op jit(solution)/shard_map/ppermute | solution.py:229
  38.8 0.6 %add_add_fusion = f32[2,128]{1,0:T(2,128)} fusion(f32[2,128]{1,0:T(2,128)S(1)} %collective-permute-done.10, f32[2,128]{1,0:T(2,128)S(1)} %collective-permute-done.9, f32[2,128]{1,0:T(2,128)S(1)} %get-tuple-element.47, f32[2,128]{1,0:T(2,128)S(1)} %collective-permute-done.8), kind=kLoop, calls=%fused_computation.8 | loop fusion | flops 768 | bytes 5120 | tf_op jit(solution)/shard_map/add | solution.py:275
  (22 shorter events, 0.1 us)
Async XLA Ops:
  0.7 25.3 %copy-start.1 = (f32[2,8,1024]{2,1,0:T(8,128)S(1)}, f32[2,8,1024]{2,1,0:T(8,128)}, u32[]{:S(2)}) copy-start(f32[2,8,1024]{2,1,0:T(8,128)} %gains_ref) | copy-start | bytes 196612
  0.7 25.3 %copy-start.2 = (s32[4096,2]{0,1:T(2,128)S(1)}, s32[4096,2]{0,1:T(2,128)}, u32[]{:S(2)}) copy-start(s32[4096,2]{0,1:T(2,128)} %param.8) | copy-start | bytes 98308
  9.4 20.3 %slice-start = ((s8[8388608]{0:T(1024)(128)(4,1)}), s8[4194304]{0:T(1024)(128)(4,1)S(1)}, s32[]{:S(2)}) async-start(s8[8388608]{0:T(1024)(128)(4,1)} %bitcast.23), calls=%async_computation | async-start | bytes 8388608
  9.5 23.2 %copy-start = (bf16[1,8,64,512]{3,2,1,0:T(8,128)(2,1)S(1)}, bf16[1,8,64,512]{3,2,1,0:T(8,128)(2,1)}, u32[]{:S(2)}) copy-start(bf16[1,8,64,512]{3,2,1,0:T(8,128)(2,1)} %param.11) | copy-start | bytes 1572868
  9.5 10.0 %collective-permute-start = (bf16[2,16,2816]{2,1,0:T(8,128)(2,1)S(1)}, bf16[2,16,2816]{2,1,0:T(8,128)(2,1)S(1)}, u32[]{:S(2)}, u32[]{:S(2)}) collective-permute-start(bf16[2,16,2816]{2,1,0:T(8,128)(2,1)S(1)} %get-tuple-element.32), channel_id=1, source_target_pairs={{0,12},{4,8},{8,4},{12,0},{16,28},{20,24},{24,20},{28,16},{1,13},{... | collective-permute-start | bytes 540680 | tf_op jit(solution)/shard_map/ppermute | solution.py:229
  13.5 9.6 %collective-permute-start.4 = (bf16[2,16,2816]{2,1,0:T(8,128)(2,1)S(1)}, bf16[2,16,2816]{2,1,0:T(8,128)(2,1)S(1)}, u32[]{:S(2)}, u32[]{:S(2)}) collective-permute-start(bf16[2,16,2816]{2,1,0:T(8,128)(2,1)S(1)} %get-tuple-element.39), channel_id=1, source_target_pairs={{0,8},{4,12},{8,0},{12,4},{16,24},{20,28},{24,16},{28,20},{1,9},{5... | collective-permute-start | bytes 540680 | tf_op jit(solution)/shard_map/ppermute | solution.py:229
  13.9 15.8 %slice-start.1 = ((s8[8388608]{0:T(1024)(128)(4,1)}), s8[4194304]{0:T(1024)(128)(4,1)S(1)}, s32[]{:S(2)}) async-start(s8[8388608]{0:T(1024)(128)(4,1)} %bitcast.23), calls=%async_computation.1 | async-start | bytes 8388608
  13.9 9.1 %collective-permute-start.5 = (bf16[2,16,2816]{2,1,0:T(8,128)(2,1)S(1)}, bf16[2,16,2816]{2,1,0:T(8,128)(2,1)S(1)}, u32[]{:S(2)}, u32[]{:S(2)}) collective-permute-start(bf16[2,16,2816]{2,1,0:T(8,128)(2,1)S(1)} %get-tuple-element.40), channel_id=1, source_target_pairs={{0,4},{4,0},{8,12},{12,8},{16,20},{20,16},{24,28},{28,24},{1,5},{5... | collective-permute-start | bytes 540680 | tf_op jit(solution)/shard_map/ppermute | solution.py:229
  19.5 8.1 %collective-permute-start.1 = (bf16[2,16,1280]{2,1,0:T(8,128)(2,1)S(1)}, bf16[2,16,1280]{2,1,0:T(8,128)(2,1)S(1)}, u32[]{:S(2)}, u32[]{:S(2)}) collective-permute-start(bf16[2,16,1280]{2,1,0:T(8,128)(2,1)S(1)} %get-tuple-element.34), channel_id=1, source_target_pairs={{0,12},{4,8},{8,4},{12,0},{16,28},{20,24},{24,20},{28,16},{1,13},{... | collective-permute-start | bytes 245768 | tf_op jit(solution)/shard_map/ppermute | solution.py:229
  22.1 5.5 %collective-permute-start.2 = (bf16[2,16,1280]{2,1,0:T(8,128)(2,1)S(1)}, bf16[2,16,1280]{2,1,0:T(8,128)(2,1)S(1)}, u32[]{:S(2)}, u32[]{:S(2)}) collective-permute-start(bf16[2,16,1280]{2,1,0:T(8,128)(2,1)S(1)} %get-tuple-element.35), channel_id=1, source_target_pairs={{0,8},{4,12},{8,0},{12,4},{16,24},{20,28},{24,16},{28,20},{1,9},{5... | collective-permute-start | bytes 245768 | tf_op jit(solution)/shard_map/ppermute | solution.py:229
  22.5 5.1 %collective-permute-start.3 = (bf16[2,16,1280]{2,1,0:T(8,128)(2,1)S(1)}, bf16[2,16,1280]{2,1,0:T(8,128)(2,1)S(1)}, u32[]{:S(2)}, u32[]{:S(2)}) collective-permute-start(bf16[2,16,1280]{2,1,0:T(8,128)(2,1)S(1)} %get-tuple-element.36), channel_id=1, source_target_pairs={{0,4},{4,0},{8,12},{12,8},{16,20},{20,16},{24,28},{28,24},{1,5},{5... | collective-permute-start | bytes 245768 | tf_op jit(solution)/shard_map/ppermute | solution.py:229
  23.2 6.5 %collective-permute-start.7 = (bf16[1,16,2816]{2,1,0:T(8,128)(2,1)S(1)}, bf16[1,16,2816]{2,1,0:T(8,128)(2,1)S(1)}, u32[]{:S(2)}, u32[]{:S(2)}) collective-permute-start(bf16[1,16,2816]{2,1,0:T(8,128)(2,1)S(1)} %fusion), channel_id=1, source_target_pairs={{0,16},{4,20},{8,24},{12,28},{16,0},{20,4},{24,8},{28,12},{1,17},{... | collective-permute-start | bytes 270344 | tf_op jit(solution)/shard_map/ppermute | solution.py:229
  27.7 5.0 %collective-permute-start.6 = (bf16[1,16,1280]{2,1,0:T(8,128)(2,1)S(1)}, bf16[1,16,1280]{2,1,0:T(8,128)(2,1)S(1)}, u32[]{:S(2)}, u32[]{:S(2)}) collective-permute-start(bf16[1,16,1280]{2,1,0:T(8,128)(2,1)S(1)} %fusion.1), channel_id=1, source_target_pairs={{0,16},{4,20},{8,24},{12,28},{16,0},{20,4},{24,8},{28,12},{1,17},{... | collective-permute-start | bytes 122888 | tf_op jit(solution)/shard_map/ppermute | solution.py:229
  34.2 1.9 %collective-permute-start.8 = (f32[2,128]{1,0:T(2,128)S(1)}, f32[2,128]{1,0:T(2,128)S(1)}, u32[]{:S(2)}, u32[]{:S(2)}) collective-permute-start(f32[2,128]{1,0:T(2,128)S(1)} %get-tuple-element.48), channel_id=1, source_target_pairs={{0,1},{1,0},{2,3},{3,2},{4,5},{5,4},{6,7},{7,6},{8,9},{9,8},{10,11... | collective-permute-start | bytes 3080 | tf_op jit(solution)/shard_map/ppermute | solution.py:229
  34.2 3.6 %collective-permute-start.9 = (f32[2,128]{1,0:T(2,128)S(1)}, f32[2,128]{1,0:T(2,128)S(1)}, u32[]{:S(2)}, u32[]{:S(2)}) collective-permute-start(f32[2,128]{1,0:T(2,128)S(1)} %get-tuple-element.49), channel_id=1, source_target_pairs={{0,2},{1,3},{2,0},{3,1},{4,6},{5,7},{6,4},{7,5},{8,10},{9,11},{10,... | collective-permute-start | bytes 3080 | tf_op jit(solution)/shard_map/ppermute | solution.py:229
  35.8 3.0 %collective-permute-start.10 = (f32[2,128]{1,0:T(2,128)S(1)}, f32[2,128]{1,0:T(2,128)S(1)}, u32[]{:S(2)}, u32[]{:S(2)}) collective-permute-start(f32[2,128]{1,0:T(2,128)S(1)} %get-tuple-element.50), channel_id=1, source_target_pairs={{0,3},{1,2},{2,1},{3,0},{4,7},{5,6},{6,5},{7,4},{8,11},{9,10},{10,... | collective-permute-start | bytes 3080 | tf_op jit(solution)/shard_map/ppermute | solution.py:229

commit v5 on v3

--- a/solution.py
+++ b/solution.py
@@ -8,13 +8,12 @@
 from jax.sharding import PartitionSpec as P
 
 LANES = 128
-PARTS = ((11,11), (10,))
+PARTS = ((11, 11), (10,))
 SHARES = 32
 MIB = 1 << 20
 F32 = jnp.float32
 BF16 = jnp.bfloat16
 VMEM = pl.BlockSpec(memory_space=pltpu.VMEM)
-SMEM = pl.BlockSpec(memory_space=pltpu.SMEM)
 HBM = pl.BlockSpec(memory_space=pltpu.HBM)
 
 
@@ -42,11 +41,11 @@
     return jnp.where(real, cosine, -sine).astype(BF16), jnp.where(real, sine, cosine).astype(BF16)
 
 
-def transform_kernel(first, ends, groups, place, order, vis_ref, *refs):
-    outs, (held, sums, order_held, order_sem, sems) = refs[:-5], refs[-5:]
+def transform_kernel(first, ends, groups, place_ref, order_ref, vis_ref, *refs):
+    outs, (held, sums, place, order, place_sem, order_sem, sems) = refs[:-7], refs[-7:]
     _, chans, local_times, _ = held.shape
     here = order.shape[0] // groups
-    rows = 2 * order.shape[0]
+    rows = 2 * groups * here
     tiles = list(zip((0, *ends), ends))
 
     def copy(t, f):
@@ -57,13 +56,16 @@
             sems.at[t, f],
         )
 
+    place_copy = pltpu.make_async_copy(place_ref, place, place_sem)
+    place_copy.start()
+    order_copy = pltpu.make_async_copy(order_ref, order, order_sem)
+    order_copy.start()
     for t in range(len(tiles)):
         for f in range(chans):
             copy(t, f).start()
-    order_copy = pltpu.make_async_copy(order, order_held, order_sem)
-    order_copy.start()
+    place_copy.wait()
     order_copy.wait()
-    table_re, table_im = twiddles(place, order_held, groups, here, local_times)
+    table_re, table_im = twiddles(place, order, groups, here, local_times)
     each = rows * chans // len(outs)
     for t, (begin, end) in enumerate(tiles):
         cols = pl.ds(begin, end - begin)
@@ -89,12 +91,14 @@
     return pl.pallas_call(
         functools.partial(transform_kernel, first, ends, groups),
         out_shape=[jax.ShapeDtypeStruct(shape, F32 if d == 0 else BF16) for d in range(4)],
-        in_specs=[SMEM, HBM, HBM],
+        in_specs=[HBM, HBM, HBM],
         out_specs=[VMEM] * 4,
         scratch_shapes=[
             pltpu.VMEM((2, chans, times, width), BF16),
             pltpu.VMEM((widest // LANES, rows * chans, LANES), F32),
+            pltpu.SMEM(place.shape, jnp.int32),
             pltpu.SMEM(order.shape, jnp.int32),
+            pltpu.SemaphoreType.DMA,
             pltpu.SemaphoreType.DMA,
             pltpu.SemaphoreType.DMA((len(ends), chans)),
         ],
@@ -191,7 +195,10 @@
     )(keep, *recvs, gains, beams)
 
 
-def finish_kernel(first, n_recv, n_tel, place, *refs):
+def finish_kernel(first, n_recv, n_tel, place_ref, *refs):
+    refs, place, place_sem = refs[:-2], refs[-2], refs[-1]
+    place_copy = pltpu.make_async_copy(place_ref, place, place_sem)
+    place_copy.start()
     keep, recvs = refs[0], refs[1 : 1 + n_recv]
     gains, beams, basis = refs[1 + n_recv : 4 + n_recv]
     tels, outs = refs[4 + n_recv : 4 + n_recv + n_tel], refs[4 + n_recv + n_tel :]
@@ -208,6 +215,7 @@
     both = jnp.concatenate(
         [jnp.sum(total[:chans], axis=0, keepdims=True), jnp.sum(total[chans:], axis=0, keepdims=True)]
     )
+    place_copy.wait()
     me = place[1]
     width = outs[0].shape[1]
     for apart, out in enumerate(outs):
@@ -223,8 +231,9 @@
     return pl.pallas_call(
         functools.partial(finish_kernel, first, len(recvs), len(tels)),
         out_shape=[shape] * blocks,
-        in_specs=[SMEM] + [VMEM] * (4 + len(recvs) + len(tels)),
+        in_specs=[HBM] + [VMEM] * (4 + len(recvs) + len(tels)),
         out_specs=[VMEM] * blocks,
+        scratch_shapes=[pltpu.SMEM(place.shape, jnp.int32), pltpu.SemaphoreType.DMA],
         compiler_params=pltpu.CompilerParams(vmem_limit_bytes=8 * MIB),
         name="finish",
     )(place, keep, *recvs, gains, beams, basis, *tels)
@@ -235,7 +244,7 @@
 
 
 def exchange(parts, shift):
-    return [swap(part, "tm", d << shift) for d, part in enumerate(parts) if d]
+    return [swap(parts[d], "tm", d << shift) for d in range(len(parts) - 1, 0, -1)]
 
 
 def combine(parts, received, left):
@@ -249,10 +258,11 @@
     groups = lax.axis_size("tm")
     count = visibilities.shape[3]
     place = jnp.stack([lax.axis_index("tm"), lax.axis_index("freq")]).astype(jnp.int32)
+    order = pltpu.with_memory_space_constraint(m_order, pltpu.HBM)
     firsts, sent, arrived = [0], [], []
     for tiles in PARTS:
         ends = tuple(count // SHARES * sum(tiles[: t + 1]) for t in range(len(tiles)))
-        parts = transform(place, m_order, visibilities, firsts[-1], ends, groups)
+        parts = transform(place, order, visibilities, firsts[-1], ends, groups)
         if arrived:
             parts, arrived[-1][:1] = lax.optimization_barrier((parts, arrived[-1][:1]))
         sent.append(parts)

time: 40.1 us -> 37.5 us (0.935)
  Pallas kernels: 18.6 us -> 17 us
  starting transfers between devices: 15.9 us -> 15.2 us
  local copies, waits for them, and re-layouts: 0.72 us -> 0.07 us
  waiting for transfers between devices: 3.73 us -> 4.31 us
    pallas_call x2, Pallas kernels: 14 us -> 12.8 us  [transform(): pl.pallas_call(functools.partial(transform_kernel, first, ends, groups),...]
    ppermute x11, starting transfers between devices: 15.9 us -> 15.2 us  [swap(): lax.ppermute(x, axis, [(i, i ^ mask) for i in range(lax.axis_size(axis))])]
    unnamed x12 -> x10, local copies, waits for them, and re-layouts: 0.68 us -> 0.02 us
    ppermute x11, waiting for transfers between devices: 3.73 us -> 4.31 us  [swap(): lax.ppermute(x, axis, [(i, i ^ mask) for i in range(lax.axis_size(axis))])]
    pallas_call x1, Pallas kernels: 1.48 us -> 0.97 us  [finish(): pl.pallas_call(functools.partial(finish_kernel, first, len(recvs), len(te...]
  transfers between devices with their start and end apart: 11 -> 11, of which waited for: 4 -> 6; matrix products, arithmetic and copies ran while one was open for 0% -> 0% of each run, Pallas kernels for 21% -> 21%
where the time goes in v5:
time: 37.5 us; the launch traced here: 37.4 us
  Pallas kernels  17 us (45%)
  starting transfers between devices  15.2 us (41%)
  waiting for transfers between devices  4.31 us (11%)
  other arithmetic  0.76 us (2%)
    ppermute x11, starting transfers between devices, swap(): lax.ppermute(x, axis, [(i, i ^ mask) for i in range(lax.axis_size(axis))])  15.2 us
    pallas_call x2, Pallas kernels, transform(): pl.pallas_call(functools.partial(transform_kernel, first, ends, groups),...  12.8 us
    ppermute x11, waiting for transfers between devices, swap(): lax.ppermute(x, axis, [(i, i ^ mask) for i in range(lax.axis_size(axis))])  4.31 us
    pallas_call x1, Pallas kernels, pair_gains(): pl.pallas_call(pair_gains_kernel, out_shape=jax.ShapeDtypeStruct((2 * cha...  1.59 us
    pallas_call x1, Pallas kernels, project(): pl.pallas_call(functools.partial(project_kernel, first, len(recvs)), out_...  1.59 us
    pallas_call x1, Pallas kernels, finish(): pl.pallas_call(functools.partial(finish_kernel, first, len(recvs), len(te...  0.97 us
  transfers between devices with their start and end apart: 11, of which 6 were waited for; matrix products, arithmetic and copies ran while one was open for 0% of the time, Pallas kernels for 21%

profile of v5, /device:TPU:0, one launch (start us, length us, event | category | flops | bytes accessed | tf_op | source)
XLA Modules:
  0.0 37.4 jit_solution(14964767637471465775)
XLA Ops:
  0.0 0.1 pad_add_fusion.place_ref
  0.1 8.2 %transform.3 = (f32[2,16,2816]{2,1,0:T(8,128)S(1)}, bf16[2,16,2816]{2,1,0:T(8,128)(2,1)S(1)}, bf16[2,16,2816]{2,1,0:T(8,128)(2,1)S(1)}, bf16[2,16,2816]{2,1,0:T(8,128)(2,1)S(1)}) custom-call(s32[2]{0:T(128)S(1)} %pad_add_fusion.place_ref, s32[8]{0:T(128)} %order_ref.3, bf16[2,8,256,4096]{3,2,1,0:T(8,128)(2,1)} %vis_ref.3), custom_call_target="tpu_custom_call" | custom-call | flops 11811160064 | bytes 23068672 | tf_op jit(solution)/shard_map/transform/pallas_call | solution.py:91
  8.3 4.0 %collective-permute-start = (bf16[2,16,2816]{2,1,0:T(8,128)(2,1)S(1)}, bf16[2,16,2816]{2,1,0:T(8,128)(2,1)S(1)}, u32[]{:S(2)}, u32[]{:S(2)}) collective-permute-start(bf16[2,16,2816]{2,1,0:T(8,128)(2,1)S(1)} %get-tuple-element.32), channel_id=1, source_target_pairs={{0,12},{4,8},{8,4},{12,0},{16,28},{20,24},{24,20},{28,16},{1,13},{... | collective-permute-start | bytes 540680 | tf_op jit(solution)/shard_map/ppermute | solution.py:243
  12.3 0.4 %collective-permute-start.4 = (bf16[2,16,2816]{2,1,0:T(8,128)(2,1)S(1)}, bf16[2,16,2816]{2,1,0:T(8,128)(2,1)S(1)}, u32[]{:S(2)}, u32[]{:S(2)}) collective-permute-start(bf16[2,16,2816]{2,1,0:T(8,128)(2,1)S(1)} %get-tuple-element.39), channel_id=1, source_target_pairs={{0,8},{4,12},{8,0},{12,4},{16,24},{20,28},{24,16},{28,20},{1,9},{5... | collective-permute-start | bytes 540680 | tf_op jit(solution)/shard_map/ppermute | solution.py:243
  12.8 0.2 collective-permute-start.5
  13.0 4.6 %transform.2 = (f32[2,16,1280]{2,1,0:T(8,128)S(1)}, bf16[2,16,1280]{2,1,0:T(8,128)(2,1)S(1)}, bf16[2,16,1280]{2,1,0:T(8,128)(2,1)S(1)}, bf16[2,16,1280]{2,1,0:T(8,128)(2,1)S(1)}) custom-call(s32[2]{0:T(128)S(1)} %pad_add_fusion.place_ref, s32[8]{0:T(128)} %order_ref.3, bf16[2,8,256,4096]{3,2,1,0:T(8,128)(2,1)} %vis_ref.3), custom_call_target="tpu_custom_call" | custom-call | flops 5368709120 | bytes 10485760 | tf_op jit(solution)/shard_map/transform/pallas_call | solution.py:91
  17.6 0.1 collective-permute-done
  17.7 3.0 %collective-permute-start.1 = (bf16[2,16,1280]{2,1,0:T(8,128)(2,1)S(1)}, bf16[2,16,1280]{2,1,0:T(8,128)(2,1)S(1)}, u32[]{:S(2)}, u32[]{:S(2)}) collective-permute-start(bf16[2,16,1280]{2,1,0:T(8,128)(2,1)S(1)} %get-tuple-element.34), channel_id=1, source_target_pairs={{0,12},{4,8},{8,4},{12,0},{16,28},{20,24},{24,20},{28,16},{1,13},{... | collective-permute-start | bytes 245768 | tf_op jit(solution)/shard_map/ppermute | solution.py:243
  20.7 0.4 %collective-permute-start.2 = (bf16[2,16,1280]{2,1,0:T(8,128)(2,1)S(1)}, bf16[2,16,1280]{2,1,0:T(8,128)(2,1)S(1)}, u32[]{:S(2)}, u32[]{:S(2)}) collective-permute-start(bf16[2,16,1280]{2,1,0:T(8,128)(2,1)S(1)} %get-tuple-element.35), channel_id=1, source_target_pairs={{0,8},{4,12},{8,0},{12,4},{16,24},{20,28},{24,16},{28,20},{1,9},{5... | collective-permute-start | bytes 245768 | tf_op jit(solution)/shard_map/ppermute | solution.py:243
  21.2 0.1 collective-permute-start.3
  21.3 0.2 collective-permute-done.4
  21.5 0.1 add_bitcast_fusion
  21.6 2.9 %collective-permute-start.7 = (bf16[1,16,2816]{2,1,0:T(8,128)(2,1)S(1)}, bf16[1,16,2816]{2,1,0:T(8,128)(2,1)S(1)}, u32[]{:S(2)}, u32[]{:S(2)}) collective-permute-start(bf16[1,16,2816]{2,1,0:T(8,128)(2,1)S(1)} %fusion), channel_id=1, source_target_pairs={{0,16},{4,20},{8,24},{12,28},{16,0},{20,4},{24,8},{28,12},{1,17},{... | collective-permute-start | bytes 270344 | tf_op jit(solution)/shard_map/ppermute | solution.py:243
  24.4 1.6 %pair_gains.1.refs_2_ = f32[16,4096]{1,0:T(8,128)S(1)} custom-call(f32[2,8,1024]{2,1,0:T(8,128)S(1)} %copy-done.1, s32[2,4096]{1,0:T(2,128)S(1)} %bitcast.31), custom_call_target="tpu_custom_call" | custom-call | flops 4194304 | bytes 4194304 | tf_op jit(solution)/shard_map/pair_gains/pallas_call | solution.py:143
  26.0 0.1 collective-permute-done.2
  26.2 2.1 %collective-permute-start.6 = (bf16[1,16,1280]{2,1,0:T(8,128)(2,1)S(1)}, bf16[1,16,1280]{2,1,0:T(8,128)(2,1)S(1)}, u32[]{:S(2)}, u32[]{:S(2)}) collective-permute-start(bf16[1,16,1280]{2,1,0:T(8,128)(2,1)S(1)} %fusion.1), channel_id=1, source_target_pairs={{0,16},{4,20},{8,24},{12,28},{16,0},{20,4},{24,8},{28,12},{1,17},{... | collective-permute-start | bytes 122888 | tf_op jit(solution)/shard_map/ppermute | solution.py:243
  28.4 1.6 %project.1.refs_5_ = f32[4,16,128]{2,1,0:T(8,128)S(1)} custom-call(f32[16,2816]{1,0:T(8,128)S(1)} %bitcast.27, bf16[16,2816]{1,0:T(8,128)(2,1)S(1)} %bitcast.29, f32[16,4096]{1,0:T(8,128)S(1)} %pair_gains.1.refs_2_, bf16[2,8,64,4096]{3,2,1,0:T(8,128)(2,1)S(1)} %bitcast.25), custom_call_target="tpu_custom_call" | custom-call | flops 738197504 | bytes 5767168 | tf_op jit(solution)/shard_map/project/pallas_call | solution.py:185
  29.9 1.2 %collective-permute-done.6 = bf16[1,16,1280]{2,1,0:T(8,128)(2,1)S(1)} collective-permute-done((bf16[1,16,1280]{2,1,0:T(8,128)(2,1)S(1)}, bf16[1,16,1280]{2,1,0:T(8,128)(2,1)S(1)}, u32[]{:S(2)}, u32[]{:S(2)}) %collective-permute-start.6) | collective-permute-done | bytes 40992 | tf_op jit(solution)/shard_map/ppermute | solution.py:243
  31.2 1.0 %finish.1 = (f32[2,128]{1,0:T(2,128)S(1)}, f32[2,128]{1,0:T(2,128)S(1)}, f32[2,128]{1,0:T(2,128)S(1)}, f32[2,128]{1,0:T(2,128)S(1)}) custom-call(s32[2]{0:T(128)S(1)} %pad_add_fusion.place_ref, f32[16,1280]{1,0:T(8,128)S(1)} %slice_bitcast_fusion.1.refs_0_, bf16[16,1280]{1,0:T(8,128)(2,1)S(1)} %bitcast.30, f32[16,4096]{1,0:T(8,128)S(1)} %pair_gains.1.refs_2_, ...), custom_call_target="tpu_custom_call" | custom-call | tf_op jit(solution)/shard_map/finish/pallas_call | solution.py:231
  32.2 1.6 %collective-permute-start.9 = (f32[2,128]{1,0:T(2,128)S(1)}, f32[2,128]{1,0:T(2,128)S(1)}, u32[]{:S(2)}, u32[]{:S(2)}) collective-permute-start(f32[2,128]{1,0:T(2,128)S(1)} %get-tuple-element.49), channel_id=1, source_target_pairs={{0,2},{1,3},{2,0},{3,1},{4,6},{5,7},{6,4},{7,5},{8,10},{9,11},{10,... | collective-permute-start | bytes 3080 | tf_op jit(solution)/shard_map/ppermute | solution.py:243
  33.8 0.3 collective-permute-start.10
  34.1 1.8 %collective-permute-done.9 = f32[2,128]{1,0:T(2,128)S(1)} collective-permute-done((f32[2,128]{1,0:T(2,128)S(1)}, f32[2,128]{1,0:T(2,128)S(1)}, u32[]{:S(2)}, u32[]{:S(2)}) %collective-permute-start.9) | collective-permute-done | bytes 1056 | tf_op jit(solution)/shard_map/ppermute | solution.py:243
  35.9 0.9 %collective-permute-done.10 = f32[2,128]{1,0:T(2,128)S(1)} collective-permute-done((f32[2,128]{1,0:T(2,128)S(1)}, f32[2,128]{1,0:T(2,128)S(1)}, u32[]{:S(2)}, u32[]{:S(2)}) %collective-permute-start.10) | collective-permute-done | bytes 1056 | tf_op jit(solution)/shard_map/ppermute | solution.py:243
  36.8 0.6 %add_add_fusion = f32[2,128]{1,0:T(2,128)} fusion(f32[2,128]{1,0:T(2,128)S(1)} %collective-permute-done.10, f32[2,128]{1,0:T(2,128)S(1)} %collective-permute-done.9, f32[2,128]{1,0:T(2,128)S(1)} %get-tuple-element.47, f32[2,128]{1,0:T(2,128)S(1)} %collective-permute-done.8), kind=kLoop, calls=%fused_computation.8 | loop fusion | flops 768 | bytes 5120 | tf_op jit(solution)/shard_map/add | solution.py:289
  (22 shorter events, 0.2 us)
Async XLA Ops:
  0.1 24.4 %copy-start.1 = (f32[2,8,1024]{2,1,0:T(8,128)S(1)}, f32[2,8,1024]{2,1,0:T(8,128)}, u32[]{:S(2)}) copy-start(f32[2,8,1024]{2,1,0:T(8,128)} %gains_ref) | copy-start | bytes 196612
  0.1 24.4 %copy-start.2 = (s32[4096,2]{0,1:T(2,128)S(1)}, s32[4096,2]{0,1:T(2,128)}, u32[]{:S(2)}) copy-start(s32[4096,2]{0,1:T(2,128)} %param.8) | copy-start | bytes 98308
  8.3 20.0 %slice-start = ((s8[8388608]{0:T(1024)(128)(4,1)}), s8[4194304]{0:T(1024)(128)(4,1)S(1)}, s32[]{:S(2)}) async-start(s8[8388608]{0:T(1024)(128)(4,1)} %bitcast.23), calls=%async_computation | async-start | bytes 8388608
  8.3 22.9 %copy-start = (bf16[1,8,64,512]{3,2,1,0:T(8,128)(2,1)S(1)}, bf16[1,8,64,512]{3,2,1,0:T(8,128)(2,1)}, u32[]{:S(2)}) copy-start(bf16[1,8,64,512]{3,2,1,0:T(8,128)(2,1)} %param.11) | copy-start | bytes 1572868
  8.3 9.4 %collective-permute-start = (bf16[2,16,2816]{2,1,0:T(8,128)(2,1)S(1)}, bf16[2,16,2816]{2,1,0:T(8,128)(2,1)S(1)}, u32[]{:S(2)}, u32[]{:S(2)}) collective-permute-start(bf16[2,16,2816]{2,1,0:T(8,128)(2,1)S(1)} %get-tuple-element.32), channel_id=1, source_target_pairs={{0,12},{4,8},{8,4},{12,0},{16,28},{20,24},{24,20},{28,16},{1,13},{... | collective-permute-start | bytes 540680 | tf_op jit(solution)/shard_map/ppermute | solution.py:243
  12.3 9.1 %collective-permute-start.4 = (bf16[2,16,2816]{2,1,0:T(8,128)(2,1)S(1)}, bf16[2,16,2816]{2,1,0:T(8,128)(2,1)S(1)}, u32[]{:S(2)}, u32[]{:S(2)}) collective-permute-start(bf16[2,16,2816]{2,1,0:T(8,128)(2,1)S(1)} %get-tuple-element.39), channel_id=1, source_target_pairs={{0,8},{4,12},{8,0},{12,4},{16,24},{20,28},{24,16},{28,20},{1,9},{5... | collective-permute-start | bytes 540680 | tf_op jit(solution)/shard_map/ppermute | solution.py:243
  12.8 15.6 %slice-start.1 = ((s8[8388608]{0:T(1024)(128)(4,1)}), s8[4194304]{0:T(1024)(128)(4,1)S(1)}, s32[]{:S(2)}) async-start(s8[8388608]{0:T(1024)(128)(4,1)} %bitcast.23), calls=%async_computation.1 | async-start | bytes 8388608
  12.8 8.7 %collective-permute-start.5 = (bf16[2,16,2816]{2,1,0:T(8,128)(2,1)S(1)}, bf16[2,16,2816]{2,1,0:T(8,128)(2,1)S(1)}, u32[]{:S(2)}, u32[]{:S(2)}) collective-permute-start(bf16[2,16,2816]{2,1,0:T(8,128)(2,1)S(1)} %get-tuple-element.40), channel_id=1, source_target_pairs={{0,4},{4,0},{8,12},{12,8},{16,20},{20,16},{24,28},{28,24},{1,5},{5... | collective-permute-start | bytes 540680 | tf_op jit(solution)/shard_map/ppermute | solution.py:243
  17.7 8.3 %collective-permute-start.1 = (bf16[2,16,1280]{2,1,0:T(8,128)(2,1)S(1)}, bf16[2,16,1280]{2,1,0:T(8,128)(2,1)S(1)}, u32[]{:S(2)}, u32[]{:S(2)}) collective-permute-start(bf16[2,16,1280]{2,1,0:T(8,128)(2,1)S(1)} %get-tuple-element.34), channel_id=1, source_target_pairs={{0,12},{4,8},{8,4},{12,0},{16,28},{20,24},{24,20},{28,16},{1,13},{... | collective-permute-start | bytes 245768 | tf_op jit(solution)/shard_map/ppermute | solution.py:243
  20.7 5.4 %collective-permute-start.2 = (bf16[2,16,1280]{2,1,0:T(8,128)(2,1)S(1)}, bf16[2,16,1280]{2,1,0:T(8,128)(2,1)S(1)}, u32[]{:S(2)}, u32[]{:S(2)}) collective-permute-start(bf16[2,16,1280]{2,1,0:T(8,128)(2,1)S(1)} %get-tuple-element.35), channel_id=1, source_target_pairs={{0,8},{4,12},{8,0},{12,4},{16,24},{20,28},{24,16},{28,20},{1,9},{5... | collective-permute-start | bytes 245768 | tf_op jit(solution)/shard_map/ppermute | solution.py:243
  21.2 5.0 %collective-permute-start.3 = (bf16[2,16,1280]{2,1,0:T(8,128)(2,1)S(1)}, bf16[2,16,1280]{2,1,0:T(8,128)(2,1)S(1)}, u32[]{:S(2)}, u32[]{:S(2)}) collective-permute-start(bf16[2,16,1280]{2,1,0:T(8,128)(2,1)S(1)} %get-tuple-element.36), channel_id=1, source_target_pairs={{0,4},{4,0},{8,12},{12,8},{16,20},{20,16},{24,28},{28,24},{1,5},{5... | collective-permute-start | bytes 245768 | tf_op jit(solution)/shard_map/ppermute | solution.py:243
  21.6 6.8 %collective-permute-start.7 = (bf16[1,16,2816]{2,1,0:T(8,128)(2,1)S(1)}, bf16[1,16,2816]{2,1,0:T(8,128)(2,1)S(1)}, u32[]{:S(2)}, u32[]{:S(2)}) collective-permute-start(bf16[1,16,2816]{2,1,0:T(8,128)(2,1)S(1)} %fusion), channel_id=1, source_target_pairs={{0,16},{4,20},{8,24},{12,28},{16,0},{20,4},{24,8},{28,12},{1,17},{... | collective-permute-start | bytes 270344 | tf_op jit(solution)/shard_map/ppermute | solution.py:243
  26.2 5.0 %collective-permute-start.6 = (bf16[1,16,1280]{2,1,0:T(8,128)(2,1)S(1)}, bf16[1,16,1280]{2,1,0:T(8,128)(2,1)S(1)}, u32[]{:S(2)}, u32[]{:S(2)}) collective-permute-start(bf16[1,16,1280]{2,1,0:T(8,128)(2,1)S(1)} %fusion.1), channel_id=1, source_target_pairs={{0,16},{4,20},{8,24},{12,28},{16,0},{20,4},{24,8},{28,12},{1,17},{... | collective-permute-start | bytes 122888 | tf_op jit(solution)/shard_map/ppermute | solution.py:243
  32.1 1.9 %collective-permute-start.8 = (f32[2,128]{1,0:T(2,128)S(1)}, f32[2,128]{1,0:T(2,128)S(1)}, u32[]{:S(2)}, u32[]{:S(2)}) collective-permute-start(f32[2,128]{1,0:T(2,128)S(1)} %get-tuple-element.48), channel_id=1, source_target_pairs={{0,1},{1,0},{2,3},{3,2},{4,5},{5,4},{6,7},{7,6},{8,9},{9,8},{10,11... | collective-permute-start | bytes 3080 | tf_op jit(solution)/shard_map/ppermute | solution.py:243
  32.2 3.6 %collective-permute-start.9 = (f32[2,128]{1,0:T(2,128)S(1)}, f32[2,128]{1,0:T(2,128)S(1)}, u32[]{:S(2)}, u32[]{:S(2)}) collective-permute-start(f32[2,128]{1,0:T(2,128)S(1)} %get-tuple-element.49), channel_id=1, source_target_pairs={{0,2},{1,3},{2,0},{3,1},{4,6},{5,7},{6,4},{7,5},{8,10},{9,11},{10,... | collective-permute-start | bytes 3080 | tf_op jit(solution)/shard_map/ppermute | solution.py:243
  33.8 3.0 %collective-permute-start.10 = (f32[2,128]{1,0:T(2,128)S(1)}, f32[2,128]{1,0:T(2,128)S(1)}, u32[]{:S(2)}, u32[]{:S(2)}) collective-permute-start(f32[2,128]{1,0:T(2,128)S(1)} %get-tuple-element.50), channel_id=1, source_target_pairs={{0,3},{1,2},{2,1},{3,0},{4,7},{5,6},{6,5},{7,4},{8,11},{9,10},{10,... | collective-permute-start | bytes 3080 | tf_op jit(solution)/shard_map/ppermute | solution.py:243

commit v6 on v5

--- a/solution.py
+++ b/solution.py
@@ -17,10 +17,10 @@
 HBM = pl.BlockSpec(memory_space=pltpu.HBM)
 
 
-def twiddles(place, order, groups, here, local_times):
+def twiddles(order, groups, here, local_times):
     slots = groups * here
     high = groups // 4
-    me = place[0]
+    me = lax.axis_index("tm")
     length = local_times * groups
     shape = (2 * slots, local_times)
     row = lax.broadcasted_iota(jnp.int32, shape, 0)
@@ -41,8 +41,8 @@
     return jnp.where(real, cosine, -sine).astype(BF16), jnp.where(real, sine, cosine).astype(BF16)
 
 
-def transform_kernel(first, ends, groups, place_ref, order_ref, vis_ref, *refs):
-    outs, (held, sums, place, order, place_sem, order_sem, sems) = refs[:-7], refs[-7:]
+def transform_kernel(first, ends, groups, order_ref, vis_ref, *refs):
+    outs, (held, sums, order, order_sem, sems) = refs[:-5], refs[-5:]
     _, chans, local_times, _ = held.shape
     here = order.shape[0] // groups
     rows = 2 * groups * here
@@ -56,16 +56,13 @@
             sems.at[t, f],
         )
 
-    place_copy = pltpu.make_async_copy(place_ref, place, place_sem)
-    place_copy.start()
     order_copy = pltpu.make_async_copy(order_ref, order, order_sem)
     order_copy.start()
     for t in range(len(tiles)):
         for f in range(chans):
             copy(t, f).start()
-    place_copy.wait()
     order_copy.wait()
-    table_re, table_im = twiddles(place, order, groups, here, local_times)
+    table_re, table_im = twiddles(order, groups, here, local_times)
     each = rows * chans // len(outs)
     for t, (begin, end) in enumerate(tiles):
         cols = pl.ds(begin, end - begin)
@@ -82,7 +79,7 @@
                 out[:, :, pl.ds(begin + lane, LANES)] = part.reshape(*out.shape[:2], LANES).astype(out.dtype)
 
 
-def transform(place, order, visibilities, first, ends, groups):
+def transform(order, visibilities, first, ends, groups):
     _, chans, times, _ = visibilities.shape
     rows = 2 * order.shape[0]
     width = ends[-1]
@@ -91,14 +88,12 @@
     return pl.pallas_call(
         functools.partial(transform_kernel, first, ends, groups),
         out_shape=[jax.ShapeDtypeStruct(shape, F32 if d == 0 else BF16) for d in range(4)],
-        in_specs=[HBM, HBM, HBM],
+        in_specs=[HBM, HBM],
         out_specs=[VMEM] * 4,
         scratch_shapes=[
             pltpu.VMEM((2, chans, times, width), BF16),
             pltpu.VMEM((widest // LANES, rows * chans, LANES), F32),
-            pltpu.SMEM(place.shape, jnp.int32),
             pltpu.SMEM(order.shape, jnp.int32),
-            pltpu.SemaphoreType.DMA,
             pltpu.SemaphoreType.DMA,
             pltpu.SemaphoreType.DMA((len(ends), chans)),
         ],
@@ -109,7 +104,7 @@
             transcendentals=0,
         ),
         name="transform",
-    )(place, order, visibilities)
+    )(order, visibilities)
 
 
 def pair_gains_kernel(gains_ref, pairs_ref, out_ref):
@@ -195,10 +190,7 @@
     )(keep, *recvs, gains, beams)
 
 
-def finish_kernel(first, n_recv, n_tel, place_ref, *refs):
-    refs, place, place_sem = refs[:-2], refs[-2], refs[-1]
-    place_copy = pltpu.make_async_copy(place_ref, place, place_sem)
-    place_copy.start()
+def finish_kernel(first, n_recv, n_tel, *refs):
     keep, recvs = refs[0], refs[1 : 1 + n_recv]
     gains, beams, basis = refs[1 + n_recv : 4 + n_recv]
     tels, outs = refs[4 + n_recv : 4 + n_recv + n_tel], refs[4 + n_recv + n_tel :]
@@ -215,8 +207,7 @@
     both = jnp.concatenate(
         [jnp.sum(total[:chans], axis=0, keepdims=True), jnp.sum(total[chans:], axis=0, keepdims=True)]
     )
-    place_copy.wait()
-    me = place[1]
+    me = lax.axis_index("freq")
     width = outs[0].shape[1]
     for apart, out in enumerate(outs):
         value = jnp.zeros((2, width), F32)
@@ -226,17 +217,16 @@
         out[...] = value
 
 
-def finish(place, keep, recvs, gains, beams, first, tels, basis, blocks):
+def finish(keep, recvs, gains, beams, first, tels, basis, blocks):
     shape = jax.ShapeDtypeStruct((2, basis.shape[2] // blocks), F32)
     return pl.pallas_call(
         functools.partial(finish_kernel, first, len(recvs), len(tels)),
         out_shape=[shape] * blocks,
-        in_specs=[HBM] + [VMEM] * (4 + len(recvs) + len(tels)),
+        in_specs=[VMEM] * (4 + len(recvs) + len(tels)),
         out_specs=[VMEM] * blocks,
-        scratch_shapes=[pltpu.SMEM(place.shape, jnp.int32), pltpu.SemaphoreType.DMA],
         compiler_params=pltpu.CompilerParams(vmem_limit_bytes=8 * MIB),
         name="finish",
-    )(place, keep, *recvs, gains, beams, basis, *tels)
+    )(keep, *recvs, gains, beams, basis, *tels)
 
 
 def swap(x, axis, mask):
@@ -257,12 +247,11 @@
 def on_device(visibilities, feed_gains, feed_pairs, m_order, beam_rows, kl_basis):
     groups = lax.axis_size("tm")
     count = visibilities.shape[3]
-    place = jnp.stack([lax.axis_index("tm"), lax.axis_index("freq")]).astype(jnp.int32)
     order = pltpu.with_memory_space_constraint(m_order, pltpu.HBM)
     firsts, sent, arrived = [0], [], []
     for tiles in PARTS:
         ends = tuple(count // SHARES * sum(tiles[: t + 1]) for t in range(len(tiles)))
-        parts = transform(place, order, visibilities, firsts[-1], ends, groups)
+        parts = transform(order, visibilities, firsts[-1], ends, groups)
         if arrived:
             parts, arrived[-1][:1] = lax.optimization_barrier((parts, arrived[-1][:1]))
         sent.append(parts)
@@ -272,8 +261,6 @@
     beams = beam_rows[:, 0]
     for index, (parts, received) in enumerate(zip(sent, arrived)):
         left, shift = groups // 4, 2
-        if index == len(PARTS) - 1:
-            received, gains = lax.optimization_barrier((received, gains))
         while left > 1:
             parts = combine(parts, received, left)
             received = exchange(parts, shift)
@@ -285,7 +272,7 @@
     tels = [project(keep, recvs, gains, beams, first) for first, (keep, recvs) in zip(firsts, spectra[:-1])]
     keep, recvs = spectra[-1]
     basis = kl_basis.reshape(kl_basis.shape[1] // 2, 2 * kl_basis.shape[2], kl_basis.shape[3])
-    held, *sent = finish(place, keep, recvs, gains, beams, firsts[-2], tels, basis, lax.axis_size("freq"))
+    held, *sent = finish(keep, recvs, gains, beams, firsts[-2], tels, basis, lax.axis_size("freq"))
     held = functools.reduce(lambda a, b: a + b, [swap(part, "freq", d + 1) for d, part in enumerate(sent)], held)
     return held[:, None, :]
 

time: 37.5 us -> 37.4 us (level)
  no operation moved by 1% of the time
where the time goes in v6:
time: 37.4 us; the launch traced here: 37.3 us
  Pallas kernels  16.9 us (45%)
  starting transfers between devices  15.2 us (41%)
  waiting for transfers between devices  4.33 us (12%)
  other arithmetic  0.68 us (2%)
    ppermute x11, starting transfers between devices, swap(): lax.ppermute(x, axis, [(i, i ^ mask) for i in range(lax.axis_size(axis))])  15.2 us
    pallas_call x2, Pallas kernels, transform(): pl.pallas_call(functools.partial(transform_kernel, first, ends, groups),...  12.8 us
    ppermute x11, waiting for transfers between devices, swap(): lax.ppermute(x, axis, [(i, i ^ mask) for i in range(lax.axis_size(axis))])  4.33 us
    pallas_call x1, Pallas kernels, project(): pl.pallas_call(functools.partial(project_kernel, first, len(recvs)), out_...  1.59 us
    pallas_call x1, Pallas kernels, pair_gains(): pl.pallas_call(pair_gains_kernel, out_shape=jax.ShapeDtypeStruct((2 * cha...  1.59 us
    pallas_call x1, Pallas kernels, finish(): pl.pallas_call(functools.partial(finish_kernel, first, len(recvs), len(te...  0.94 us
  transfers between devices with their start and end apart: 11, of which 6 were waited for; matrix products, arithmetic and copies ran while one was open for 0% of the time, Pallas kernels for 21%

profile of v6, /device:TPU:0, one launch (start us, length us, event | category | flops | bytes accessed | tf_op | source)
XLA Modules:
  0.0 37.3 jit_solution(3743573662628703780)
XLA Ops:
  0.0 8.2 %transform.3 = (f32[2,16,2816]{2,1,0:T(8,128)S(1)}, bf16[2,16,2816]{2,1,0:T(8,128)(2,1)S(1)}, bf16[2,16,2816]{2,1,0:T(8,128)(2,1)S(1)}, bf16[2,16,2816]{2,1,0:T(8,128)(2,1)S(1)}) custom-call(s32[8]{0:T(128)} %order_ref.3, bf16[2,8,256,4096]{3,2,1,0:T(8,128)(2,1)} %vis_ref.3), custom_call_target="tpu_custom_call" | custom-call | flops 11811160064 | bytes 23068672 | tf_op jit(solution)/shard_map/transform/pallas_call | solution.py:88
  8.2 4.0 %collective-permute-start = (bf16[2,16,2816]{2,1,0:T(8,128)(2,1)S(1)}, bf16[2,16,2816]{2,1,0:T(8,128)(2,1)S(1)}, u32[]{:S(2)}, u32[]{:S(2)}) collective-permute-start(bf16[2,16,2816]{2,1,0:T(8,128)(2,1)S(1)} %get-tuple-element.28), channel_id=1, source_target_pairs={{0,12},{4,8},{8,4},{12,0},{16,28},{20,24},{24,20},{28,16},{1,13},{... | collective-permute-start | bytes 540680 | tf_op jit(solution)/shard_map/ppermute | solution.py:233
  12.3 0.4 %collective-permute-start.5 = (bf16[2,16,2816]{2,1,0:T(8,128)(2,1)S(1)}, bf16[2,16,2816]{2,1,0:T(8,128)(2,1)S(1)}, u32[]{:S(2)}, u32[]{:S(2)}) collective-permute-start(bf16[2,16,2816]{2,1,0:T(8,128)(2,1)S(1)} %get-tuple-element.35), channel_id=1, source_target_pairs={{0,8},{4,12},{8,0},{12,4},{16,24},{20,28},{24,16},{28,20},{1,9},{5... | collective-permute-start | bytes 540680 | tf_op jit(solution)/shard_map/ppermute | solution.py:233
  12.7 0.2 collective-permute-start.6
  12.9 4.6 %transform.2 = (f32[2,16,1280]{2,1,0:T(8,128)S(1)}, bf16[2,16,1280]{2,1,0:T(8,128)(2,1)S(1)}, bf16[2,16,1280]{2,1,0:T(8,128)(2,1)S(1)}, bf16[2,16,1280]{2,1,0:T(8,128)(2,1)S(1)}) custom-call(s32[8]{0:T(128)} %order_ref.3, bf16[2,8,256,4096]{3,2,1,0:T(8,128)(2,1)} %vis_ref.3), custom_call_target="tpu_custom_call" | custom-call | flops 5368709120 | bytes 10485760 | tf_op jit(solution)/shard_map/transform/pallas_call | solution.py:88
  17.5 0.1 collective-permute-done
  17.6 3.0 %collective-permute-start.1 = (bf16[2,16,1280]{2,1,0:T(8,128)(2,1)S(1)}, bf16[2,16,1280]{2,1,0:T(8,128)(2,1)S(1)}, u32[]{:S(2)}, u32[]{:S(2)}) collective-permute-start(bf16[2,16,1280]{2,1,0:T(8,128)(2,1)S(1)} %get-tuple-element.30), channel_id=1, source_target_pairs={{0,12},{4,8},{8,4},{12,0},{16,28},{20,24},{24,20},{28,16},{1,13},{... | collective-permute-start | bytes 245768 | tf_op jit(solution)/shard_map/ppermute | solution.py:233
  20.6 0.4 %collective-permute-start.2 = (bf16[2,16,1280]{2,1,0:T(8,128)(2,1)S(1)}, bf16[2,16,1280]{2,1,0:T(8,128)(2,1)S(1)}, u32[]{:S(2)}, u32[]{:S(2)}) collective-permute-start(bf16[2,16,1280]{2,1,0:T(8,128)(2,1)S(1)} %get-tuple-element.31), channel_id=1, source_target_pairs={{0,8},{4,12},{8,0},{12,4},{16,24},{20,28},{24,16},{28,20},{1,9},{5... | collective-permute-start | bytes 245768 | tf_op jit(solution)/shard_map/ppermute | solution.py:233
  21.1 0.1 collective-permute-start.3
  21.2 0.2 collective-permute-done.5
  21.4 0.1 add_bitcast_fusion
  21.5 2.9 %collective-permute-start.7 = (bf16[1,16,2816]{2,1,0:T(8,128)(2,1)S(1)}, bf16[1,16,2816]{2,1,0:T(8,128)(2,1)S(1)}, u32[]{:S(2)}, u32[]{:S(2)}) collective-permute-start(bf16[1,16,2816]{2,1,0:T(8,128)(2,1)S(1)} %fusion), channel_id=1, source_target_pairs={{0,16},{4,20},{8,24},{12,28},{16,0},{20,4},{24,8},{28,12},{1,17},{... | collective-permute-start | bytes 270344 | tf_op jit(solution)/shard_map/ppermute | solution.py:233
  24.4 1.6 %pair_gains.1.refs_2_ = f32[16,4096]{1,0:T(8,128)S(1)} custom-call(f32[2,8,1024]{2,1,0:T(8,128)S(1)} %copy-done.1, s32[2,4096]{1,0:T(2,128)S(1)} %bitcast.29), custom_call_target="tpu_custom_call" | custom-call | flops 4194304 | bytes 4194304 | tf_op jit(solution)/shard_map/pair_gains/pallas_call | solution.py:138
  26.0 0.1 collective-permute-done.2
  26.1 2.1 %collective-permute-start.4 = (bf16[1,16,1280]{2,1,0:T(8,128)(2,1)S(1)}, bf16[1,16,1280]{2,1,0:T(8,128)(2,1)S(1)}, u32[]{:S(2)}, u32[]{:S(2)}) collective-permute-start(bf16[1,16,1280]{2,1,0:T(8,128)(2,1)S(1)} %fusion.1), channel_id=1, source_target_pairs={{0,16},{4,20},{8,24},{12,28},{16,0},{20,4},{24,8},{28,12},{1,17},{... | collective-permute-start | bytes 122888 | tf_op jit(solution)/shard_map/ppermute | solution.py:233
  28.3 1.6 %project.1.refs_5_ = f32[4,16,128]{2,1,0:T(8,128)S(1)} custom-call(f32[16,2816]{1,0:T(8,128)S(1)} %bitcast.25, bf16[16,2816]{1,0:T(8,128)(2,1)S(1)} %bitcast.27, f32[16,4096]{1,0:T(8,128)S(1)} %pair_gains.1.refs_2_, bf16[2,8,64,4096]{3,2,1,0:T(8,128)(2,1)S(1)} %bitcast.23), custom_call_target="tpu_custom_call" | custom-call | flops 738197504 | bytes 5767168 | tf_op jit(solution)/shard_map/project/pallas_call | solution.py:180
  29.9 1.2 %collective-permute-done.4 = bf16[1,16,1280]{2,1,0:T(8,128)(2,1)S(1)} collective-permute-done((bf16[1,16,1280]{2,1,0:T(8,128)(2,1)S(1)}, bf16[1,16,1280]{2,1,0:T(8,128)(2,1)S(1)}, u32[]{:S(2)}, u32[]{:S(2)}) %collective-permute-start.4) | collective-permute-done | bytes 40992 | tf_op jit(solution)/shard_map/ppermute | solution.py:233
  31.1 0.9 %finish.1 = (f32[2,128]{1,0:T(2,128)S(1)}, f32[2,128]{1,0:T(2,128)S(1)}, f32[2,128]{1,0:T(2,128)S(1)}, f32[2,128]{1,0:T(2,128)S(1)}) custom-call(f32[16,1280]{1,0:T(8,128)S(1)} %slice_bitcast_fusion.1.refs_0_, bf16[16,1280]{1,0:T(8,128)(2,1)S(1)} %bitcast.28, f32[16,4096]{1,0:T(8,128)S(1)} %pair_gains.1.refs_2_, bf16[2,8,64,4096]{3,2,1,0:T(8,128)(2,1)S(1)} %bitcast.24, ...), custom_call_target="tpu_custom_call" | custom-call | tf_op jit(solution)/shard_map/finish/pallas_call | solution.py:222
  32.0 0.1 collective-permute-start.8
  32.1 1.6 %collective-permute-start.9 = (f32[2,128]{1,0:T(2,128)S(1)}, f32[2,128]{1,0:T(2,128)S(1)}, u32[]{:S(2)}, u32[]{:S(2)}) collective-permute-start(f32[2,128]{1,0:T(2,128)S(1)} %get-tuple-element.41), channel_id=1, source_target_pairs={{0,2},{1,3},{2,0},{3,1},{4,6},{5,7},{6,4},{7,5},{8,10},{9,11},{10,... | collective-permute-start | bytes 3080 | tf_op jit(solution)/shard_map/ppermute | solution.py:233
  33.7 0.3 collective-permute-start.10
  34.0 1.8 %collective-permute-done.9 = f32[2,128]{1,0:T(2,128)S(1)} collective-permute-done((f32[2,128]{1,0:T(2,128)S(1)}, f32[2,128]{1,0:T(2,128)S(1)}, u32[]{:S(2)}, u32[]{:S(2)}) %collective-permute-start.9) | collective-permute-done | bytes 1056 | tf_op jit(solution)/shard_map/ppermute | solution.py:233
  35.7 0.9 %collective-permute-done.10 = f32[2,128]{1,0:T(2,128)S(1)} collective-permute-done((f32[2,128]{1,0:T(2,128)S(1)}, f32[2,128]{1,0:T(2,128)S(1)}, u32[]{:S(2)}, u32[]{:S(2)}) %collective-permute-start.10) | collective-permute-done | bytes 1056 | tf_op jit(solution)/shard_map/ppermute | solution.py:233
  36.7 0.6 %add_add_fusion = f32[2,128]{1,0:T(2,128)} fusion(f32[2,128]{1,0:T(2,128)S(1)} %collective-permute-done.10, f32[2,128]{1,0:T(2,128)S(1)} %collective-permute-done.9, f32[2,128]{1,0:T(2,128)S(1)} %get-tuple-element.39, f32[2,128]{1,0:T(2,128)S(1)} %collective-permute-done.8), kind=kLoop, calls=%fused_computation.8 | loop fusion | flops 768 | bytes 5120 | tf_op jit(solution)/shard_map/add | solution.py:276
  (21 shorter events, 0.1 us)
Async XLA Ops:
  0.0 24.4 %copy-start.1 = (f32[2,8,1024]{2,1,0:T(8,128)S(1)}, f32[2,8,1024]{2,1,0:T(8,128)}, u32[]{:S(2)}) copy-start(f32[2,8,1024]{2,1,0:T(8,128)} %gains_ref) | copy-start | bytes 196612
  0.0 24.4 %copy-start.2 = (s32[4096,2]{0,1:T(2,128)S(1)}, s32[4096,2]{0,1:T(2,128)}, u32[]{:S(2)}) copy-start(s32[4096,2]{0,1:T(2,128)} %param.8) | copy-start | bytes 98308
  8.2 20.1 %slice-start = ((s8[8388608]{0:T(1024)(128)(4,1)}), s8[4194304]{0:T(1024)(128)(4,1)S(1)}, s32[]{:S(2)}) async-start(s8[8388608]{0:T(1024)(128)(4,1)} %bitcast.21), calls=%async_computation | async-start | bytes 8388608
  8.2 22.9 %copy-start = (bf16[1,8,64,512]{3,2,1,0:T(8,128)(2,1)S(1)}, bf16[1,8,64,512]{3,2,1,0:T(8,128)(2,1)}, u32[]{:S(2)}) copy-start(bf16[1,8,64,512]{3,2,1,0:T(8,128)(2,1)} %param.11) | copy-start | bytes 1572868
  8.2 9.4 %collective-permute-start = (bf16[2,16,2816]{2,1,0:T(8,128)(2,1)S(1)}, bf16[2,16,2816]{2,1,0:T(8,128)(2,1)S(1)}, u32[]{:S(2)}, u32[]{:S(2)}) collective-permute-start(bf16[2,16,2816]{2,1,0:T(8,128)(2,1)S(1)} %get-tuple-element.28), channel_id=1, source_target_pairs={{0,12},{4,8},{8,4},{12,0},{16,28},{20,24},{24,20},{28,16},{1,13},{... | collective-permute-start | bytes 540680 | tf_op jit(solution)/shard_map/ppermute | solution.py:233
  12.3 9.1 %collective-permute-start.5 = (bf16[2,16,2816]{2,1,0:T(8,128)(2,1)S(1)}, bf16[2,16,2816]{2,1,0:T(8,128)(2,1)S(1)}, u32[]{:S(2)}, u32[]{:S(2)}) collective-permute-start(bf16[2,16,2816]{2,1,0:T(8,128)(2,1)S(1)} %get-tuple-element.35), channel_id=1, source_target_pairs={{0,8},{4,12},{8,0},{12,4},{16,24},{20,28},{24,16},{28,20},{1,9},{5... | collective-permute-start | bytes 540680 | tf_op jit(solution)/shard_map/ppermute | solution.py:233
  12.7 15.6 %slice-start.1 = ((s8[8388608]{0:T(1024)(128)(4,1)}), s8[4194304]{0:T(1024)(128)(4,1)S(1)}, s32[]{:S(2)}) async-start(s8[8388608]{0:T(1024)(128)(4,1)} %bitcast.21), calls=%async_computation.1 | async-start | bytes 8388608
  12.7 8.7 %collective-permute-start.6 = (bf16[2,16,2816]{2,1,0:T(8,128)(2,1)S(1)}, bf16[2,16,2816]{2,1,0:T(8,128)(2,1)S(1)}, u32[]{:S(2)}, u32[]{:S(2)}) collective-permute-start(bf16[2,16,2816]{2,1,0:T(8,128)(2,1)S(1)} %get-tuple-element.36), channel_id=1, source_target_pairs={{0,4},{4,0},{8,12},{12,8},{16,20},{20,16},{24,28},{28,24},{1,5},{5... | collective-permute-start | bytes 540680 | tf_op jit(solution)/shard_map/ppermute | solution.py:233
  17.6 8.3 %collective-permute-start.1 = (bf16[2,16,1280]{2,1,0:T(8,128)(2,1)S(1)}, bf16[2,16,1280]{2,1,0:T(8,128)(2,1)S(1)}, u32[]{:S(2)}, u32[]{:S(2)}) collective-permute-start(bf16[2,16,1280]{2,1,0:T(8,128)(2,1)S(1)} %get-tuple-element.30), channel_id=1, source_target_pairs={{0,12},{4,8},{8,4},{12,0},{16,28},{20,24},{24,20},{28,16},{1,13},{... | collective-permute-start | bytes 245768 | tf_op jit(solution)/shard_map/ppermute | solution.py:233
  20.6 5.4 %collective-permute-start.2 = (bf16[2,16,1280]{2,1,0:T(8,128)(2,1)S(1)}, bf16[2,16,1280]{2,1,0:T(8,128)(2,1)S(1)}, u32[]{:S(2)}, u32[]{:S(2)}) collective-permute-start(bf16[2,16,1280]{2,1,0:T(8,128)(2,1)S(1)} %get-tuple-element.31), channel_id=1, source_target_pairs={{0,8},{4,12},{8,0},{12,4},{16,24},{20,28},{24,16},{28,20},{1,9},{5... | collective-permute-start | bytes 245768 | tf_op jit(solution)/shard_map/ppermute | solution.py:233
  21.1 5.0 %collective-permute-start.3 = (bf16[2,16,1280]{2,1,0:T(8,128)(2,1)S(1)}, bf16[2,16,1280]{2,1,0:T(8,128)(2,1)S(1)}, u32[]{:S(2)}, u32[]{:S(2)}) collective-permute-start(bf16[2,16,1280]{2,1,0:T(8,128)(2,1)S(1)} %get-tuple-element.32), channel_id=1, source_target_pairs={{0,4},{4,0},{8,12},{12,8},{16,20},{20,16},{24,28},{28,24},{1,5},{5... | collective-permute-start | bytes 245768 | tf_op jit(solution)/shard_map/ppermute | solution.py:233
  21.5 6.8 %collective-permute-start.7 = (bf16[1,16,2816]{2,1,0:T(8,128)(2,1)S(1)}, bf16[1,16,2816]{2,1,0:T(8,128)(2,1)S(1)}, u32[]{:S(2)}, u32[]{:S(2)}) collective-permute-start(bf16[1,16,2816]{2,1,0:T(8,128)(2,1)S(1)} %fusion), channel_id=1, source_target_pairs={{0,16},{4,20},{8,24},{12,28},{16,0},{20,4},{24,8},{28,12},{1,17},{... | collective-permute-start | bytes 270344 | tf_op jit(solution)/shard_map/ppermute | solution.py:233
  26.1 5.0 %collective-permute-start.4 = (bf16[1,16,1280]{2,1,0:T(8,128)(2,1)S(1)}, bf16[1,16,1280]{2,1,0:T(8,128)(2,1)S(1)}, u32[]{:S(2)}, u32[]{:S(2)}) collective-permute-start(bf16[1,16,1280]{2,1,0:T(8,128)(2,1)S(1)} %fusion.1), channel_id=1, source_target_pairs={{0,16},{4,20},{8,24},{12,28},{16,0},{20,4},{24,8},{28,12},{1,17},{... | collective-permute-start | bytes 122888 | tf_op jit(solution)/shard_map/ppermute | solution.py:233
  32.0 1.9 %collective-permute-start.8 = (f32[2,128]{1,0:T(2,128)S(1)}, f32[2,128]{1,0:T(2,128)S(1)}, u32[]{:S(2)}, u32[]{:S(2)}) collective-permute-start(f32[2,128]{1,0:T(2,128)S(1)} %get-tuple-element.40), channel_id=1, source_target_pairs={{0,1},{1,0},{2,3},{3,2},{4,5},{5,4},{6,7},{7,6},{8,9},{9,8},{10,11... | collective-permute-start | bytes 3080 | tf_op jit(solution)/shard_map/ppermute | solution.py:233
  32.1 3.6 %collective-permute-start.9 = (f32[2,128]{1,0:T(2,128)S(1)}, f32[2,128]{1,0:T(2,128)S(1)}, u32[]{:S(2)}, u32[]{:S(2)}) collective-permute-start(f32[2,128]{1,0:T(2,128)S(1)} %get-tuple-element.41), channel_id=1, source_target_pairs={{0,2},{1,3},{2,0},{3,1},{4,6},{5,7},{6,4},{7,5},{8,10},{9,11},{10,... | collective-permute-start | bytes 3080 | tf_op jit(solution)/shard_map/ppermute | solution.py:233
  33.7 3.0 %collective-permute-start.10 = (f32[2,128]{1,0:T(2,128)S(1)}, f32[2,128]{1,0:T(2,128)S(1)}, u32[]{:S(2)}, u32[]{:S(2)}) collective-permute-start(f32[2,128]{1,0:T(2,128)S(1)} %get-tuple-element.42), channel_id=1, source_target_pairs={{0,3},{1,2},{2,1},{3,0},{4,7},{5,6},{6,5},{7,4},{8,11},{9,10},{10,... | collective-permute-start | bytes 3080 | tf_op jit(solution)/shard_map/ppermute | solution.py:233

commit v7 on v6

--- a/solution.py
+++ b/solution.py
@@ -273,7 +273,7 @@
     keep, recvs = spectra[-1]
     basis = kl_basis.reshape(kl_basis.shape[1] // 2, 2 * kl_basis.shape[2], kl_basis.shape[3])
     held, *sent = finish(keep, recvs, gains, beams, firsts[-2], tels, basis, lax.axis_size("freq"))
-    held = functools.reduce(lambda a, b: a + b, [swap(part, "freq", d + 1) for d, part in enumerate(sent)], held)
+    held = functools.reduce(lambda a, b: a + b, [swap(sent[d - 1], "freq", d) for d in range(len(sent), 0, -1)], held)
     return held[:, None, :]
 
 

time: 37.4 us -> 36.5 us (0.976)
  waiting for transfers between devices: 4.33 us -> 3.4 us
    ppermute x11, waiting for transfers between devices: 4.33 us -> 3.4 us  [swap(): lax.ppermute(x, axis, [(i, i ^ mask) for i in range(lax.axis_size(axis))])]
where the time goes in v7:
time: 36.5 us; the launch traced here: 36.3 us
  Pallas kernels  16.9 us (46%)
  starting transfers between devices  15.1 us (41%)
  waiting for transfers between devices  3.4 us (9%)
  other arithmetic  0.68 us (2%)
    ppermute x11, starting transfers between devices, swap(): lax.ppermute(x, axis, [(i, i ^ mask) for i in range(lax.axis_size(axis))])  15.1 us
    pallas_call x2, Pallas kernels, transform(): pl.pallas_call(functools.partial(transform_kernel, first, ends, groups),...  12.8 us
    ppermute x11, waiting for transfers between devices, swap(): lax.ppermute(x, axis, [(i, i ^ mask) for i in range(lax.axis_size(axis))])  3.4 us
    pallas_call x1, Pallas kernels, project(): pl.pallas_call(functools.partial(project_kernel, first, len(recvs)), out_...  1.59 us
    pallas_call x1, Pallas kernels, pair_gains(): pl.pallas_call(pair_gains_kernel, out_shape=jax.ShapeDtypeStruct((2 * cha...  1.59 us
    pallas_call x1, Pallas kernels, finish(): pl.pallas_call(functools.partial(finish_kernel, first, len(recvs), len(te...  0.94 us
  transfers between devices with their start and end apart: 11, of which 6 were waited for; matrix products, arithmetic and copies ran while one was open for 0% of the time, Pallas kernels for 21%

profile of v7, /device:TPU:0, one launch (start us, length us, event | category | flops | bytes accessed | tf_op | source)
XLA Modules:
  0.0 36.3 jit_solution(12483120299341700928)
XLA Ops:
  0.0 8.2 %transform.3 = (f32[2,16,2816]{2,1,0:T(8,128)S(1)}, bf16[2,16,2816]{2,1,0:T(8,128)(2,1)S(1)}, bf16[2,16,2816]{2,1,0:T(8,128)(2,1)S(1)}, bf16[2,16,2816]{2,1,0:T(8,128)(2,1)S(1)}) custom-call(s32[8]{0:T(128)} %order_ref.3, bf16[2,8,256,4096]{3,2,1,0:T(8,128)(2,1)} %vis_ref.3), custom_call_target="tpu_custom_call" | custom-call | flops 11811160064 | bytes 23068672 | tf_op jit(solution)/shard_map/transform/pallas_call | solution.py:88
  8.2 4.0 %collective-permute-start = (bf16[2,16,2816]{2,1,0:T(8,128)(2,1)S(1)}, bf16[2,16,2816]{2,1,0:T(8,128)(2,1)S(1)}, u32[]{:S(2)}, u32[]{:S(2)}) collective-permute-start(bf16[2,16,2816]{2,1,0:T(8,128)(2,1)S(1)} %get-tuple-element.28), channel_id=1, source_target_pairs={{0,12},{4,8},{8,4},{12,0},{16,28},{20,24},{24,20},{28,16},{1,13},{... | collective-permute-start | bytes 540680 | tf_op jit(solution)/shard_map/ppermute | solution.py:233
  12.3 0.4 %collective-permute-start.5 = (bf16[2,16,2816]{2,1,0:T(8,128)(2,1)S(1)}, bf16[2,16,2816]{2,1,0:T(8,128)(2,1)S(1)}, u32[]{:S(2)}, u32[]{:S(2)}) collective-permute-start(bf16[2,16,2816]{2,1,0:T(8,128)(2,1)S(1)} %get-tuple-element.35), channel_id=1, source_target_pairs={{0,8},{4,12},{8,0},{12,4},{16,24},{20,28},{24,16},{28,20},{1,9},{5... | collective-permute-start | bytes 540680 | tf_op jit(solution)/shard_map/ppermute | solution.py:233
  12.7 0.2 collective-permute-start.6
  12.9 4.6 %transform.2 = (f32[2,16,1280]{2,1,0:T(8,128)S(1)}, bf16[2,16,1280]{2,1,0:T(8,128)(2,1)S(1)}, bf16[2,16,1280]{2,1,0:T(8,128)(2,1)S(1)}, bf16[2,16,1280]{2,1,0:T(8,128)(2,1)S(1)}) custom-call(s32[8]{0:T(128)} %order_ref.3, bf16[2,8,256,4096]{3,2,1,0:T(8,128)(2,1)} %vis_ref.3), custom_call_target="tpu_custom_call" | custom-call | flops 5368709120 | bytes 10485760 | tf_op jit(solution)/shard_map/transform/pallas_call | solution.py:88
  17.5 0.1 collective-permute-done
  17.6 3.0 %collective-permute-start.1 = (bf16[2,16,1280]{2,1,0:T(8,128)(2,1)S(1)}, bf16[2,16,1280]{2,1,0:T(8,128)(2,1)S(1)}, u32[]{:S(2)}, u32[]{:S(2)}) collective-permute-start(bf16[2,16,1280]{2,1,0:T(8,128)(2,1)S(1)} %get-tuple-element.30), channel_id=1, source_target_pairs={{0,12},{4,8},{8,4},{12,0},{16,28},{20,24},{24,20},{28,16},{1,13},{... | collective-permute-start | bytes 245768 | tf_op jit(solution)/shard_map/ppermute | solution.py:233
  20.6 0.4 %collective-permute-start.2 = (bf16[2,16,1280]{2,1,0:T(8,128)(2,1)S(1)}, bf16[2,16,1280]{2,1,0:T(8,128)(2,1)S(1)}, u32[]{:S(2)}, u32[]{:S(2)}) collective-permute-start(bf16[2,16,1280]{2,1,0:T(8,128)(2,1)S(1)} %get-tuple-element.31), channel_id=1, source_target_pairs={{0,8},{4,12},{8,0},{12,4},{16,24},{20,28},{24,16},{28,20},{1,9},{5... | collective-permute-start | bytes 245768 | tf_op jit(solution)/shard_map/ppermute | solution.py:233
  21.1 0.1 collective-permute-start.3
  21.2 0.2 collective-permute-done.5
  21.4 0.1 add_bitcast_fusion
  21.5 2.9 %collective-permute-start.7 = (bf16[1,16,2816]{2,1,0:T(8,128)(2,1)S(1)}, bf16[1,16,2816]{2,1,0:T(8,128)(2,1)S(1)}, u32[]{:S(2)}, u32[]{:S(2)}) collective-permute-start(bf16[1,16,2816]{2,1,0:T(8,128)(2,1)S(1)} %fusion), channel_id=1, source_target_pairs={{0,16},{4,20},{8,24},{12,28},{16,0},{20,4},{24,8},{28,12},{1,17},{... | collective-permute-start | bytes 270344 | tf_op jit(solution)/shard_map/ppermute | solution.py:233
  24.4 1.6 %pair_gains.1.refs_2_ = f32[16,4096]{1,0:T(8,128)S(1)} custom-call(f32[2,8,1024]{2,1,0:T(8,128)S(1)} %copy-done.1, s32[2,4096]{1,0:T(2,128)S(1)} %bitcast.29), custom_call_target="tpu_custom_call" | custom-call | flops 4194304 | bytes 4194304 | tf_op jit(solution)/shard_map/pair_gains/pallas_call | solution.py:138
  26.0 0.1 collective-permute-done.2
  26.1 2.1 %collective-permute-start.4 = (bf16[1,16,1280]{2,1,0:T(8,128)(2,1)S(1)}, bf16[1,16,1280]{2,1,0:T(8,128)(2,1)S(1)}, u32[]{:S(2)}, u32[]{:S(2)}) collective-permute-start(bf16[1,16,1280]{2,1,0:T(8,128)(2,1)S(1)} %fusion.1), channel_id=1, source_target_pairs={{0,16},{4,20},{8,24},{12,28},{16,0},{20,4},{24,8},{28,12},{1,17},{... | collective-permute-start | bytes 122888 | tf_op jit(solution)/shard_map/ppermute | solution.py:233
  28.3 1.6 %project.1.refs_5_ = f32[4,16,128]{2,1,0:T(8,128)S(1)} custom-call(f32[16,2816]{1,0:T(8,128)S(1)} %bitcast.25, bf16[16,2816]{1,0:T(8,128)(2,1)S(1)} %bitcast.27, f32[16,4096]{1,0:T(8,128)S(1)} %pair_gains.1.refs_2_, bf16[2,8,64,4096]{3,2,1,0:T(8,128)(2,1)S(1)} %bitcast.23), custom_call_target="tpu_custom_call" | custom-call | flops 738197504 | bytes 5767168 | tf_op jit(solution)/shard_map/project/pallas_call | solution.py:180
  29.9 1.2 %collective-permute-done.4 = bf16[1,16,1280]{2,1,0:T(8,128)(2,1)S(1)} collective-permute-done((bf16[1,16,1280]{2,1,0:T(8,128)(2,1)S(1)}, bf16[1,16,1280]{2,1,0:T(8,128)(2,1)S(1)}, u32[]{:S(2)}, u32[]{:S(2)}) %collective-permute-start.4) | collective-permute-done | bytes 40992 | tf_op jit(solution)/shard_map/ppermute | solution.py:233
  31.1 0.9 %finish.1 = (f32[2,128]{1,0:T(2,128)S(1)}, f32[2,128]{1,0:T(2,128)S(1)}, f32[2,128]{1,0:T(2,128)S(1)}, f32[2,128]{1,0:T(2,128)S(1)}) custom-call(f32[16,1280]{1,0:T(8,128)S(1)} %slice_bitcast_fusion.1.refs_0_, bf16[16,1280]{1,0:T(8,128)(2,1)S(1)} %bitcast.28, f32[16,4096]{1,0:T(8,128)S(1)} %pair_gains.1.refs_2_, bf16[2,8,64,4096]{3,2,1,0:T(8,128)(2,1)S(1)} %bitcast.24, ...), custom_call_target="tpu_custom_call" | custom-call | tf_op jit(solution)/shard_map/finish/pallas_call | solution.py:222
  32.0 0.1 collective-permute-start.8
  32.1 1.6 %collective-permute-start.9 = (f32[2,128]{1,0:T(2,128)S(1)}, f32[2,128]{1,0:T(2,128)S(1)}, u32[]{:S(2)}, u32[]{:S(2)}) collective-permute-start(f32[2,128]{1,0:T(2,128)S(1)} %get-tuple-element.41), channel_id=1, source_target_pairs={{0,2},{1,3},{2,0},{3,1},{4,6},{5,7},{6,4},{7,5},{8,10},{9,11},{10,... | collective-permute-start | bytes 3080 | tf_op jit(solution)/shard_map/ppermute | solution.py:233
  33.7 0.3 collective-permute-start.10
  34.0 1.1 %collective-permute-done.8 = f32[2,128]{1,0:T(2,128)S(1)} collective-permute-done((f32[2,128]{1,0:T(2,128)S(1)}, f32[2,128]{1,0:T(2,128)S(1)}, u32[]{:S(2)}, u32[]{:S(2)}) %collective-permute-start.8) | collective-permute-done | bytes 1056 | tf_op jit(solution)/shard_map/ppermute | solution.py:233
  35.1 0.7 %collective-permute-done.9 = f32[2,128]{1,0:T(2,128)S(1)} collective-permute-done((f32[2,128]{1,0:T(2,128)S(1)}, f32[2,128]{1,0:T(2,128)S(1)}, u32[]{:S(2)}, u32[]{:S(2)}) %collective-permute-start.9) | collective-permute-done | bytes 1056 | tf_op jit(solution)/shard_map/ppermute | solution.py:233
  35.7 0.6 %add_add_fusion = f32[2,128]{1,0:T(2,128)} fusion(f32[2,128]{1,0:T(2,128)S(1)} %collective-permute-done.10, f32[2,128]{1,0:T(2,128)S(1)} %collective-permute-done.9, f32[2,128]{1,0:T(2,128)S(1)} %get-tuple-element.39, f32[2,128]{1,0:T(2,128)S(1)} %collective-permute-done.8), kind=kLoop, calls=%fused_computation.8 | loop fusion | flops 768 | bytes 5120 | tf_op jit(solution)/shard_map/add | solution.py:276
  (21 shorter events, 0.1 us)
Async XLA Ops:
  0.0 24.4 %copy-start.1 = (f32[2,8,1024]{2,1,0:T(8,128)S(1)}, f32[2,8,1024]{2,1,0:T(8,128)}, u32[]{:S(2)}) copy-start(f32[2,8,1024]{2,1,0:T(8,128)} %gains_ref) | copy-start | bytes 196612
  0.0 24.4 %copy-start.2 = (s32[4096,2]{0,1:T(2,128)S(1)}, s32[4096,2]{0,1:T(2,128)}, u32[]{:S(2)}) copy-start(s32[4096,2]{0,1:T(2,128)} %param.8) | copy-start | bytes 98308
  8.2 20.1 %slice-start = ((s8[8388608]{0:T(1024)(128)(4,1)}), s8[4194304]{0:T(1024)(128)(4,1)S(1)}, s32[]{:S(2)}) async-start(s8[8388608]{0:T(1024)(128)(4,1)} %bitcast.21), calls=%async_computation | async-start | bytes 8388608
  8.2 22.9 %copy-start = (bf16[1,8,64,512]{3,2,1,0:T(8,128)(2,1)S(1)}, bf16[1,8,64,512]{3,2,1,0:T(8,128)(2,1)}, u32[]{:S(2)}) copy-start(bf16[1,8,64,512]{3,2,1,0:T(8,128)(2,1)} %param.11) | copy-start | bytes 1572868
  8.2 9.4 %collective-permute-start = (bf16[2,16,2816]{2,1,0:T(8,128)(2,1)S(1)}, bf16[2,16,2816]{2,1,0:T(8,128)(2,1)S(1)}, u32[]{:S(2)}, u32[]{:S(2)}) collective-permute-start(bf16[2,16,2816]{2,1,0:T(8,128)(2,1)S(1)} %get-tuple-element.28), channel_id=1, source_target_pairs={{0,12},{4,8},{8,4},{12,0},{16,28},{20,24},{24,20},{28,16},{1,13},{... | collective-permute-start | bytes 540680 | tf_op jit(solution)/shard_map/ppermute | solution.py:233
  12.3 9.1 %collective-permute-start.5 = (bf16[2,16,2816]{2,1,0:T(8,128)(2,1)S(1)}, bf16[2,16,2816]{2,1,0:T(8,128)(2,1)S(1)}, u32[]{:S(2)}, u32[]{:S(2)}) collective-permute-start(bf16[2,16,2816]{2,1,0:T(8,128)(2,1)S(1)} %get-tuple-element.35), channel_id=1, source_target_pairs={{0,8},{4,12},{8,0},{12,4},{16,24},{20,28},{24,16},{28,20},{1,9},{5... | collective-permute-start | bytes 540680 | tf_op jit(solution)/shard_map/ppermute | solution.py:233
  12.7 15.6 %slice-start.1 = ((s8[8388608]{0:T(1024)(128)(4,1)}), s8[4194304]{0:T(1024)(128)(4,1)S(1)}, s32[]{:S(2)}) async-start(s8[8388608]{0:T(1024)(128)(4,1)} %bitcast.21), calls=%async_computation.1 | async-start | bytes 8388608
  12.7 8.7 %collective-permute-start.6 = (bf16[2,16,2816]{2,1,0:T(8,128)(2,1)S(1)}, bf16[2,16,2816]{2,1,0:T(8,128)(2,1)S(1)}, u32[]{:S(2)}, u32[]{:S(2)}) collective-permute-start(bf16[2,16,2816]{2,1,0:T(8,128)(2,1)S(1)} %get-tuple-element.36), channel_id=1, source_target_pairs={{0,4},{4,0},{8,12},{12,8},{16,20},{20,16},{24,28},{28,24},{1,5},{5... | collective-permute-start | bytes 540680 | tf_op jit(solution)/shard_map/ppermute | solution.py:233
  17.6 8.3 %collective-permute-start.1 = (bf16[2,16,1280]{2,1,0:T(8,128)(2,1)S(1)}, bf16[2,16,1280]{2,1,0:T(8,128)(2,1)S(1)}, u32[]{:S(2)}, u32[]{:S(2)}) collective-permute-start(bf16[2,16,1280]{2,1,0:T(8,128)(2,1)S(1)} %get-tuple-element.30), channel_id=1, source_target_pairs={{0,12},{4,8},{8,4},{12,0},{16,28},{20,24},{24,20},{28,16},{1,13},{... | collective-permute-start | bytes 245768 | tf_op jit(solution)/shard_map/ppermute | solution.py:233
  20.6 5.4 %collective-permute-start.2 = (bf16[2,16,1280]{2,1,0:T(8,128)(2,1)S(1)}, bf16[2,16,1280]{2,1,0:T(8,128)(2,1)S(1)}, u32[]{:S(2)}, u32[]{:S(2)}) collective-permute-start(bf16[2,16,1280]{2,1,0:T(8,128)(2,1)S(1)} %get-tuple-element.31), channel_id=1, source_target_pairs={{0,8},{4,12},{8,0},{12,4},{16,24},{20,28},{24,16},{28,20},{1,9},{5... | collective-permute-start | bytes 245768 | tf_op jit(solution)/shard_map/ppermute | solution.py:233
  21.1 5.0 %collective-permute-start.3 = (bf16[2,16,1280]{2,1,0:T(8,128)(2,1)S(1)}, bf16[2,16,1280]{2,1,0:T(8,128)(2,1)S(1)}, u32[]{:S(2)}, u32[]{:S(2)}) collective-permute-start(bf16[2,16,1280]{2,1,0:T(8,128)(2,1)S(1)} %get-tuple-element.32), channel_id=1, source_target_pairs={{0,4},{4,0},{8,12},{12,8},{16,20},{20,16},{24,28},{28,24},{1,5},{5... | collective-permute-start | bytes 245768 | tf_op jit(solution)/shard_map/ppermute | solution.py:233
  21.5 6.8 %collective-permute-start.7 = (bf16[1,16,2816]{2,1,0:T(8,128)(2,1)S(1)}, bf16[1,16,2816]{2,1,0:T(8,128)(2,1)S(1)}, u32[]{:S(2)}, u32[]{:S(2)}) collective-permute-start(bf16[1,16,2816]{2,1,0:T(8,128)(2,1)S(1)} %fusion), channel_id=1, source_target_pairs={{0,16},{4,20},{8,24},{12,28},{16,0},{20,4},{24,8},{28,12},{1,17},{... | collective-permute-start | bytes 270344 | tf_op jit(solution)/shard_map/ppermute | solution.py:233
  26.1 5.0 %collective-permute-start.4 = (bf16[1,16,1280]{2,1,0:T(8,128)(2,1)S(1)}, bf16[1,16,1280]{2,1,0:T(8,128)(2,1)S(1)}, u32[]{:S(2)}, u32[]{:S(2)}) collective-permute-start(bf16[1,16,1280]{2,1,0:T(8,128)(2,1)S(1)} %fusion.1), channel_id=1, source_target_pairs={{0,16},{4,20},{8,24},{12,28},{16,0},{20,4},{24,8},{28,12},{1,17},{... | collective-permute-start | bytes 122888 | tf_op jit(solution)/shard_map/ppermute | solution.py:233
  32.0 3.1 %collective-permute-start.8 = (f32[2,128]{1,0:T(2,128)S(1)}, f32[2,128]{1,0:T(2,128)S(1)}, u32[]{:S(2)}, u32[]{:S(2)}) collective-permute-start(f32[2,128]{1,0:T(2,128)S(1)} %get-tuple-element.40), channel_id=1, source_target_pairs={{0,3},{1,2},{2,1},{3,0},{4,7},{5,6},{6,5},{7,4},{8,11},{9,10},{10,... | collective-permute-start | bytes 3080 | tf_op jit(solution)/shard_map/ppermute | solution.py:233
  32.1 3.6 %collective-permute-start.9 = (f32[2,128]{1,0:T(2,128)S(1)}, f32[2,128]{1,0:T(2,128)S(1)}, u32[]{:S(2)}, u32[]{:S(2)}) collective-permute-start(f32[2,128]{1,0:T(2,128)S(1)} %get-tuple-element.41), channel_id=1, source_target_pairs={{0,2},{1,3},{2,0},{3,1},{4,6},{5,7},{6,4},{7,5},{8,10},{9,11},{10,... | collective-permute-start | bytes 3080 | tf_op jit(solution)/shard_map/ppermute | solution.py:233
  33.7 2.1 %collective-permute-start.10 = (f32[2,128]{1,0:T(2,128)S(1)}, f32[2,128]{1,0:T(2,128)S(1)}, u32[]{:S(2)}, u32[]{:S(2)}) collective-permute-start(f32[2,128]{1,0:T(2,128)S(1)} %get-tuple-element.42), channel_id=1, source_target_pairs={{0,1},{1,0},{2,3},{3,2},{4,5},{5,4},{6,7},{7,6},{8,9},{9,8},{10,11... | collective-permute-start | bytes 3080 | tf_op jit(solution)/shard_map/ppermute | solution.py:233

commit v8 on v7

--- a/solution.py
+++ b/solution.py
@@ -129,7 +129,7 @@
         out_ref[chans : 2 * chans, cols] = i_im * j_re - i_re * j_im
         return 0
 
-    lax.fori_loop(0, pairs_ref.shape[1] // LANES, step, 0, unroll=8)
+    lax.fori_loop(0, pairs_ref.shape[1] // LANES, step, 0, unroll=16)
 
 
 def pair_gains(feed_gains, feed_pairs):

time: 36.5 us -> 36.5 us (level)
  no operation moved by 1% of the time
where the time goes in v8:
time: 36.5 us; the launch traced here: 36.3 us
  Pallas kernels  16.8 us (46%)
  starting transfers between devices  15.1 us (41%)
  waiting for transfers between devices  3.55 us (10%)
  other arithmetic  0.68 us (2%)
    ppermute x11, starting transfers between devices, swap(): lax.ppermute(x, axis, [(i, i ^ mask) for i in range(lax.axis_size(axis))])  15.1 us
    pallas_call x2, Pallas kernels, transform(): pl.pallas_call(functools.partial(transform_kernel, first, ends, groups),...  12.8 us
    ppermute x11, waiting for transfers between devices, swap(): lax.ppermute(x, axis, [(i, i ^ mask) for i in range(lax.axis_size(axis))])  3.55 us
    pallas_call x1, Pallas kernels, project(): pl.pallas_call(functools.partial(project_kernel, first, len(recvs)), out_...  1.59 us
    pallas_call x1, Pallas kernels, pair_gains(): pl.pallas_call(pair_gains_kernel, out_shape=jax.ShapeDtypeStruct((2 * cha...  1.43 us
    pallas_call x1, Pallas kernels, finish(): pl.pallas_call(functools.partial(finish_kernel, first, len(recvs), len(te...  0.94 us
  transfers between devices with their start and end apart: 11, of which 6 were waited for; matrix products, arithmetic and copies ran while one was open for 0% of the time, Pallas kernels for 21%

profile of v8, /device:TPU:0, one launch (start us, length us, event | category | flops | bytes accessed | tf_op | source)
XLA Modules:
  0.0 36.3 jit_solution(723077318290969856)
XLA Ops:
  0.0 8.2 %transform.3 = (f32[2,16,2816]{2,1,0:T(8,128)S(1)}, bf16[2,16,2816]{2,1,0:T(8,128)(2,1)S(1)}, bf16[2,16,2816]{2,1,0:T(8,128)(2,1)S(1)}, bf16[2,16,2816]{2,1,0:T(8,128)(2,1)S(1)}) custom-call(s32[8]{0:T(128)} %order_ref.3, bf16[2,8,256,4096]{3,2,1,0:T(8,128)(2,1)} %vis_ref.3), custom_call_target="tpu_custom_call" | custom-call | flops 11811160064 | bytes 23068672 | tf_op jit(solution)/shard_map/transform/pallas_call | solution.py:88
  8.2 4.0 %collective-permute-start = (bf16[2,16,2816]{2,1,0:T(8,128)(2,1)S(1)}, bf16[2,16,2816]{2,1,0:T(8,128)(2,1)S(1)}, u32[]{:S(2)}, u32[]{:S(2)}) collective-permute-start(bf16[2,16,2816]{2,1,0:T(8,128)(2,1)S(1)} %get-tuple-element.28), channel_id=1, source_target_pairs={{0,12},{4,8},{8,4},{12,0},{16,28},{20,24},{24,20},{28,16},{1,13},{... | collective-permute-start | bytes 540680 | tf_op jit(solution)/shard_map/ppermute | solution.py:233
  12.3 0.4 %collective-permute-start.5 = (bf16[2,16,2816]{2,1,0:T(8,128)(2,1)S(1)}, bf16[2,16,2816]{2,1,0:T(8,128)(2,1)S(1)}, u32[]{:S(2)}, u32[]{:S(2)}) collective-permute-start(bf16[2,16,2816]{2,1,0:T(8,128)(2,1)S(1)} %get-tuple-element.35), channel_id=1, source_target_pairs={{0,8},{4,12},{8,0},{12,4},{16,24},{20,28},{24,16},{28,20},{1,9},{5... | collective-permute-start | bytes 540680 | tf_op jit(solution)/shard_map/ppermute | solution.py:233
  12.7 0.2 collective-permute-start.6
  12.9 4.6 %transform.2 = (f32[2,16,1280]{2,1,0:T(8,128)S(1)}, bf16[2,16,1280]{2,1,0:T(8,128)(2,1)S(1)}, bf16[2,16,1280]{2,1,0:T(8,128)(2,1)S(1)}, bf16[2,16,1280]{2,1,0:T(8,128)(2,1)S(1)}) custom-call(s32[8]{0:T(128)} %order_ref.3, bf16[2,8,256,4096]{3,2,1,0:T(8,128)(2,1)} %vis_ref.3), custom_call_target="tpu_custom_call" | custom-call | flops 5368709120 | bytes 10485760 | tf_op jit(solution)/shard_map/transform/pallas_call | solution.py:88
  17.5 0.1 collective-permute-done
  17.6 3.0 %collective-permute-start.1 = (bf16[2,16,1280]{2,1,0:T(8,128)(2,1)S(1)}, bf16[2,16,1280]{2,1,0:T(8,128)(2,1)S(1)}, u32[]{:S(2)}, u32[]{:S(2)}) collective-permute-start(bf16[2,16,1280]{2,1,0:T(8,128)(2,1)S(1)} %get-tuple-element.30), channel_id=1, source_target_pairs={{0,12},{4,8},{8,4},{12,0},{16,28},{20,24},{24,20},{28,16},{1,13},{... | collective-permute-start | bytes 245768 | tf_op jit(solution)/shard_map/ppermute | solution.py:233
  20.6 0.4 %collective-permute-start.2 = (bf16[2,16,1280]{2,1,0:T(8,128)(2,1)S(1)}, bf16[2,16,1280]{2,1,0:T(8,128)(2,1)S(1)}, u32[]{:S(2)}, u32[]{:S(2)}) collective-permute-start(bf16[2,16,1280]{2,1,0:T(8,128)(2,1)S(1)} %get-tuple-element.31), channel_id=1, source_target_pairs={{0,8},{4,12},{8,0},{12,4},{16,24},{20,28},{24,16},{28,20},{1,9},{5... | collective-permute-start | bytes 245768 | tf_op jit(solution)/shard_map/ppermute | solution.py:233
  21.1 0.1 collective-permute-start.3
  21.2 0.2 collective-permute-done.5
  21.4 0.1 add_bitcast_fusion
  21.5 2.9 %collective-permute-start.7 = (bf16[1,16,2816]{2,1,0:T(8,128)(2,1)S(1)}, bf16[1,16,2816]{2,1,0:T(8,128)(2,1)S(1)}, u32[]{:S(2)}, u32[]{:S(2)}) collective-permute-start(bf16[1,16,2816]{2,1,0:T(8,128)(2,1)S(1)} %fusion), channel_id=1, source_target_pairs={{0,16},{4,20},{8,24},{12,28},{16,0},{20,4},{24,8},{28,12},{1,17},{... | collective-permute-start | bytes 270344 | tf_op jit(solution)/shard_map/ppermute | solution.py:233
  24.4 1.4 %pair_gains.1.refs_2_ = f32[16,4096]{1,0:T(8,128)S(1)} custom-call(f32[2,8,1024]{2,1,0:T(8,128)S(1)} %copy-done.1, s32[2,4096]{1,0:T(2,128)S(1)} %bitcast.29), custom_call_target="tpu_custom_call" | custom-call | flops 4194304 | bytes 4194304 | tf_op jit(solution)/shard_map/pair_gains/pallas_call | solution.py:138
  25.8 0.2 collective-permute-done.2
  26.1 2.1 %collective-permute-start.4 = (bf16[1,16,1280]{2,1,0:T(8,128)(2,1)S(1)}, bf16[1,16,1280]{2,1,0:T(8,128)(2,1)S(1)}, u32[]{:S(2)}, u32[]{:S(2)}) collective-permute-start(bf16[1,16,1280]{2,1,0:T(8,128)(2,1)S(1)} %fusion.1), channel_id=1, source_target_pairs={{0,16},{4,20},{8,24},{12,28},{16,0},{20,4},{24,8},{28,12},{1,17},{... | collective-permute-start | bytes 122888 | tf_op jit(solution)/shard_map/ppermute | solution.py:233
  28.3 1.6 %project.1.refs_5_ = f32[4,16,128]{2,1,0:T(8,128)S(1)} custom-call(f32[16,2816]{1,0:T(8,128)S(1)} %bitcast.25, bf16[16,2816]{1,0:T(8,128)(2,1)S(1)} %bitcast.27, f32[16,4096]{1,0:T(8,128)S(1)} %pair_gains.1.refs_2_, bf16[2,8,64,4096]{3,2,1,0:T(8,128)(2,1)S(1)} %bitcast.23), custom_call_target="tpu_custom_call" | custom-call | flops 738197504 | bytes 5767168 | tf_op jit(solution)/shard_map/project/pallas_call | solution.py:180
  29.9 1.2 %collective-permute-done.4 = bf16[1,16,1280]{2,1,0:T(8,128)(2,1)S(1)} collective-permute-done((bf16[1,16,1280]{2,1,0:T(8,128)(2,1)S(1)}, bf16[1,16,1280]{2,1,0:T(8,128)(2,1)S(1)}, u32[]{:S(2)}, u32[]{:S(2)}) %collective-permute-start.4) | collective-permute-done | bytes 40992 | tf_op jit(solution)/shard_map/ppermute | solution.py:233
  31.1 0.9 %finish.1 = (f32[2,128]{1,0:T(2,128)S(1)}, f32[2,128]{1,0:T(2,128)S(1)}, f32[2,128]{1,0:T(2,128)S(1)}, f32[2,128]{1,0:T(2,128)S(1)}) custom-call(f32[16,1280]{1,0:T(8,128)S(1)} %slice_bitcast_fusion.1.refs_0_, bf16[16,1280]{1,0:T(8,128)(2,1)S(1)} %bitcast.28, f32[16,4096]{1,0:T(8,128)S(1)} %pair_gains.1.refs_2_, bf16[2,8,64,4096]{3,2,1,0:T(8,128)(2,1)S(1)} %bitcast.24, ...), custom_call_target="tpu_custom_call" | custom-call | tf_op jit(solution)/shard_map/finish/pallas_call | solution.py:222
  32.0 0.1 collective-permute-start.8
  32.1 1.6 %collective-permute-start.9 = (f32[2,128]{1,0:T(2,128)S(1)}, f32[2,128]{1,0:T(2,128)S(1)}, u32[]{:S(2)}, u32[]{:S(2)}) collective-permute-start(f32[2,128]{1,0:T(2,128)S(1)} %get-tuple-element.41), channel_id=1, source_target_pairs={{0,2},{1,3},{2,0},{3,1},{4,6},{5,7},{6,4},{7,5},{8,10},{9,11},{10,... | collective-permute-start | bytes 3080 | tf_op jit(solution)/shard_map/ppermute | solution.py:233
  33.7 0.3 collective-permute-start.10
  34.0 1.1 %collective-permute-done.8 = f32[2,128]{1,0:T(2,128)S(1)} collective-permute-done((f32[2,128]{1,0:T(2,128)S(1)}, f32[2,128]{1,0:T(2,128)S(1)}, u32[]{:S(2)}, u32[]{:S(2)}) %collective-permute-start.8) | collective-permute-done | bytes 1056 | tf_op jit(solution)/shard_map/ppermute | solution.py:233
  35.1 0.7 %collective-permute-done.9 = f32[2,128]{1,0:T(2,128)S(1)} collective-permute-done((f32[2,128]{1,0:T(2,128)S(1)}, f32[2,128]{1,0:T(2,128)S(1)}, u32[]{:S(2)}, u32[]{:S(2)}) %collective-permute-start.9) | collective-permute-done | bytes 1056 | tf_op jit(solution)/shard_map/ppermute | solution.py:233
  35.7 0.6 %add_add_fusion = f32[2,128]{1,0:T(2,128)} fusion(f32[2,128]{1,0:T(2,128)S(1)} %collective-permute-done.10, f32[2,128]{1,0:T(2,128)S(1)} %collective-permute-done.9, f32[2,128]{1,0:T(2,128)S(1)} %get-tuple-element.39, f32[2,128]{1,0:T(2,128)S(1)} %collective-permute-done.8), kind=kLoop, calls=%fused_computation.8 | loop fusion | flops 768 | bytes 5120 | tf_op jit(solution)/shard_map/add | solution.py:276
  (21 shorter events, 0.1 us)
Async XLA Ops:
  0.0 24.4 %copy-start.1 = (f32[2,8,1024]{2,1,0:T(8,128)S(1)}, f32[2,8,1024]{2,1,0:T(8,128)}, u32[]{:S(2)}) copy-start(f32[2,8,1024]{2,1,0:T(8,128)} %gains_ref) | copy-start | bytes 196612
  0.0 24.4 %copy-start.2 = (s32[4096,2]{0,1:T(2,128)S(1)}, s32[4096,2]{0,1:T(2,128)}, u32[]{:S(2)}) copy-start(s32[4096,2]{0,1:T(2,128)} %param.8) | copy-start | bytes 98308
  8.2 20.1 %slice-start = ((s8[8388608]{0:T(1024)(128)(4,1)}), s8[4194304]{0:T(1024)(128)(4,1)S(1)}, s32[]{:S(2)}) async-start(s8[8388608]{0:T(1024)(128)(4,1)} %bitcast.21), calls=%async_computation | async-start | bytes 8388608
  8.2 22.9 %copy-start = (bf16[1,8,64,512]{3,2,1,0:T(8,128)(2,1)S(1)}, bf16[1,8,64,512]{3,2,1,0:T(8,128)(2,1)}, u32[]{:S(2)}) copy-start(bf16[1,8,64,512]{3,2,1,0:T(8,128)(2,1)} %param.11) | copy-start | bytes 1572868
  8.2 9.4 %collective-permute-start = (bf16[2,16,2816]{2,1,0:T(8,128)(2,1)S(1)}, bf16[2,16,2816]{2,1,0:T(8,128)(2,1)S(1)}, u32[]{:S(2)}, u32[]{:S(2)}) collective-permute-start(bf16[2,16,2816]{2,1,0:T(8,128)(2,1)S(1)} %get-tuple-element.28), channel_id=1, source_target_pairs={{0,12},{4,8},{8,4},{12,0},{16,28},{20,24},{24,20},{28,16},{1,13},{... | collective-permute-start | bytes 540680 | tf_op jit(solution)/shard_map/ppermute | solution.py:233
  12.3 9.1 %collective-permute-start.5 = (bf16[2,16,2816]{2,1,0:T(8,128)(2,1)S(1)}, bf16[2,16,2816]{2,1,0:T(8,128)(2,1)S(1)}, u32[]{:S(2)}, u32[]{:S(2)}) collective-permute-start(bf16[2,16,2816]{2,1,0:T(8,128)(2,1)S(1)} %get-tuple-element.35), channel_id=1, source_target_pairs={{0,8},{4,12},{8,0},{12,4},{16,24},{20,28},{24,16},{28,20},{1,9},{5... | collective-permute-start | bytes 540680 | tf_op jit(solution)/shard_map/ppermute | solution.py:233
  12.7 15.6 %slice-start.1 = ((s8[8388608]{0:T(1024)(128)(4,1)}), s8[4194304]{0:T(1024)(128)(4,1)S(1)}, s32[]{:S(2)}) async-start(s8[8388608]{0:T(1024)(128)(4,1)} %bitcast.21), calls=%async_computation.1 | async-start | bytes 8388608
  12.7 8.7 %collective-permute-start.6 = (bf16[2,16,2816]{2,1,0:T(8,128)(2,1)S(1)}, bf16[2,16,2816]{2,1,0:T(8,128)(2,1)S(1)}, u32[]{:S(2)}, u32[]{:S(2)}) collective-permute-start(bf16[2,16,2816]{2,1,0:T(8,128)(2,1)S(1)} %get-tuple-element.36), channel_id=1, source_target_pairs={{0,4},{4,0},{8,12},{12,8},{16,20},{20,16},{24,28},{28,24},{1,5},{5... | collective-permute-start | bytes 540680 | tf_op jit(solution)/shard_map/ppermute | solution.py:233
  17.6 8.2 %collective-permute-start.1 = (bf16[2,16,1280]{2,1,0:T(8,128)(2,1)S(1)}, bf16[2,16,1280]{2,1,0:T(8,128)(2,1)S(1)}, u32[]{:S(2)}, u32[]{:S(2)}) collective-permute-start(bf16[2,16,1280]{2,1,0:T(8,128)(2,1)S(1)} %get-tuple-element.30), channel_id=1, source_target_pairs={{0,12},{4,8},{8,4},{12,0},{16,28},{20,24},{24,20},{28,16},{1,13},{... | collective-permute-start | bytes 245768 | tf_op jit(solution)/shard_map/ppermute | solution.py:233
  20.6 5.4 %collective-permute-start.2 = (bf16[2,16,1280]{2,1,0:T(8,128)(2,1)S(1)}, bf16[2,16,1280]{2,1,0:T(8,128)(2,1)S(1)}, u32[]{:S(2)}, u32[]{:S(2)}) collective-permute-start(bf16[2,16,1280]{2,1,0:T(8,128)(2,1)S(1)} %get-tuple-element.31), channel_id=1, source_target_pairs={{0,8},{4,12},{8,0},{12,4},{16,24},{20,28},{24,16},{28,20},{1,9},{5... | collective-permute-start | bytes 245768 | tf_op jit(solution)/shard_map/ppermute | solution.py:233
  21.1 5.0 %collective-permute-start.3 = (bf16[2,16,1280]{2,1,0:T(8,128)(2,1)S(1)}, bf16[2,16,1280]{2,1,0:T(8,128)(2,1)S(1)}, u32[]{:S(2)}, u32[]{:S(2)}) collective-permute-start(bf16[2,16,1280]{2,1,0:T(8,128)(2,1)S(1)} %get-tuple-element.32), channel_id=1, source_target_pairs={{0,4},{4,0},{8,12},{12,8},{16,20},{20,16},{24,28},{28,24},{1,5},{5... | collective-permute-start | bytes 245768 | tf_op jit(solution)/shard_map/ppermute | solution.py:233
  21.5 6.8 %collective-permute-start.7 = (bf16[1,16,2816]{2,1,0:T(8,128)(2,1)S(1)}, bf16[1,16,2816]{2,1,0:T(8,128)(2,1)S(1)}, u32[]{:S(2)}, u32[]{:S(2)}) collective-permute-start(bf16[1,16,2816]{2,1,0:T(8,128)(2,1)S(1)} %fusion), channel_id=1, source_target_pairs={{0,16},{4,20},{8,24},{12,28},{16,0},{20,4},{24,8},{28,12},{1,17},{... | collective-permute-start | bytes 270344 | tf_op jit(solution)/shard_map/ppermute | solution.py:233
  26.1 5.0 %collective-permute-start.4 = (bf16[1,16,1280]{2,1,0:T(8,128)(2,1)S(1)}, bf16[1,16,1280]{2,1,0:T(8,128)(2,1)S(1)}, u32[]{:S(2)}, u32[]{:S(2)}) collective-permute-start(bf16[1,16,1280]{2,1,0:T(8,128)(2,1)S(1)} %fusion.1), channel_id=1, source_target_pairs={{0,16},{4,20},{8,24},{12,28},{16,0},{20,4},{24,8},{28,12},{1,17},{... | collective-permute-start | bytes 122888 | tf_op jit(solution)/shard_map/ppermute | solution.py:233
  32.0 3.1 %collective-permute-start.8 = (f32[2,128]{1,0:T(2,128)S(1)}, f32[2,128]{1,0:T(2,128)S(1)}, u32[]{:S(2)}, u32[]{:S(2)}) collective-permute-start(f32[2,128]{1,0:T(2,128)S(1)} %get-tuple-element.40), channel_id=1, source_target_pairs={{0,3},{1,2},{2,1},{3,0},{4,7},{5,6},{6,5},{7,4},{8,11},{9,10},{10,... | collective-permute-start | bytes 3080 | tf_op jit(solution)/shard_map/ppermute | solution.py:233
  32.1 3.6 %collective-permute-start.9 = (f32[2,128]{1,0:T(2,128)S(1)}, f32[2,128]{1,0:T(2,128)S(1)}, u32[]{:S(2)}, u32[]{:S(2)}) collective-permute-start(f32[2,128]{1,0:T(2,128)S(1)} %get-tuple-element.41), channel_id=1, source_target_pairs={{0,2},{1,3},{2,0},{3,1},{4,6},{5,7},{6,4},{7,5},{8,10},{9,11},{10,... | collective-permute-start | bytes 3080 | tf_op jit(solution)/shard_map/ppermute | solution.py:233
  33.7 2.1 %collective-permute-start.10 = (f32[2,128]{1,0:T(2,128)S(1)}, f32[2,128]{1,0:T(2,128)S(1)}, u32[]{:S(2)}, u32[]{:S(2)}) collective-permute-start(f32[2,128]{1,0:T(2,128)S(1)} %get-tuple-element.42), channel_id=1, source_target_pairs={{0,1},{1,0},{2,3},{3,2},{4,5},{5,4},{6,7},{7,6},{8,9},{9,8},{10,11... | collective-permute-start | bytes 3080 | tf_op jit(solution)/shard_map/ppermute | solution.py:233
